TPU v7x, 32 devices: a whole 2x2x4 slice. The times are simulated.
32 devices in a mesh: apa: 16 (over z, x, core), chan: 2 (over y).
Axes of the slice: x: 2, y: 2, z: 4, core: 2. Of those that a mesh axis runs over, the one named last changes fastest.
Arguments:
- frames: bfloat16 [16, 2560, 256], P('apa', 'chan'), may hold values from -6 to 6
- link_to_wire: int32 [16, 2560], P('apa'), may hold values from 0 to 2559, each once within a row
- neighbours: int32 [16, 2], P('apa'), may hold values from -1 to 15, as said below
- kernel: float32 [2, 128, 2816], P(None, 'chan'), may hold values from -6 to 6
- wide_filter: float32 [128], replicated, may hold values from 0.3 to 1
- tight_filter: float32 [128], replicated, may hold values from 0.05 to 0.5
- roi_mask: int32 [16, 160, 4], P('apa', 'chan'), may hold values 0 or 1
Outputs:
- deconvolved: float32 [16, 2560, 256], P('apa', 'chan')
Inputs may be any that keep to these rules, and one draw needn't show every extreme that they name: `link_to_wire`: each row names every channel once. `neighbours`: the 16 APAs form one chain along the detector: column 0 names the APA before, column 1 the APA after, -1 at the two ends of the chain; every named APA lies on the same index of apa as the naming APA or on an adjacent one.
All inputs are finite; a program needn't handle non-finite values. No bound on the sum of `roi_mask` on one device may be relied on, other than what follows from the above.
Results may differ from a plain program's by a relative error of at most 0.0023.
Values may be sent and summed in bfloat16 or wider, within the bound.
No kernel may reach another device: no remote copies, remote signals or barrier semaphores. Data moves between devices by JAX's collectives and lax.ppermute only.
A program may use at most 128 MiB of HBM per device.

v0:
```python
import math

import jax
import jax.numpy as jnp
from jax import lax
from jax.sharding import PartitionSpec as P

PU = 800
PV = 800
PW = 960
HALO_CH = 128
BC = 16
BT = 64
CHANNELS = 2560


two_pi = 2.0 * math.pi
highest = lax.Precision.HIGHEST
block_width = 256


def extended_2(array, sides, width):
    for axis, dim in sides:
        count, length = (lax.axis_size(axis), array.shape[dim])
        up = [(i, (i + 1) % count) for i in range(count - 1)]
        down = [(j, i) for i, j in up]
        last = lax.slice_in_dim(array, length - width, length, axis=dim)
        leading = lax.slice_in_dim(array, 0, width, axis=dim)
        before = lax.ppermute(last, axis, up)
        after = lax.ppermute(leading, axis, down)
        array = jnp.concatenate([before, array, after], axis=dim)
    return array


def tick_angles(ticks):
    moment = lax.iota(jnp.int32, ticks)
    harmonic = lax.iota(jnp.int32, ticks // 2)
    return (moment[:, None] * harmonic[None, :] % ticks).astype(jnp.float32) * (two_pi / ticks)


def forward_table(ticks):
    angles = tick_angles(ticks)
    return jnp.concatenate([jnp.cos(angles), -jnp.sin(angles)], axis=1).astype(jnp.bfloat16)


def inverse_basis(ticks, filter_gain):
    angles = tick_angles(ticks).T
    harmonic = lax.iota(jnp.int32, ticks // 2)
    weights = jnp.where(harmonic == 0, 1.0, 2.0).astype(jnp.float32) / ticks * filter_gain
    return jnp.stack([jnp.cos(angles) * weights[:, None], -jnp.sin(angles) * weights[:, None]])


def dense_product(left, right):
    return jnp.dot(left, right, precision=highest, preferred_element_type=jnp.float32)


def against_rows(left, right):
    return lax.dot_general(
        left, right, (((1,), (1,)), ((), ())), precision=highest, preferred_element_type=jnp.float32
    )


def select_rows(apa_ids, candidates, first_row):
    slots = first_row + lax.iota(jnp.int32, candidates.shape[0])
    matches = (apa_ids[:, None] == slots[None, :]).astype(jnp.float32)
    return jnp.einsum(
        "an,nzfc->azfc", matches, candidates, precision=highest, preferred_element_type=jnp.float32
    )


def deconvolve(plane_field, kernel_part, keep_lo, keep_hi):
    groups = plane_field.shape[0]
    freq_share = plane_field.shape[2]
    plane_width = plane_field.shape[3]
    keep_count = keep_hi - keep_lo
    real_rows = plane_field[:, 0].reshape(-1, plane_width)
    imag_rows = plane_field[:, 1].reshape(-1, plane_width)
    channel_index = lax.iota(jnp.int32, plane_width)
    out_re = jnp.zeros((real_rows.shape[0], keep_count), jnp.float32)
    out_im = jnp.zeros((real_rows.shape[0], keep_count), jnp.float32)
    for block_start in range(0, plane_width, block_width):
        block_stop = min(plane_width, block_start + block_width)
        count = block_stop - block_start
        freq_index = lax.iota(jnp.int32, count) + block_start
        angles = (channel_index[:, None] * freq_index[None, :] % plane_width).astype(
            jnp.float32
        ) * (two_pi / plane_width)
        cosine = jnp.cos(angles)
        sine_part = jnp.sin(angles)
        spec_re = (dense_product(real_rows, cosine) + dense_product(imag_rows, sine_part)).reshape(
            groups, freq_share, count
        )
        spec_im = (dense_product(imag_rows, cosine) - dense_product(real_rows, sine_part)).reshape(
            groups, freq_share, count
        )
        kern_re = kernel_part[0][None, :, block_start:block_stop]
        kern_im = kernel_part[1][None, :, block_start:block_stop]
        prod_re = (spec_re * kern_re - spec_im * kern_im).reshape(-1, count)
        prod_im = (spec_re * kern_im + spec_im * kern_re).reshape(-1, count)
        cos_keep = cosine[keep_lo:keep_hi]
        sin_keep = sine_part[keep_lo:keep_hi]
        out_re = out_re + against_rows(prod_re, cos_keep) - against_rows(prod_im, sin_keep)
        out_im = out_im + against_rows(prod_im, cos_keep) + against_rows(prod_re, sin_keep)
    scale = 1.0 / plane_width
    return jnp.stack(
        [
            (out_re * scale).reshape(groups, freq_share, keep_count),
            (out_im * scale).reshape(groups, freq_share, keep_count),
        ],
        axis=1,
    )


def body(frames, link_to_wire, neighbours, kernel, wide_filter, tight_filter, roi_mask):
    groups = frames.shape[0]
    share = frames.shape[1]
    ticks = frames.shape[2]
    plane_start = PU + PV
    group_index = lax.iota(jnp.int32, groups)
    channel_ids = lax.iota(jnp.int32, CHANNELS)[None, :]
    inverse = (
        jnp.zeros((groups, CHANNELS), jnp.int32)
        .at[group_index[:, None], link_to_wire]
        .set(channel_ids)
    )
    every = lax.all_gather(frames, "chan", axis=1, tiled=True)
    owned = lax.axis_index("chan") * share + lax.iota(jnp.int32, share)
    link_rows = jnp.take(inverse, owned, axis=1)
    source = jnp.take_along_axis(every, link_rows[:, :, None], axis=1)
    spectra = jnp.einsum(
        "act,tk->akc", source, forward_table(ticks), preferred_element_type=jnp.float32
    )
    spectra = spectra.reshape(groups, 2, ticks // 2, share)
    spread = lax.all_to_all(spectra, "chan", split_axis=2, concat_axis=3, tiled=True)
    edge_band = jnp.concatenate(
        [
            spread[:, :, :, plane_start : plane_start + HALO_CH],
            spread[:, :, :, CHANNELS - HALO_CH :],
        ],
        axis=3,
    )
    lower_id = neighbours[:, 0]
    upper_id = neighbours[:, 1]
    nearby = extended_2(edge_band, (("apa", 0),), groups)
    first_row = (lax.axis_index("apa") - 1) * groups
    lower_rim = select_rows(lower_id, nearby[:, :, :, HALO_CH:], first_row)
    upper_rim = select_rows(upper_id, nearby[:, :, :, :HALO_CH], first_row)
    extended = jnp.concatenate([lower_rim, spread[:, :, :, plane_start:], upper_rim], axis=3)
    deconv = jnp.concatenate(
        [
            deconvolve(spread[:, :, :, :PU], kernel[:, :, :PU], 0, PU),
            deconvolve(spread[:, :, :, PU:plane_start], kernel[:, :, PU:plane_start], 0, PV),
            deconvolve(extended, kernel[:, :, plane_start:], HALO_CH, HALO_CH + PW),
        ],
        axis=3,
    )
    returned = lax.all_to_all(deconv, "chan", split_axis=3, concat_axis=2, tiled=True)

    def signal(filter_gain):
        return jnp.einsum(
            "azkc,zkt->act",
            returned,
            inverse_basis(ticks, filter_gain),
            precision=highest,
            preferred_element_type=jnp.float32,
        )

    expanded = jnp.broadcast_to(
        roi_mask[:, :, None, :, None], (groups, share // BC, BC, ticks // BT, BT)
    ).reshape(groups, share, ticks)
    return jnp.where(expanded == 1, signal(wide_filter), signal(tight_filter))


def solution(mesh):
    placed = (
        P("apa", "chan", None),
        P("apa", None),
        P("apa", None),
        P(None, "chan", None),
        P(),
        P(),
        P("apa", "chan", None),
    )
    return jax.shard_map(
        body, mesh=mesh, in_specs=placed, out_specs=P("apa", "chan", None), check_vma=False
    )
```

profile of v0, /device:TPU:24, one launch (start us, length us, event | category | flops | bytes accessed | tf_op | source)
XLA Modules:
  0.0 527.7 jit_solution(16503415408090372901)
XLA Ops:
  9.6 9.9 %scatter_custom_fusion = s32[2560]{0:T(1024)S(1)} fusion(s32[2560]{0:T(1024)S(1)} %broadcast_select_fusion, s32[2560]{0:T(1024)S(1)} %iota.269, s32[]{:T(128)} %constant.134.clone.1), kind=kCustom, calls=%fused_computation.503 | custom fusion | bytes 10244 | tf_op jit(solution)/shard_map/scatter | solution.py:124
  19.6 7.1 %gather_fusion = s32[1280]{0:T(1024)S(1)} fusion(s32[2560]{0:T(1024)S(1)} %scatter_custom_fusion, s32[2048]{0:T(1024)S(1)} %pad_clamp_fusion.1), kind=kCustom, calls=%fused_computation | custom fusion | bytes 15360 | tf_op jit(solution)/shard_map/jit(_take)/gather | solution.py:128
  43.6 6.3 %fusion.22 = (f32[1216,256]{1,0:T(8,128)}, f32[1216,256]{1,0:T(8,128)}) fusion(s32[256]{0:T(256)S(1)} %iota_add_fusion.2), kind=kLoop, calls=%fused_computation.37 | loop fusion | flops 2801664 | bytes 2491392 | tf_op jit(solution)/shard_map/sin | solution.py:89
  50.5 6.5 %fusion.26 = (f32[1216,256]{1,0:T(8,128)}, f32[1216,256]{1,0:T(8,128)}) fusion(s32[256]{0:T(256)S(1)} %iota_add_fusion.3), kind=kLoop, calls=%fused_computation.42 | loop fusion | flops 2801664 | bytes 2491392 | tf_op jit(solution)/shard_map/sin | solution.py:89
  73.8 6.3 %fusion.18 = (f32[1216,256]{1,0:T(8,128)}, f32[1216,256]{1,0:T(8,128)}) fusion(s32[256]{0:T(256)S(1)} %iota_add_fusion.1), kind=kLoop, calls=%fused_computation.32 | loop fusion | flops 2801664 | bytes 2491392 | tf_op jit(solution)/shard_map/sin | solution.py:89
  80.1 10.4 %all-to-all-done = f32[1,2,128,1280]{3,1,0,2:T(2,128)} async-done(((f32[1,2,128,1280]{3,1,0,2:T(2,128)}), f32[1,2,128,1280]{3,1,0,2:T(2,128)}, u32[]{:S(2)}, u32[]{:S(2)}) %all-to-all-start) | async-done | bytes 1310752 | tf_op jit(solution)/shard_map/all_to_all | solution.py:134
  333.9 6.9 %fusion.164 = f32[64,256]{1,0:T(8,128)S(1)} fusion(f32[1,2,64,1216]{3,2,1,0:T(8,128)} %concatenate.23), kind=kOutput, calls=%fused_computation.208 | convolution fusion | flops 241876992 | bytes 393216 | tf_op jit(solution)/shard_map/dot_general | solution.py:54
  340.8 5.6 %fusion.170 = f32[64,256]{1,0:T(8,128)S(1)} fusion(s32[256]{0:T(256)S(1)} %iota_add_fusion.3, f32[1,2,64,1216]{3,2,1,0:T(8,128)S(1)} %copy-done.12), kind=kOutput, calls=%fused_computation.210 | convolution fusion | flops 241876992 | bytes 394240 | tf_op jit(solution)/shard_map/dot_general | solution.py:54
  346.4 5.8 %fusion.176 = f32[64,256]{1,0:T(8,128)S(1)} fusion(s32[256]{0:T(256)S(1)} %iota_add_fusion.2, f32[1,2,64,1216]{3,2,1,0:T(8,128)S(1)} %copy-done.12), kind=kOutput, calls=%fused_computation.212 | convolution fusion | flops 241876992 | bytes 394240 | tf_op jit(solution)/shard_map/dot_general | solution.py:54
  357.9 6.0 %fusion.158 = f32[64,192]{1,0:T(8,128)S(1)} fusion(s32[192]{0:T(256)S(1)} %iota_add_fusion, f32[1,2,64,1216]{3,2,1,0:T(8,128)S(1)} %copy-done.12), kind=kOutput, calls=%fused_computation.206 | convolution fusion | flops 181407744 | bytes 377856 | tf_op jit(solution)/shard_map/dot_general | solution.py:54
  369.5 5.8 %fusion.178 = f32[64,256]{1,0:T(8,128)S(1)} fusion(s32[256]{0:T(256)S(1)} %iota_add_fusion.2, f32[1,2,64,1216]{3,2,1,0:T(8,128)S(1)} %copy-done.12), kind=kOutput, calls=%fused_computation.213 | convolution fusion | flops 241876992 | bytes 394240 | tf_op jit(solution)/shard_map/dot_general | solution.py:54
  381.0 5.8 %fusion.160 = f32[64,192]{1,0:T(8,128)S(1)} fusion(s32[192]{0:T(256)S(1)} %iota_add_fusion, f32[1,2,64,1216]{3,2,1,0:T(8,128)S(1)} %copy-done.12), kind=kOutput, calls=%fused_computation.207 | convolution fusion | flops 181407744 | bytes 377856 | tf_op jit(solution)/shard_map/dot_general | solution.py:54
  386.8 5.6 %fusion.166 = f32[64,256]{1,0:T(8,128)S(1)} fusion(f32[1,2,64,1216]{3,2,1,0:T(8,128)S(1)} %copy-done.12), kind=kOutput, calls=%fused_computation.209 | convolution fusion | flops 241876992 | bytes 393216 | tf_op jit(solution)/shard_map/dot_general | solution.py:54
  392.5 6.1 %convolution_subtract_fusion.16 = f32[64,256]{1,0:T(8,128)S(1)} fusion(f32[64,256]{1,0:T(8,128)S(1)} %fusion.170, s32[256]{0:T(256)S(1)} %iota_add_fusion.3, f32[1,2,64,1216]{3,2,1,0:T(8,128)S(1)} %copy-done.12), kind=kOutput, calls=%fused_computation.121 | convolution fusion | flops 241893376 | bytes 459776 | tf_op jit(solution)/shard_map/dot_general | solution.py:54
  398.5 5.7 %convolution_subtract_fusion.15 = f32[64,256]{1,0:T(8,128)S(1)} fusion(f32[64,256]{1,0:T(8,128)S(1)} %fusion.176, s32[256]{0:T(256)S(1)} %iota_add_fusion.2, f32[1,2,64,1216]{3,2,1,0:T(8,128)S(1)} %copy-done.12), kind=kOutput, calls=%fused_computation.119 | convolution fusion | flops 241893376 | bytes 459776 | tf_op jit(solution)/shard_map/dot_general | solution.py:54
  404.2 5.7 %convolution_add_fusion.36 = f32[64,256]{1,0:T(8,128)S(1)} fusion(f32[64,256]{1,0:T(8,128)S(1)} %fusion.172, s32[256]{0:T(256)S(1)} %iota_add_fusion.3, f32[1,2,64,1216]{3,2,1,0:T(8,128)S(1)} %copy-done.12), kind=kOutput, calls=%fused_computation.122 | convolution fusion | flops 241893376 | bytes 459776 | tf_op jit(solution)/shard_map/dot_general | solution.py:54
  409.9 5.8 %convolution_add_fusion.35 = f32[64,256]{1,0:T(8,128)S(1)} fusion(f32[64,256]{1,0:T(8,128)S(1)} %fusion.178, s32[256]{0:T(256)S(1)} %iota_add_fusion.2, f32[1,2,64,1216]{3,2,1,0:T(8,128)S(1)} %copy-done.12), kind=kOutput, calls=%fused_computation.120 | convolution fusion | flops 241893376 | bytes 459776 | tf_op jit(solution)/shard_map/dot_general | solution.py:54
  415.7 5.7 %convolution_add_fusion.34 = f32[64,256]{1,0:T(8,128)S(1)} fusion(f32[64,256]{1,0:T(8,128)S(1)} %fusion.184, s32[256]{0:T(256)S(1)} %iota_add_fusion.1, f32[1,2,64,1216]{3,2,1,0:T(8,128)S(1)} %copy-done.12), kind=kOutput, calls=%fused_computation.118 | convolution fusion | flops 241893376 | bytes 459776 | tf_op jit(solution)/shard_map/dot_general | solution.py:54
  421.4 5.9 %convolution_add_fusion.33 = f32[64,192]{1,0:T(8,128)S(1)} fusion(f32[64,192]{1,0:T(8,128)S(1)} %fusion.160, s32[192]{0:T(256)S(1)} %iota_add_fusion, f32[1,2,64,1216]{3,2,1,0:T(8,128)S(1)} %copy-done.12), kind=kOutput, calls=%fused_computation.116 | convolution fusion | flops 181420032 | bytes 443392 | tf_op jit(solution)/shard_map/dot_general | solution.py:54
  427.3 5.7 %convolution_add_fusion.37 = f32[64,256]{1,0:T(8,128)S(1)} fusion(f32[64,256]{1,0:T(8,128)S(1)} %fusion.166, f32[1,2,64,1216]{3,2,1,0:T(8,128)S(1)} %copy-done.12), kind=kOutput, calls=%fused_computation.124 | convolution fusion | flops 241893376 | bytes 458752 | tf_op jit(solution)/shard_map/dot_general | solution.py:54
  433.0 6.1 %multiply_subtract_fusion.4 = (f32[64,256]{1,0:T(8,128)S(1)}, f32[64,256]{1,0:T(8,128)S(1)}) fusion(f32[64,256]{1,0:T(8,128)S(1)} %convolution_add_fusion.37, f32[64,1216]{1,0:T(8,128)S(1)} %copy-done.14, f32[64,1216]{1,0:T(8,128)S(1)} %copy-done.13, f32[64,256]{1,0:T(8,128)S(1)} %fusion.164, f32[1,2,64,1216]{3,2,1,0:T(8,128)S(1)} %copy-done.12), kind=kOutput, calls=%fused_computation.469 | convolution fusion | flops 241991680 | bytes 720896 | tf_op jit(solution)/shard_map/dot_general | solution.py:54
  443.2 5.8 %multiply_subtract_fusion.1 = (f32[64,256]{1,0:T(8,128)S(1)}, f32[64,256]{1,0:T(8,128)S(1)}, f32[64,256]{1,0:T(8,128)S(1)}, f32[64,256]{1,0:T(8,128)S(1)}, f32[64,256]{1,0:T(8,128)S(1)}, /*index=5*/f32[64,256]{1,0:T(8,128)S(1)}) fusion(f32[64,256]{1,0:T(8,128)S(1)} %convolution_add_fusion.34, f32[64,1216]{1,0:T(8,128)S(1)} %copy-done.14, ...), kind=kOutput, calls=%fused_computation.463 | convolution fusion | flops 242188288 | bytes 1508352 | tf_op jit(solution)/shard_map/dot_general | solution.py:54
  461.4 5.9 %multiply_subtract_fusion = (f32[64,192]{1,0:T(8,128)S(1)}, f32[64,192]{1,0:T(8,128)S(1)}) fusion(f32[64,192]{1,0:T(8,128)S(1)} %convolution_add_fusion.33, f32[64,1216]{1,0:T(8,128)S(1)} %copy-done.14, f32[64,1216]{1,0:T(8,128)S(1)} %copy-done.13, f32[64,192]{1,0:T(8,128)S(1)} %fusion.158, s32[192]{0:T(256)S(1)} %iota_add_fusion, ...), kind=kOutput, calls=%fused_computation.461 | convolution fusion | flops 181493760 | bytes 689152 | tf_op jit(solution)/shard_map/dot_general | solution.py:54
  484.3 16.5 %all-to-all-done.1 = f32[2,1,163840]{2,1,0:T(1,128)S(1)} async-done(((f32[2,1,163840]{2,1,0:T(1,128)}), f32[2,1,163840]{2,1,0:T(1,128)S(1)}, u32[]{:S(2)}, u32[]{:S(2)}) %all-to-all-start.1) | async-done | bytes 1310752 | tf_op jit(solution)/shard_map/all_to_all | solution.py:157
  (193 shorter events, 349.6 us)
Async XLA Ops:
  6.5 55.6 %all-gather.2.cloned.1.call-start = ((), (), s32[]{:S(2)}) async-start(), calls=%async_computation.2 | async-start | bytes 1966080 | tf_op jit(solution)/shard_map/all_gather | solution.py:126
  19.6 7.7 %copy-start.10 = (f32[2,64,2816]{2,1,0:T(8,128)S(1)}, f32[2,64,2816]{2,1,0:T(8,128)}, u32[]{:S(2)}) copy-start(f32[2,64,2816]{2,1,0:T(8,128)} %param.10) | copy-start | bytes 4325380
  29.4 11.2 %copy-start.15 = (s32[1,80,4]{1,2,0:T(4,128)S(1)}, s32[1,80,4]{1,2,0:T(4,128)}, u32[]{:S(2)}) copy-start(s32[1,80,4]{1,2,0:T(4,128)} %param.13) | copy-start | bytes 3844
  29.4 11.2 %copy-start.16 = (s32[1,2]{1,0:T(1,128)S(1)}, s32[1,2]{1,0:T(1,128)}, u32[]{:S(2)}) copy-start(s32[1,2]{1,0:T(1,128)} %param.9) | copy-start | bytes 28
  43.6 6.3 %copy-start.18 = (f32[128]{0:T(128)S(1)}, f32[128]{0:T(128)}, u32[]{:S(2)}) copy-start(f32[128]{0:T(128)} %param.11) | copy-start | bytes 1540
  69.3 21.3 %all-to-all-start = ((f32[1,2,128,1280]{3,1,0,2:T(2,128)}), f32[1,2,128,1280]{3,1,0,2:T(2,128)}, u32[]{:S(2)}, u32[]{:S(2)}) async-start(f32[1,2,128,1280]{3,1,0,2:T(2,128)} %copy.46), calls=%async_computation | async-start | bytes 2621440 | tf_op jit(solution)/shard_map/all_to_all | solution.py:134
  97.5 5.9 %copy-start.8 = (f32[1,2,64,2560]{3,2,1,0:T(8,128)S(1)}, f32[1,2,64,2560]{3,2,1,0:T(8,128)}, u32[]{:S(2)}) copy-start(f32[1,2,64,2560]{3,2,1,0:T(8,128)} %all_to_all.27) | copy-start | bytes 3932164
  152.6 176.6 %collective-permute-start.1 = (f32[1,2,64,256]{3,2,1,0:T(8,128)S(1)}, f32[1,2,64,256]{3,2,1,0:T(8,128)S(1)}, u32[]{:S(2)}, u32[]{:S(2)}) collective-permute-start(f32[1,2,64,256]{3,2,1,0:T(8,128)S(1)} %pad_maximum_fusion.5), channel_id=1, source_target_pairs={{2,0},{4,2},{6,4},{8,6},{10,8},{12,10},{14,12},{16,14},{18,16},{20... | collective-permute-start | bytes 393224 | tf_op jit(solution)/shard_map/ppermute | solution.py:30
  154.6 174.7 %collective-permute-start = (f32[1,2,64,256]{3,2,1,0:T(8,128)S(1)}, f32[1,2,64,256]{3,2,1,0:T(8,128)S(1)}, u32[]{:S(2)}, u32[]{:S(2)}) collective-permute-start(f32[1,2,64,256]{3,2,1,0:T(8,128)S(1)} %pad_maximum_fusion.5), channel_id=1, source_target_pairs={{0,2},{2,4},{4,6},{6,8},{8,10},{10,12},{12,14},{14,16},{16,18},{18... | collective-permute-start | bytes 393224 | tf_op jit(solution)/shard_map/ppermute | solution.py:29
  333.9 6.9 %copy-start.12 = (f32[1,2,64,1216]{3,2,1,0:T(8,128)S(1)}, f32[1,2,64,1216]{3,2,1,0:T(8,128)}, u32[]{:S(2)}) copy-start(f32[1,2,64,1216]{3,2,1,0:T(8,128)} %concatenate.23) | copy-start | bytes 1867780
  427.3 5.7 %copy-start.13 = (f32[64,1216]{1,0:T(8,128)S(1)}, f32[64,1216]{1,0:T(8,128)}, u32[]{:S(2)}) copy-start(f32[64,1216]{1,0:T(8,128)} %get-tuple-element.5) | copy-start | bytes 933892
  427.3 5.7 %copy-start.14 = (f32[64,1216]{1,0:T(8,128)S(1)}, f32[64,1216]{1,0:T(8,128)}, u32[]{:S(2)}) copy-start(f32[64,1216]{1,0:T(8,128)} %get-tuple-element.6) | copy-start | bytes 933892
  433.0 6.1 %copy-start.4 = (f32[1216,256]{1,0:T(8,128)S(1)}, f32[1216,256]{1,0:T(8,128)}, u32[]{:S(2)}) copy-start(f32[1216,256]{1,0:T(8,128)} %fusion.31) | copy-start | bytes 3735556
  439.1 2.0 copy-start.2
  443.2 5.9 %copy-start.7 = (f32[1216,256]{1,0:T(8,128)S(1)}, f32[1216,256]{1,0:T(8,128)}, u32[]{:S(2)}) copy-start(f32[1216,256]{1,0:T(8,128)} %get-tuple-element.60) | copy-start | bytes 3735556
  449.1 2.0 copy-start.5
  451.1 2.0 copy-start.1
  453.2 2.0 copy-start
  455.2 2.0 copy-start.6
  457.3 2.0 copy-start.3
  479.1 4.0 copy-start.19
  479.1 4.6 copy-start.17
  479.1 21.7 %all-to-all-start.1 = ((f32[2,1,163840]{2,1,0:T(1,128)}), f32[2,1,163840]{2,1,0:T(1,128)S(1)}, u32[]{:S(2)}, u32[]{:S(2)}) async-start(f32[2,1,163840]{2,1,0:T(1,128)} %reshape.572), calls=%async_computation.1 | async-start | bytes 2621440 | tf_op jit(solution)/shard_map/all_to_all | solution.py:157
  514.9 2.2 copy-start.11
  (1 other events, 1.1 us)
Sparse Core Ops, SparseCore 0:
  8.9 25.2 all-gather.1
where the time goes:
time: 536 us; the launch traced here: 528 us
  matrix products  371 us (69%)
  local copies, waits for them, and re-layouts  54.3 us (10%)
  other arithmetic  46.5 us (9%)
  waiting for transfers between devices  27.7 us (5%)
  between operations  15 us (3%)
  starting transfers between devices  12.8 us (2%)
    dot_general x52, matrix products, dense_product(): jnp.dot(left, right, precision=highest, preferred_element_type=jnp.float32)  228 us
    dot_general x52, matrix products, against_rows(): lax.dot_general(left, right, (((1,), (1,)), ((), ())), precision=highest,...  134 us
    sin x5, other arithmetic, deconvolve(): sine_part = jnp.sin(angles)  29.8 us
    all_to_all x1, waiting for transfers between devices, body(): lax.all_to_all(deconv, 'chan', split_axis=3, concat_axis=2, tiled=True)  16.5 us
  transfers between devices with their start and end apart: 5, of which 2 were waited for; matrix products, arithmetic and copies ran while one was open for 44% of the time, Pallas kernels for 0%

commit v1 on v0

v1 whole, which is shorter than its diff:
```python
import functools
import math

import jax
import jax.numpy as jnp
import ml_dtypes
import numpy as np
from jax import lax
from jax.experimental import pallas as pl
from jax.experimental.pallas import tpu as pltpu
from jax.sharding import PartitionSpec as P

PU = 800
PV = 800
PW = 960
HALO_CH = 128
BC = 16
BT = 64
CHANNELS = 2560

two_pi = 2.0 * math.pi
lane = 128
f32 = jnp.float32
bf16 = jnp.bfloat16
whole = pl.BlockSpec(memory_space=pltpu.VMEM)
scalars = pl.BlockSpec(memory_space=pltpu.SMEM)


def ceil_to(size, step):
    return -(-size // step) * step


class Plane:
    def __init__(self, length, wire, count, keep, kernel_start, row):
        self.length, self.wire, self.count, self.keep = length, wire, count, keep
        self.kernel_start, self.row = kernel_start, row
        self.half = length // 2
        self.rows = ceil_to(self.half + 1, 16)


def make_planes():
    found, row, start = [], 0, 0
    for length, wire, count, keep in (
        (PU, 0, PU, 0),
        (PV, PU, PV, 0),
        (PW + 2 * HALO_CH, PU + PV, PW, HALO_CH),
    ):
        found.append(Plane(length, wire, count, keep, start, row))
        row += found[-1].rows
        start += length
    return found


planes = make_planes()
all_rows = planes[-1].row + planes[-1].rows


def split(values):
    high = values.astype(bf16)
    return high, (values - high.astype(f32)).astype(bf16)


def channel_tables(length, rows):
    index = np.arange(rows)
    angles = (index[:, None] * index[None, :] % length) * (two_pi / length)
    inside = (index <= length // 2).astype(np.float64)
    mask = inside[:, None] * inside[None, :]
    parts = []
    for values in (np.cos(angles) * mask, np.sin(angles) * mask):
        high = values.astype(np.float32).astype(ml_dtypes.bfloat16)
        parts += [high, (values - high.astype(np.float64)).astype(np.float32).astype(ml_dtypes.bfloat16)]
    return np.stack(parts)


def tick_angles(ticks):
    return (np.arange(ticks)[:, None] * np.arange(ticks // 2)[None, :] % ticks) * (two_pi / ticks)


def in_blocks(values, blocks, padded):
    parts = np.stack(np.split(values, blocks, axis=-1))
    return np.pad(parts, [(0, 0)] * (parts.ndim - 1) + [(0, padded - parts.shape[-1])])


def forward_tables(ticks, blocks, padded):
    angles = tick_angles(ticks)
    halves = [in_blocks(part, blocks, padded) for part in (np.cos(angles), -np.sin(angles))]
    return np.concatenate(halves, axis=-1).astype(np.float32).astype(ml_dtypes.bfloat16)


def inverse_tables(ticks, blocks, padded):
    angles = tick_angles(ticks)
    weights = np.where(np.arange(ticks // 2) == 0, 1.0, 2.0) / ticks
    halves = [in_blocks(part * weights, blocks, padded) for part in (np.cos(angles), -np.sin(angles))]
    return np.ascontiguousarray(np.swapaxes(np.concatenate(halves, axis=-1), 1, 2)).astype(np.float32)


def dot(left, right):
    return jnp.dot(left, right, preferred_element_type=f32)


def one_hot(rows, first, targets):
    numbers = lax.broadcasted_iota(jnp.int32, (rows, targets.shape[1]), 0) + first
    return jnp.where(numbers == targets, 1.0, 0.0).astype(bf16)


def far_spectra(blocks, where, frames, table, *outs):
    for shift, out in enumerate(outs, 1):
        out[...] = dot(frames[...], table[lax.rem(where[0] + shift, blocks)]).astype(bf16)


def near_spectra(blocks, where, frames, table, wires, own, *bands):
    spectra = [dot(frames[...], table[lax.rem(where[0] + s, blocks)]).astype(bf16) for s in range(blocks)]
    own[...] = spectra[0]
    for way in range(2):
        chosen = one_hot(HALO_CH, where[1 + way], wires[...])
        for s in range(blocks):
            bands[way * blocks + s][...] = dot(chosen, spectra[s]).astype(bf16)


def rotated(values):
    half = values.shape[1] // 2
    first = lax.broadcasted_iota(jnp.int32, values.shape, 1) < half
    turned = pltpu.roll(values, half, 1)
    return jnp.where(first, turned, -turned)


def fold_operand(spectra, sign_row):
    width = spectra.shape[1]
    signs = jnp.transpose(jnp.broadcast_to(sign_row, (width, sign_row.shape[1])))
    turned = rotated(spectra.astype(f32)) * signs
    return jnp.concatenate([spectra, turned.astype(bf16)], axis=1)


def prepare(share, kernel, targets, signs, own, sums, diffs, folded):
    harmonics, width = kernel.shape[1], sums.shape[1]
    spare = width // 2 - harmonics
    operand = fold_operand(own[...], signs[:, :share])
    for plane in planes:
        rows = pl.ds(plane.row, plane.rows)
        folded[rows, :] = dot(one_hot(plane.rows, plane.row, targets[:, :share]), operand)
        start = plane.kernel_start // lane * lane
        stop = ceil_to(plane.kernel_start + plane.length, lane)
        parts = []
        for z in range(2):
            parts.append(kernel[z, :, start:stop])
            if spare:
                parts.append(jnp.zeros((spare, stop - start), f32))
        high, low = split(jnp.concatenate(parts, axis=0))
        values = jnp.concatenate([high, low], axis=0)
        row = lax.broadcasted_iota(jnp.int32, (plane.rows, stop - start), 0)
        column = lax.broadcasted_iota(jnp.int32, (plane.rows, stop - start), 1) + (start - plane.kernel_start)
        direct = jnp.where((column == row) & (row <= plane.half), 1.0, 0.0)
        mirror = jnp.where((column == plane.length - row) & (row > 0) & (row < plane.half), 1.0, 0.0)
        for out, matrix in ((sums, direct + mirror), (diffs, direct - mirror)):
            both = lax.dot_general(
                matrix.astype(bf16), values, (((1,), (1,)), ((), ())), preferred_element_type=f32
            )
            out[rows, :] = (both[:, :width] + both[:, width:]) * (1.0 / plane.length)


def two_pass(high, low, values):
    width = values.shape[1]
    joined = jnp.concatenate(split(values), axis=1)
    both = dot(high, joined) + dot(low, joined)
    return both[:, :width] + both[:, width:]


def times(values, factor):
    half = values.shape[1] // 2
    first = lax.broadcasted_iota(jnp.int32, values.shape, 1) < half
    other = pltpu.roll(factor, half, 1)
    real = jnp.where(first, factor, other)
    imag = jnp.where(first, other, factor)
    return values * real - rotated(values) * imag


def channel_stage(blocks, share, where, *refs):
    received = refs[: blocks - 1]
    halo = refs[blocks - 1 : 3 * blocks - 1]
    targets, signs, folded, sums, diffs, narrow, wide = refs[3 * blocks - 1 : 3 * blocks + 6]
    own = refs[3 * blocks + 6]
    sends = refs[3 * blocks + 7 : 4 * blocks + 6]
    result = refs[4 * blocks + 6]
    far = (blocks - 1) * share
    spectra = jnp.concatenate([ref[...] for ref in received + halo], axis=0)
    operand = fold_operand(spectra, signs[:, share:])
    for plane in planes:
        rows = pl.ds(plane.row, plane.rows)
        used = operand.shape[0] if plane.keep else far
        wanted = targets[:, share : share + used]
        both = folded[rows, :] + dot(one_hot(plane.rows, plane.row, wanted), operand[:used])
        table = wide if plane.keep else narrow
        width = both.shape[1] // 2
        even = two_pass(table[0], table[1], both[:, :width])
        odd = two_pass(table[2], table[3], both[:, width:])
        plus, minus = sums[rows, :], diffs[rows, :]
        total = times(even, plus) + times(odd, minus)
        gap = times(even, minus) + times(odd, plus)
        kept = slice(plane.keep, plane.rows)
        cosine = two_pass(table[0, kept], table[1, kept], total)
        sine = two_pass(table[2, kept], table[3, kept], -rotated(gap))
        straight = plane.count // 2
        result[plane.wire : plane.wire + straight, :] = (cosine + sine)[:straight]
        back = jnp.concatenate(split(cosine - sine), axis=1)
        row = lax.broadcasted_iota(jnp.int32, (straight, back.shape[0]), 0)
        column = lax.broadcasted_iota(jnp.int32, (straight, back.shape[0]), 1) + plane.keep
        turned = dot(jnp.where(column == plane.half - row, 1.0, 0.0).astype(bf16), back)
        result[plane.wire + straight : plane.wire + plane.count, :] = turned[:, :width] + turned[:, width:]
    here = where[0]
    own[...] = result[pl.ds(pl.multiple_of(here * share, share), share), :]
    for shift, out in enumerate(sends, 1):
        first = pl.multiple_of(lax.rem(here + shift, blocks) * share, share)
        out[...] = result[pl.ds(first, share), :].astype(bf16)


def chosen_signal(both, mask, ticks):
    column = lax.broadcasted_iota(jnp.int32, (mask.shape[0], ticks), 1)
    inside = jnp.zeros((mask.shape[0], ticks), jnp.int32)
    for block in range(ticks // BT):
        inside = jnp.where(column // BT == block, mask[:, block : block + 1], inside)
    inside = jnp.broadcast_to(inside[:, None, :], (mask.shape[0], BC, ticks)).reshape(-1, ticks)
    return jnp.where(inside == 1, both[:, :ticks], both[:, ticks:])


def own_signal(blocks, where, own, basis, mask, signal, bases):
    here = where[0]
    ticks = signal.shape[1]
    high, low = split(basis[here])
    joined = jnp.concatenate(split(own[...]), axis=1)
    both = dot(joined, jnp.concatenate([high, high], axis=0))
    both += dot(joined, jnp.concatenate([low, low], axis=0))
    signal[...] = chosen_signal(both, mask[...], ticks)
    for shift in range(1, blocks):
        parts = split(basis[lax.rem(here + blocks - shift, blocks)])
        bases[shift - 1] = jnp.concatenate(parts, axis=0)


def whole_signal(blocks, signal, bases, mask, *refs):
    out = refs[-1]
    ticks = out.shape[1]
    both = None
    for shift in range(1, blocks):
        values = refs[shift - 1][...]
        term = dot(jnp.concatenate([values, values], axis=1), bases[shift - 1])
        both = term if both is None else both + term
    if both is None:
        out[...] = signal[...]
    else:
        out[...] = signal[...] + chosen_signal(both, mask[...], ticks)


def call(kernel, outs, ins, name, scratch=()):
    return pl.pallas_call(
        kernel,
        out_shape=[jax.ShapeDtypeStruct(shape, dtype) for shape, dtype in outs],
        in_specs=ins,
        out_specs=[whole] * len(outs),
        scratch_shapes=scratch,
        compiler_params=pltpu.CompilerParams(vmem_limit_bytes=48 * 1024 * 1024),
        name=name,
    )


def fold_targets(wires, lower, upper, here, blocks):
    first = wires < PU
    second = wires < PU + PV
    last = planes[2]
    offset = jnp.where(first, wires, jnp.where(second, wires - PU, wires - (PU + PV) + HALO_CH))
    length = jnp.where(first, PU, jnp.where(second, PV, last.length))
    row = jnp.where(first, 0, jnp.where(second, planes[1].row, last.row))
    spot = jnp.tile(lax.iota(jnp.int32, HALO_CH), blocks)
    far = last.length - HALO_CH
    sides = []
    for other in (here - 1, here + 1):
        begin = jnp.where(lower == other, 0, far)
        known = (other >= 0) & ((lower == other) | (upper == other))
        sides.append((jnp.where(known, begin, 0) + spot, jnp.where(known, last.row, -last.length) + 0 * spot))
    offset = jnp.concatenate([offset] + [side[0] for side in sides])
    length = jnp.concatenate([length, jnp.full((2 * blocks * HALO_CH,), last.length, jnp.int32)])
    row = jnp.concatenate([row] + [side[1] for side in sides])
    behind = 2 * offset > length
    target = row + jnp.where(behind, length - offset, offset)
    return target[None], jnp.where(behind, -1.0, 1.0).astype(f32)[None]


def body(frames, link_to_wire, neighbours, kernel, wide_filter, tight_filter, roi_mask):
    frames, roi_mask = frames[0], roi_mask[0]
    share, ticks = frames.shape
    blocks = lax.axis_size("chan")
    detectors = lax.axis_size("apa")
    harmonics = kernel.shape[1]
    padded = max(harmonics, lane // 2)
    width = 2 * padded
    here = lax.axis_index("chan")
    detector = lax.axis_index("apa")
    lower, upper = neighbours[0, 0], neighbours[0, 1]
    head, tail = PU + PV, CHANNELS - HALO_CH
    to_next = jnp.where(upper == detector + 1, tail, head)
    to_before = jnp.where(lower == detector - 1, head, tail)
    where = jnp.stack([here, to_next, to_before]).astype(jnp.int32)
    table = jnp.asarray(forward_tables(ticks, blocks, padded))

    far = call(
        functools.partial(far_spectra, blocks), [((share, width), bf16)] * (blocks - 1),
        [scalars, whole, whole], "far_spectra",
    )(where, frames, table)
    received = [
        lax.ppermute(part, "chan", [(i, (i + s) % blocks) for i in range(blocks)])
        for s, part in enumerate(far, 1)
    ]
    wires = link_to_wire.reshape(blocks, share)
    wires = jnp.concatenate([wires[(here - s) % blocks] for s in range(blocks)])
    own, *bands = call(
        functools.partial(near_spectra, blocks),
        [((share, width), bf16)] + [((HALO_CH, width), bf16)] * (2 * blocks),
        [scalars, whole, whole, whole], "near_spectra",
    )(where, frames, table, wires[None, :share])
    halo = []
    for way, step in enumerate((1, -1)):
        for s in range(blocks):
            pairs = [
                (a * blocks + i, (a + step) * blocks + (i + s) % blocks)
                for a in range(detectors) if 0 <= a + step < detectors
                for i in range(blocks)
            ]
            halo.append(lax.ppermute(bands[way * blocks + s], ("apa", "chan"), pairs))
    targets, signs = fold_targets(wires, lower, upper, detector, blocks)
    sums, diffs, folded = call(
        functools.partial(prepare, share),
        [((all_rows, width), f32)] * 2 + [((all_rows, 2 * width), f32)],
        [whole] * 4, "prepare",
    )(kernel, targets, signs, own)
    narrow = jnp.asarray(channel_tables(planes[0].length, planes[0].rows))
    wide = jnp.asarray(channel_tables(planes[2].length, planes[2].rows))
    own, *sends = call(
        functools.partial(channel_stage, blocks, share),
        [((share, width), f32)] + [((share, width), bf16)] * (blocks - 1),
        [scalars] + [whole] * (3 * blocks + 6), "channel_stage",
        [pltpu.VMEM((CHANNELS, width), f32)],
    )(where, *received, *halo, targets, signs, folded, sums, diffs, narrow, wide)
    returned = [
        lax.ppermute(part, "chan", [(i, (i + s) % blocks) for i in range(blocks)])
        for s, part in enumerate(sends, 1)
    ]

    def in_rows(gain):
        parts = jnp.pad(gain.reshape(blocks, harmonics), ((0, 0), (0, padded - harmonics)))
        return jnp.concatenate([parts, parts], axis=1)[:, :, None]

    inverse = jnp.asarray(inverse_tables(ticks, blocks, padded))
    basis = jnp.concatenate([inverse * in_rows(wide_filter), inverse * in_rows(tight_filter)], axis=2)
    signal, bases = call(
        functools.partial(own_signal, blocks),
        [((share, ticks), f32), ((max(blocks - 1, 1), 2 * width, 2 * ticks), bf16)],
        [scalars] + [whole] * 3, "own_signal",
    )(where, own, basis, roi_mask)
    (out,) = call(
        functools.partial(whole_signal, blocks), [((share, ticks), f32)],
        [whole] * (blocks + 2), "whole_signal",
    )(signal, bases, roi_mask, *returned)
    return out[None]


def solution(mesh):
    placed = (
        P("apa", "chan", None),
        P("apa", None),
        P("apa", None),
        P(None, "chan", None),
        P(),
        P(),
        P("apa", "chan", None),
    )
    return jax.shard_map(
        body, mesh=mesh, in_specs=placed, out_specs=P("apa", "chan", None), check_vma=False
    )
```

time: 536 us -> 55.5 us (0.10)
  the two profiles are of different devices: /device:TPU:24 before, /device:TPU:0 now
where the time goes in v1:
time: 55.5 us; the launch traced here: 55.1 us
  Pallas kernels  21.3 us (38%)
  starting transfers between devices  12 us (22%)
  waiting for transfers between devices  10.7 us (19%)
  local copies, waits for them, and re-layouts  6.51 us (12%)
  between operations  2.8 us (5%)
  other arithmetic  1.91 us (3%)
    pallas_call x1, Pallas kernels, body(): call(functools.partial(channel_stage, blocks, share), [((share, width), f...  11.6 us
    ppermute x4, starting transfers between devices, body(): halo.append(lax.ppermute(bands[way * blocks + s], ('apa', 'chan'), pairs))  11.3 us
    ppermute x2, waiting for transfers between devices, body(): lax.ppermute(part, 'chan', [(i, (i + s) % blocks) for i in range(blocks)])  10.7 us
    unnamed x21, local copies, waits for them, and re-layouts  3.81 us
    pallas_call x1, Pallas kernels, body(): call(functools.partial(prepare, share), [((all_rows, width), f32)] * 2 +...  2.99 us
    pallas_call x1, Pallas kernels, body(): call(functools.partial(near_spectra, blocks), [((share, width), bf16)] +...  2.06 us
    pallas_call x1, Pallas kernels, body(): call(functools.partial(far_spectra, blocks), [((share, width), bf16)] * (...  1.6 us
    pallas_call x1, Pallas kernels, body(): call(functools.partial(whole_signal, blocks), [((share, ticks), f32)], [w...  1.56 us
  transfers between devices with their start and end apart: 6, of which 2 were waited for; matrix products, arithmetic and copies ran while one was open for 4% of the time, Pallas kernels for 11%

profile of v1, /device:TPU:0, one launch (start us, length us, event | category | flops | bytes accessed | tf_op | source)
XLA Modules:
  0.0 55.1 jit_solution(15173960548890873699)
XLA Ops:
  0.0 0.8 %reduce = s32[2560]{0:T(1024)S(1)} reduce(s32[1,2560]{1,0:T(1,128)} %param.12, s32[]{:T(128)} %constant.56.clone.1), dimensions={0}, to_apply=%param.12.reduce_sub_computation | reduce | bytes 20484 | tf_op args[1]
  0.8 1.4 %fusion.3 = (s32[1,1]{1,0:T(1,128)}, s32[1,1]{1,0:T(1,128)}) fusion(s32[1,2]{1,0:T(1,128)} %param.13), kind=kLoop, calls=%fused_computation.22 | loop fusion | bytes 16 | tf_op jit(solution)/shard_map/slice | solution.py:296
  3.6 1.1 %copy-done = bf16[1,1280,256]{2,1,0:T(8,128)(2,1)S(1)} copy-done((bf16[1,1280,256]{2,1,0:T(8,128)(2,1)S(1)}, bf16[1,1280,256]{2,1,0:T(8,128)(2,1)}, u32[]{:S(2)}) %copy-start) | copy-done | bytes 655384
  4.7 0.9 %copy-done.3 = bf16[2,256,128]{2,1,0:T(8,128)(2,1)S(1)} copy-done((bf16[2,256,128]{2,1,0:T(8,128)(2,1)S(1)}, bf16[2,256,128]{2,1,0:T(8,128)(2,1)}, u32[]{:S(2)}) %copy-start.3) | copy-done | bytes 131096
  5.6 2.1 %near_spectra.1 = (bf16[1280,128]{1,0:T(8,128)(2,1)S(1)}, bf16[128,128]{1,0:T(8,128)(2,1)}, bf16[128,128]{1,0:T(8,128)(2,1)}, bf16[128,128]{1,0:T(8,128)(2,1)}, bf16[128,128]{1,0:T(8,128)(2,1)}) custom-call(s32[3]{0:T(128)S(1)} %pad_add_fusion.2.where, bf16[1280,256]{1,0:T(8,128)(2,1)S(1)} %bitcast.14, bf16[2,256,128]{2,1,0:T(8,128)(2,1)S(1)} %copy-done.3, ...), custom_call_target="tpu_custom_call" | custom-call | tf_op jit(solution)/shard_map/near_spectra/pallas_call | solution.py:313
  7.7 0.7 %copy-done.4 = bf16[1280,128]{1,0:T(8,128)(2,1)} copy-done((bf16[1280,128]{1,0:T(8,128)(2,1)}, bf16[1280,128]{1,0:T(8,128)(2,1)S(1)}, u32[]{:S(2)}) %copy-start.4) | copy-done | bytes 327704
  8.4 3.0 %collective-permute-start.1 = (bf16[128,128]{1,0:T(8,128)(2,1)}, bf16[128,128]{1,0:T(8,128)(2,1)}, u32[]{:S(2)}, u32[]{:S(2)}) collective-permute-start(bf16[128,128]{1,0:T(8,128)(2,1)} %get-tuple-element.17), channel_id=1, source_target_pairs={{0,2},{1,3},{2,4},{3,5},{4,6},{5,7},{6,8},{7,9},{8,10},{9,11},{10,... | collective-permute-start | bytes 98312 | tf_op jit(solution)/shard_map/ppermute | solution.py:326
  11.3 5.7 %collective-permute-start.2 = (bf16[128,128]{1,0:T(8,128)(2,1)}, bf16[128,128]{1,0:T(8,128)(2,1)}, u32[]{:S(2)}, u32[]{:S(2)}) collective-permute-start(bf16[128,128]{1,0:T(8,128)(2,1)} %get-tuple-element.18), channel_id=1, source_target_pairs={{0,3},{1,2},{2,5},{3,4},{4,7},{5,6},{6,9},{7,8},{8,11},{9,10},{10,... | collective-permute-start | bytes 98312 | tf_op jit(solution)/shard_map/ppermute | solution.py:326
  17.0 1.3 %collective-permute-start.3 = (bf16[128,128]{1,0:T(8,128)(2,1)}, bf16[128,128]{1,0:T(8,128)(2,1)}, u32[]{:S(2)}, u32[]{:S(2)}) collective-permute-start(bf16[128,128]{1,0:T(8,128)(2,1)} %get-tuple-element.19), channel_id=1, source_target_pairs={{2,0},{3,1},{4,2},{5,3},{6,4},{7,5},{8,6},{9,7},{10,8},{11,9},{12,... | collective-permute-start | bytes 98312 | tf_op jit(solution)/shard_map/ppermute | solution.py:326
  18.3 1.4 %collective-permute-start.4 = (bf16[128,128]{1,0:T(8,128)(2,1)}, bf16[128,128]{1,0:T(8,128)(2,1)}, u32[]{:S(2)}, u32[]{:S(2)}) collective-permute-start(bf16[128,128]{1,0:T(8,128)(2,1)} %get-tuple-element.20), channel_id=1, source_target_pairs={{2,1},{3,0},{4,3},{5,2},{6,5},{7,4},{8,7},{9,6},{10,9},{11,8},{12,... | collective-permute-start | bytes 98312 | tf_op jit(solution)/shard_map/ppermute | solution.py:326
  19.7 1.6 %far_spectra.1 = bf16[1280,128]{1,0:T(8,128)(2,1)} custom-call(s32[3]{0:T(128)S(1)} %pad_add_fusion.2.where, bf16[1280,256]{1,0:T(8,128)(2,1)S(1)} %bitcast.15, bf16[2,256,128]{2,1,0:T(8,128)(2,1)S(1)} %copy-done.3), custom_call_target="tpu_custom_call" | custom-call | tf_op jit(solution)/shard_map/far_spectra/pallas_call | solution.py:303
  21.3 0.5 collective-permute-start
  23.2 0.7 %reshape.16 = f32[2,64]{1,0:T(2,128)} reshape(f32[128]{0:T(128)S(1)} %copy-done.8) | data formatting | bytes 1024 | tf_op jit(solution)/shard_map/reshape | solution.py:347
  23.8 0.6 %reshape.17 = f32[2,64]{1,0:T(2,128)} reshape(f32[128]{0:T(128)S(1)} %copy-done.9) | data formatting | bytes 1024 | tf_op jit(solution)/shard_map/reshape | solution.py:347
  24.5 0.8 %pad_maximum_fusion.1 = (f32[2,128]{1,0:T(2,128)S(1)}, f32[2,128]{1,0:T(2,128)S(1)}) fusion(f32[2,64]{1,0:T(2,128)} %reshape.16, f32[2,64]{1,0:T(2,128)} %reshape.17), kind=kLoop, calls=%fused_computation.15 | loop fusion | flops 512 | bytes 3072 | tf_op jit(solution)/shard_map/concatenate | solution.py:348
  25.5 1.0 %copy-done.5 = bf16[1280,128]{1,0:T(8,128)(2,1)S(1)} copy-done((bf16[1280,128]{1,0:T(8,128)(2,1)S(1)}, bf16[1280,128]{1,0:T(8,128)(2,1)}, u32[]{:S(2)}) %copy-start.5) | copy-done | bytes 327704
  26.4 3.0 %prepare.1 = (f32[1456,128]{1,0:T(8,128)S(1)}, f32[1456,128]{1,0:T(8,128)S(1)}, f32[1456,256]{1,0:T(8,128)S(1)}) custom-call(f32[2,64,2816]{2,1,0:T(8,128)S(1)} %copy-done.2, s32[1,3072]{1,0:T(1,128)S(1)} %bitcast.20, f32[1,3072]{1,0:T(1,128)S(1)} %bitcast.18, bf16[1280,128]{1,0:T(8,128)(2,1)S(1)} %copy-done.5), custom_call_target="tpu_custom_call" | custom-call | tf_op jit(solution)/shard_map/prepare/pallas_call | solution.py:328
  29.5 2.3 %collective-permute-done.refs_0_ = bf16[1280,128]{1,0:T(8,128)(2,1)S(1)} collective-permute-done((bf16[1280,128]{1,0:T(8,128)(2,1)}, bf16[1280,128]{1,0:T(8,128)(2,1)S(1)}, u32[]{:S(2)}, u32[]{:S(2)}) %collective-permute-start) | collective-permute-done | bytes 327712 | tf_op jit(solution)/shard_map/ppermute | solution.py:308
  31.8 11.6 %channel_stage.1 = (f32[1280,128]{1,0:T(8,128)S(1)}, bf16[1280,128]{1,0:T(8,128)(2,1)S(1)}) custom-call(s32[3]{0:T(128)S(1)} %pad_add_fusion.2.where, bf16[1280,128]{1,0:T(8,128)(2,1)S(1)} %collective-permute-done.refs_0_, bf16[128,128]{1,0:T(8,128)(2,1)} %collective-permute-done.1.refs_1_, bf16[128,128]{1,0:T(8,128)(2,1)} %collective-permute-done.2.refs_2_, ...), custom_call_target="tpu_custom_call" | custom-call | tf_op jit(solution)/shard_map/channel_stage/pallas_call | solution.py:335
  43.4 0.2 collective-permute-start.5
  43.5 0.1 broadcast_multiply_fusion.1
  43.7 1.5 %own_signal.1 = (f32[1280,256]{1,0:T(8,128)S(1)}, bf16[1,256,512]{2,1,0:T(8,128)(2,1)S(1)}) custom-call(s32[3]{0:T(128)S(1)} %pad_add_fusion.2.where, f32[1280,128]{1,0:T(8,128)S(1)} %get-tuple-element.25.own, f32[2,128,512]{2,1,0:T(8,128)S(1)} %pad_maximum_fusion.basis, s32[80,4]{1,0:T(8,128)S(1)} %bitcast.16), custom_call_target="tpu_custom_call" | custom-call | tf_op jit(solution)/shard_map/own_signal/pallas_call | solution.py:352
  45.2 8.4 %collective-permute-done.5.refs_0_ = bf16[1280,128]{1,0:T(8,128)(2,1)S(1)} collective-permute-done((bf16[1280,128]{1,0:T(8,128)(2,1)S(1)}, bf16[1280,128]{1,0:T(8,128)(2,1)S(1)}, u32[]{:S(2)}, u32[]{:S(2)}) %collective-permute-start.5) | collective-permute-done | bytes 327712 | tf_op jit(solution)/shard_map/ppermute | solution.py:342
  53.6 1.6 %whole_signal.1 = f32[1280,256]{1,0:T(8,128)} custom-call(f32[1280,256]{1,0:T(8,128)S(1)} %get-tuple-element.26.signal, bf16[1,256,512]{2,1,0:T(8,128)(2,1)S(1)} %get-tuple-element.27.bases, s32[80,4]{1,0:T(8,128)S(1)} %bitcast.17, bf16[1280,128]{1,0:T(8,128)(2,1)S(1)} %collective-permute-done.5.refs_0_), custom_call_target="tpu_custom_call" | custom-call | tf_op jit(solution)/shard_map/whole_signal/pallas_call | solution.py:357
  (32 shorter events, 0.4 us)
Async XLA Ops:
  0.0 23.1 %copy-start.8 = (f32[128]{0:T(128)S(1)}, f32[128]{0:T(128)}, u32[]{:S(2)}) copy-start(f32[128]{0:T(128)} %param.15) | copy-start | bytes 1540
  0.0 23.8 %copy-start.9 = (f32[128]{0:T(128)S(1)}, f32[128]{0:T(128)}, u32[]{:S(2)}) copy-start(f32[128]{0:T(128)} %param.16) | copy-start | bytes 1540
  0.0 25.3 %copy-start.7 = (s32[1,80,4]{1,2,0:T(4,128)S(1)}, s32[1,80,4]{1,2,0:T(4,128)}, u32[]{:S(2)}) copy-start(s32[1,80,4]{1,2,0:T(4,128)} %param.17) | copy-start | bytes 3844
  3.6 1.1 %copy-start = (bf16[1,1280,256]{2,1,0:T(8,128)(2,1)S(1)}, bf16[1,1280,256]{2,1,0:T(8,128)(2,1)}, u32[]{:S(2)}) copy-start(bf16[1,1280,256]{2,1,0:T(8,128)(2,1)} %param.11) | copy-start | bytes 1966084
  4.7 0.9 %copy-start.3 = (bf16[2,256,128]{2,1,0:T(8,128)(2,1)S(1)}, bf16[2,256,128]{2,1,0:T(8,128)(2,1)}, u32[]{:S(2)}) copy-start(bf16[2,256,128]{2,1,0:T(8,128)(2,1)} %constant.68.clone.table) | copy-start | bytes 393220
  5.6 19.9 %copy-start.2 = (f32[2,64,2816]{2,1,0:T(8,128)S(1)}, f32[2,64,2816]{2,1,0:T(8,128)}, u32[]{:S(2)}) copy-start(f32[2,64,2816]{2,1,0:T(8,128)} %kernel.1) | copy-start | bytes 4325380
  7.7 0.7 %copy-start.4 = (bf16[1280,128]{1,0:T(8,128)(2,1)}, bf16[1280,128]{1,0:T(8,128)(2,1)S(1)}, u32[]{:S(2)}) copy-start(bf16[1280,128]{1,0:T(8,128)(2,1)S(1)} %get-tuple-element.21.own) | copy-start | bytes 983044
  8.4 21.0 %collective-permute-start.1 = (bf16[128,128]{1,0:T(8,128)(2,1)}, bf16[128,128]{1,0:T(8,128)(2,1)}, u32[]{:S(2)}, u32[]{:S(2)}) collective-permute-start(bf16[128,128]{1,0:T(8,128)(2,1)} %get-tuple-element.17), channel_id=1, source_target_pairs={{0,2},{1,3},{2,4},{3,5},{4,6},{5,7},{6,8},{7,9},{8,10},{9,11},{10,... | collective-permute-start | bytes 98312 | tf_op jit(solution)/shard_map/ppermute | solution.py:326
  11.3 18.1 %collective-permute-start.2 = (bf16[128,128]{1,0:T(8,128)(2,1)}, bf16[128,128]{1,0:T(8,128)(2,1)}, u32[]{:S(2)}, u32[]{:S(2)}) collective-permute-start(bf16[128,128]{1,0:T(8,128)(2,1)} %get-tuple-element.18), channel_id=1, source_target_pairs={{0,3},{1,2},{2,5},{3,4},{4,7},{5,6},{6,9},{7,8},{8,11},{9,10},{10,... | collective-permute-start | bytes 98312 | tf_op jit(solution)/shard_map/ppermute | solution.py:326
  17.0 12.5 %collective-permute-start.3 = (bf16[128,128]{1,0:T(8,128)(2,1)}, bf16[128,128]{1,0:T(8,128)(2,1)}, u32[]{:S(2)}, u32[]{:S(2)}) collective-permute-start(bf16[128,128]{1,0:T(8,128)(2,1)} %get-tuple-element.19), channel_id=1, source_target_pairs={{2,0},{3,1},{4,2},{5,3},{6,4},{7,5},{8,6},{9,7},{10,8},{11,9},{12,... | collective-permute-start | bytes 98312 | tf_op jit(solution)/shard_map/ppermute | solution.py:326
  18.3 13.5 %copy-start.1 = (bf16[4,416,416]{2,1,0:T(8,128)(2,1)S(1)}, bf16[4,416,416]{2,1,0:T(8,128)(2,1)}, u32[]{:S(2)}) copy-start(bf16[4,416,416]{2,1,0:T(8,128)(2,1)} %constant.69.clone.refs_10_) | copy-start | bytes 4153348
  18.3 11.2 %collective-permute-start.4 = (bf16[128,128]{1,0:T(8,128)(2,1)}, bf16[128,128]{1,0:T(8,128)(2,1)}, u32[]{:S(2)}, u32[]{:S(2)}) collective-permute-start(bf16[128,128]{1,0:T(8,128)(2,1)} %get-tuple-element.20), channel_id=1, source_target_pairs={{2,1},{3,0},{4,3},{5,2},{6,5},{7,4},{8,7},{9,6},{10,9},{11,8},{12,... | collective-permute-start | bytes 98312 | tf_op jit(solution)/shard_map/ppermute | solution.py:326
  21.3 10.5 %collective-permute-start = (bf16[1280,128]{1,0:T(8,128)(2,1)}, bf16[1280,128]{1,0:T(8,128)(2,1)S(1)}, u32[]{:S(2)}, u32[]{:S(2)}) collective-permute-start(bf16[1280,128]{1,0:T(8,128)(2,1)} %far_spectra.1), channel_id=1, source_target_pairs={{0,1},{1,0},{2,3},{3,2},{4,5},{5,4},{6,7},{7,6},{8,9},{9,8},{10,11... | collective-permute-start | bytes 983048 | tf_op jit(solution)/shard_map/ppermute | solution.py:308
  25.5 1.0 %copy-start.5 = (bf16[1280,128]{1,0:T(8,128)(2,1)S(1)}, bf16[1280,128]{1,0:T(8,128)(2,1)}, u32[]{:S(2)}) copy-start(bf16[1280,128]{1,0:T(8,128)(2,1)} %copy-done.4) | copy-start | bytes 983044
  31.8 11.7 %copy-start.6 = (f32[2,128,256]{2,1,0:T(8,128)S(1)}, f32[2,128,256]{2,1,0:T(8,128)}, u32[]{:S(2)}) copy-start(f32[2,128,256]{2,1,0:T(8,128)} %constant.71.clone) | copy-start | bytes 786436
  43.4 10.2 %collective-permute-start.5 = (bf16[1280,128]{1,0:T(8,128)(2,1)S(1)}, bf16[1280,128]{1,0:T(8,128)(2,1)S(1)}, u32[]{:S(2)}, u32[]{:S(2)}) collective-permute-start(bf16[1280,128]{1,0:T(8,128)(2,1)S(1)} %get-tuple-element.28), channel_id=1, source_target_pairs={{0,1},{1,0},{2,3},{3,2},{4,5},{5,4},{6,7},{7,6},{8,9},{9,8},{10,11... | collective-permute-start | bytes 983048 | tf_op jit(solution)/shard_map/ppermute | solution.py:342

commit v2 on v1

v2 whole, which is shorter than its diff:
```python
import functools
import math

import jax
import jax.numpy as jnp
import ml_dtypes
import numpy as np
from jax import lax
from jax.experimental import pallas as pl
from jax.experimental.pallas import tpu as pltpu
from jax.sharding import PartitionSpec as P

PU = 800
PV = 800
PW = 960
HALO_CH = 128
BC = 16
BT = 64
CHANNELS = 2560

two_pi = 2.0 * math.pi
lane = 128
f32 = jnp.float32
bf16 = jnp.bfloat16
whole = pl.BlockSpec(memory_space=pltpu.VMEM)
scalars = pl.BlockSpec(memory_space=pltpu.SMEM)
pinned = pl.BlockSpec(memory_space=pltpu.HBM)


def near(array):
    return pltpu.with_memory_space_constraint(array, pltpu.VMEM)


def distant(array):
    return pltpu.with_memory_space_constraint(array, pltpu.HBM)


def ceil_to(size, step):
    return -(-size // step) * step


class Plane:
    def __init__(self, length, wire, count, keep, kernel_start, row):
        self.length, self.wire, self.count, self.keep = length, wire, count, keep
        self.kernel_start, self.row = kernel_start, row
        self.half = length // 2
        self.rows = ceil_to(self.half + 1, 16)


def make_planes():
    found, row, start = [], 0, 0
    for length, wire, count, keep in (
        (PU, 0, PU, 0),
        (PV, PU, PV, 0),
        (PW + 2 * HALO_CH, PU + PV, PW, HALO_CH),
    ):
        found.append(Plane(length, wire, count, keep, start, row))
        row += found[-1].rows
        start += length
    return found


planes = make_planes()
all_rows = planes[-1].row + planes[-1].rows


def split(values):
    high = values.astype(bf16)
    return high, (values - high.astype(f32)).astype(bf16)


def channel_tables(length, rows):
    index = np.arange(rows)
    angles = (index[:, None] * index[None, :] % length) * (two_pi / length)
    inside = (index <= length // 2).astype(np.float64)
    mask = inside[:, None] * inside[None, :]
    parts = []
    for values in (np.cos(angles) * mask, np.sin(angles) * mask):
        high = values.astype(np.float32).astype(ml_dtypes.bfloat16)
        parts += [high, (values - high.astype(np.float64)).astype(np.float32).astype(ml_dtypes.bfloat16)]
    return np.stack(parts)


def tick_angles(ticks):
    return (np.arange(ticks)[:, None] * np.arange(ticks // 2)[None, :] % ticks) * (two_pi / ticks)


def in_blocks(values, blocks, padded):
    parts = np.stack(np.split(values, blocks, axis=-1))
    return np.pad(parts, [(0, 0)] * (parts.ndim - 1) + [(0, padded - parts.shape[-1])])


def forward_tables(ticks, blocks, padded):
    angles = tick_angles(ticks)
    halves = [in_blocks(part, blocks, padded) for part in (np.cos(angles), -np.sin(angles))]
    return np.concatenate(halves, axis=-1).astype(np.float32).astype(ml_dtypes.bfloat16)


def inverse_tables(ticks, blocks, padded):
    angles = tick_angles(ticks)
    weights = np.where(np.arange(ticks // 2) == 0, 1.0, 2.0) / ticks
    halves = [in_blocks(part * weights, blocks, padded) for part in (np.cos(angles), -np.sin(angles))]
    return np.ascontiguousarray(np.swapaxes(np.concatenate(halves, axis=-1), 1, 2)).astype(np.float32)


def dot(left, right):
    return jnp.dot(left, right, preferred_element_type=f32)


def one_hot(rows, first, targets):
    numbers = lax.broadcasted_iota(jnp.int32, (rows, targets.shape[1]), 0) + first
    return jnp.where(numbers == targets, 1.0, 0.0).astype(bf16)


def far_spectra(blocks, where, frames, table, *refs):
    outs, (rows, columns, sems) = refs[: blocks - 1], refs[blocks - 1 :]
    parts = 4
    size = frames.shape[0] // parts
    loads = [pltpu.make_async_copy(table, columns, sems.at[parts])]
    spans = [pl.ds(i * size, size) for i in range(parts)]
    reads = [pltpu.make_async_copy(frames.at[span], rows.at[span], sems.at[i]) for i, span in enumerate(spans)]
    for copy in loads + reads:
        copy.start()
    for copy in loads:
        copy.wait()
    for copy, span in zip(reads, spans):
        copy.wait()
        for s, out in enumerate(outs, 1):
            out[span, :] = dot(rows[span, :], columns[lax.rem(where[0] + s, blocks)]).astype(bf16)


def wires_of(wires, block, share):
    if wires.shape[0] > 1:
        return wires[pl.ds(block, 1), :]
    return wires[:, pl.ds(pl.multiple_of(block * share, lane), share)]


def edge_bands(blocks, where, neighbours, frames, table, wires, *bands):
    mine = wires_of(wires, where[0], frames.shape[0])
    head, tail = PU + PV, CHANNELS - HALO_CH
    to_next = jnp.where(neighbours[0, 1] == where[1] + 1, tail, head)
    to_before = jnp.where(neighbours[0, 0] == where[1] - 1, head, tail)
    for first, out in zip((to_next, to_before), bands):
        rows = dot(one_hot(HALO_CH, first, mine), frames[...]).astype(bf16)
        for s in range(blocks):
            spectra = dot(rows, table[lax.rem(where[0] + s, blocks)])
            out[s * HALO_CH : (s + 1) * HALO_CH, :] = spectra.astype(bf16)


def rotated(values):
    half = values.shape[1] // 2
    first = lax.broadcasted_iota(jnp.int32, values.shape, 1) < half
    turned = pltpu.roll(values, half, 1)
    return jnp.where(first, turned, -turned)


def fold_of(offset, length, row):
    behind = 2 * offset > length
    return row + jnp.where(behind, length - offset, offset), jnp.where(behind, -1.0, 1.0)


def fold_of_wires(wires):
    first, second = wires < PU, wires < PU + PV
    offset = jnp.where(first, wires, jnp.where(second, wires - PU, wires - (PU + PV) + HALO_CH))
    length = jnp.where(first, PU, jnp.where(second, PV, planes[2].length))
    row = jnp.where(first, planes[0].row, jnp.where(second, planes[1].row, planes[2].row))
    return fold_of(offset, length, row)


def fold_of_halo(begin):
    offset = lax.broadcasted_iota(jnp.int32, (1, HALO_CH), 1) + begin
    return fold_of(offset, planes[2].length, planes[2].row)


def sign_columns(signs, width):
    return jnp.transpose(jnp.broadcast_to(signs, (width, signs.shape[1])))


def fold_operand(spectra, signs):
    turned = rotated(spectra.astype(f32)) * sign_columns(signs, spectra.shape[1])
    return jnp.concatenate([spectra, turned.astype(bf16)], axis=1)


def prepare(blocks, where, kernel_source, wires, frames, table, *refs):
    sources, (sums, diffs, folded), kept = refs[:2], refs[2:5], refs[5:7]
    kernel, sems = refs[7:]
    harmonics, width = kernel.shape[1], sums.shape[1]
    kernel_copy = pltpu.make_async_copy(kernel_source, kernel, sems.at[0])
    kernel_copy.start()
    copies = [pltpu.make_async_copy(sources[i], kept[i], sems.at[1 + i]) for i in range(2)]
    for copy in copies:
        copy.start()
    spare = width // 2 - harmonics
    targets, signs = fold_of_wires(wires_of(wires, where[0], frames.shape[0]))
    spectra = dot(frames[...], table[where[0]])
    turned = rotated(spectra) * sign_columns(signs, width)
    operand = jnp.concatenate(split(spectra) + split(turned), axis=1)
    for plane in planes:
        rows = pl.ds(plane.row, plane.rows)
        both = dot(one_hot(plane.rows, plane.row, targets), operand)
        folded[rows, :width] = both[:, :width] + both[:, width : 2 * width]
        folded[rows, width:] = both[:, 2 * width : 3 * width] + both[:, 3 * width :]
    kernel_copy.wait()
    for plane in planes:
        rows = pl.ds(plane.row, plane.rows)
        start = plane.kernel_start // lane * lane
        stop = ceil_to(plane.kernel_start + plane.length, lane)
        offset = plane.kernel_start - start
        parts = []
        for z in range(2):
            parts.append(kernel[z, :, start:stop])
            if spare:
                parts.append(jnp.zeros((spare, stop - start), f32))
        values = jnp.concatenate(parts, axis=0)
        direct = jnp.transpose(values[:, : ceil_to(offset + plane.rows, lane)])[offset : offset + plane.rows]
        row = lax.broadcasted_iota(jnp.int32, (plane.rows, 1), 0)
        source = jnp.where((row > 0) & (row < plane.half), plane.length - row + offset, -1)
        column = lax.broadcasted_iota(jnp.int32, (plane.rows, stop - start), 1)
        matrix = jnp.where(column == source, 1.0, 0.0).astype(bf16)
        both = lax.dot_general(
            matrix, jnp.concatenate(split(values), axis=0), (((1,), (1,)), ((), ())), preferred_element_type=f32
        )
        mirror = (both[:, :width] + both[:, width:]) * (1.0 / plane.length)
        row = lax.broadcasted_iota(jnp.int32, (plane.rows, width), 0)
        direct = jnp.where(row <= plane.half, direct * (1.0 / plane.length), 0.0)
        sums[rows, :] = direct + mirror
        diffs[rows, :] = direct - mirror
    for copy in copies:
        copy.wait()


def two_pass(high, low, values):
    width = values.shape[1]
    joined = jnp.concatenate(split(values), axis=1)
    both = dot(high, joined) + dot(low, joined)
    return both[:, :width] + both[:, width:]


def times(values, factor):
    half = values.shape[1] // 2
    first = lax.broadcasted_iota(jnp.int32, values.shape, 1) < half
    other = pltpu.roll(factor, half, 1)
    real = jnp.where(first, factor, other)
    imag = jnp.where(first, other, factor)
    return values * real - rotated(values) * imag


def far_operand(blocks, share, where, wires, received):
    targets, signs = [], []
    for s in range(1, blocks):
        target, sign = fold_of_wires(wires_of(wires, lax.rem(where[0] + blocks - s, blocks), share))
        targets.append(target)
        signs.append(sign)
    operand = fold_operand(jnp.concatenate([ref[...] for ref in received], axis=0), jnp.concatenate(signs, axis=1))
    return jnp.concatenate(targets, axis=1), operand


def halo_operand(blocks, where, neighbours, halo):
    bands, targets, signs = [], [], []
    lower, upper = neighbours[0, 0], neighbours[0, 1]
    never = -4 * planes[2].length
    for way in range(2):
        total = halo[way][:HALO_CH, :].astype(f32)
        for ref in halo[2:]:
            total += ref[way * HALO_CH : (way + 1) * HALO_CH, :].astype(f32)
        bands.append(total.astype(bf16))
        other = where[1] + 2 * way - 1
        begin = jnp.where(upper == other, planes[2].length - HALO_CH, never)
        begin = jnp.where(lower == other, 0, begin)
        target, sign = fold_of_halo(jnp.where(other < 0, never, begin))
        targets.append(target)
        signs.append(sign)
    operand = fold_operand(jnp.concatenate(bands, axis=0), jnp.concatenate(signs, axis=1))
    return jnp.concatenate(targets, axis=1), operand


def plane_result(plane, far, halo, folded, sums, diffs, table):
    rows = pl.ds(plane.row, plane.rows)
    both = folded[rows, :] + dot(one_hot(plane.rows, plane.row, far[0]), far[1])
    if plane.keep:
        both += dot(one_hot(plane.rows, plane.row, halo[0]), halo[1])
    width = both.shape[1] // 2
    even = two_pass(table[0], table[1], both[:, :width])
    odd = two_pass(table[2], table[3], both[:, width:])
    plus, minus = sums[rows, :], diffs[rows, :]
    total = times(even, plus) + times(odd, minus)
    gap = times(even, minus) + times(odd, plus)
    kept = slice(plane.keep, plane.rows)
    cosine = two_pass(table[0, kept], table[1, kept], total)
    sine = two_pass(table[2, kept], table[3, kept], -rotated(gap))
    straight = plane.count // 2
    back = jnp.concatenate(split(cosine - sine), axis=1)
    row = lax.broadcasted_iota(jnp.int32, (straight, back.shape[0]), 0)
    column = lax.broadcasted_iota(jnp.int32, (straight, back.shape[0]), 1) + plane.keep
    turned = dot(jnp.where(column == plane.half - row, 1.0, 0.0).astype(bf16), back)
    return (cosine + sine)[:straight], turned[:, :width] + turned[:, width:]


def put(result, plane, *operands):
    lower, upper = plane_result(plane, *operands)
    result[: plane.count // 2, :] = lower
    result[plane.count // 2 : plane.count, :] = upper


def all_planes(blocks, share, where, neighbours, *refs):
    received, halo = refs[: blocks - 1], refs[blocks - 1 : 2 * blocks]
    wires, folded, sums, diffs, narrow, wide, own = refs[2 * blocks : 2 * blocks + 7]
    sends, result = refs[2 * blocks + 7 : 3 * blocks + 6], refs[3 * blocks + 6]
    far = far_operand(blocks, share, where, wires, received)
    bands = halo_operand(blocks, where, neighbours, halo)
    for plane in planes:
        operands = (far, bands, folded, sums, diffs, wide if plane.keep else narrow)
        put(result.at[pl.ds(plane.wire, plane.count)], plane, *operands)
    here = where[0]
    own[...] = result[pl.ds(pl.multiple_of(here * share, share), share), :]
    for shift, out in enumerate(sends, 1):
        first = pl.multiple_of(lax.rem(here + shift, blocks) * share, share)
        out[...] = result[pl.ds(first, share), :].astype(bf16)


def middle_plane(share, where, far, wires, folded, sums, diffs, narrow, send, own, result):
    middle = planes[1]
    operand = far_operand(2, share, where, wires, [far])
    put(result, middle, operand, None, folded, sums, diffs, narrow)
    below = share - middle.wire
    above = middle.count - below

    @pl.when(where[0] == 0)
    def _():
        send[:above, :] = result[below:, :].astype(bf16)
        send[above:, :] = jnp.zeros((below - above, send.shape[1]), bf16)
        own[...] = result[:below, :]

    @pl.when(where[0] != 0)
    def _():
        send[...] = result[:below, :].astype(bf16)
        own[:above, :] = result[below:, :]
        own[above:, :] = jnp.zeros((below - above, own.shape[1]), f32)


def outer_plane(share, where, neighbours, far, halo0, halo1, halo2, wires, folded, sums, diffs, narrow, wide, send, result):
    first, _, last = planes
    operand = far_operand(2, share, where, wires, [far])

    @pl.when(where[0] == 0)
    def _():
        bands = halo_operand(2, where, neighbours, (halo0, halo1, halo2))
        put(result, last, operand, bands, folded, sums, diffs, wide)
        send[...] = result[...].astype(bf16)

    @pl.when(where[0] != 0)
    def _():
        put(result, first, operand, None, folded, sums, diffs, narrow)
        send[: first.count, :] = result[: first.count, :].astype(bf16)
        send[first.count :, :] = jnp.zeros((last.count - first.count, send.shape[1]), bf16)


def own_planes(share, where, neighbours, far, halo0, halo1, halo2, wires, folded, sums, diffs, narrow, wide, part, basis,
               wide_filter, tight_filter, mask, signal, bases, inside, result, basis_room, sem):
    first, middle, last = planes
    basis_copy = pltpu.make_async_copy(basis, basis_room, sem)
    basis_copy.start()
    operand = far_operand(2, share, where, wires, [far])
    above = middle.count - (share - middle.wire)

    @pl.when(where[0] == 0)
    def _():
        put(result, first, operand, None, folded, sums, diffs, narrow)
        result[first.count :, :] = part[...]

    @pl.when(where[0] != 0)
    def _():
        bands = halo_operand(2, where, neighbours, (halo0, halo1, halo2))
        put(result.at[pl.ds(above, last.count)], last, operand, bands, folded, sums, diffs, wide)
        result[:above, :] = part[:above, :]

    basis_copy.wait()
    own_signal(2, where, result, basis_room, wide_filter, tight_filter, mask, signal, bases, inside)


def spread_mask(mask, share, ticks):
    marked = jnp.where(mask == 1, 1.0, 0.0).astype(bf16)
    row = lax.broadcasted_iota(jnp.int32, (share, mask.shape[1]), 0)
    column = lax.broadcasted_iota(jnp.int32, (share, mask.shape[1]), 1)
    taken = jnp.where(row // BC == column, 1.0, 0.0).astype(bf16)
    rows = lax.dot_general(taken, marked, (((1,), (1,)), ((), ())), preferred_element_type=f32).astype(bf16)
    row = lax.broadcasted_iota(jnp.int32, (mask.shape[0], ticks), 0)
    column = lax.broadcasted_iota(jnp.int32, (mask.shape[0], ticks), 1)
    return dot(rows, jnp.where(column // BT == row, 1.0, 0.0).astype(bf16))


def chosen_signal(both, inside):
    ticks = inside.shape[1]
    return jnp.where(inside > 0.5, both[:, :ticks], both[:, ticks:])


def scaled_basis(block, blocks, basis, filters, harmonics):
    padded = basis.shape[1] // 2
    ticks = basis.shape[2]
    spread = []
    for gain in filters:
        columns = gain[...] if blocks == 1 else None
        for b in range(blocks):
            piece = gain[:, b * harmonics : (b + 1) * harmonics]
            columns = piece if columns is None else jnp.where(block == b, piece, columns)
        if padded > harmonics:
            columns = jnp.concatenate([columns, jnp.zeros((1, padded - harmonics), f32)], axis=1)
        columns = jnp.concatenate([columns, columns], axis=1)
        tall = jnp.transpose(jnp.broadcast_to(columns, (lane, 2 * padded)))
        spread.append(jnp.concatenate([tall] * (ticks // lane), axis=1))
    values = basis[block]
    return split(jnp.concatenate([values * part for part in spread], axis=1))


def own_signal(blocks, where, own, basis, wide_filter, tight_filter, mask, signal, bases, inside):
    here = where[0]
    ticks = signal.shape[1]
    harmonics = wide_filter.shape[1] // blocks
    filters = (wide_filter, tight_filter)
    high, low = scaled_basis(here, blocks, basis, filters, harmonics)
    joined = jnp.concatenate(split(own[...]), axis=1)
    both = dot(joined, jnp.concatenate([high, high], axis=0))
    both += dot(joined, jnp.concatenate([low, low], axis=0))
    inside[...] = spread_mask(mask[...], own.shape[0], ticks)
    signal[...] = chosen_signal(both, inside[...])
    for shift in range(1, blocks):
        parts = scaled_basis(lax.rem(here + blocks - shift, blocks), blocks, basis, filters, harmonics)
        bases[shift - 1] = jnp.concatenate(parts, axis=0)


def whole_signal(blocks, signal, bases, inside, *refs):
    out = refs[-1]
    both = None
    for shift in range(1, blocks):
        values = refs[shift - 1][...]
        term = dot(jnp.concatenate([values, values], axis=1), bases[shift - 1])
        both = term if both is None else both + term
    if both is None:
        out[...] = signal[...]
    else:
        out[...] = signal[...] + chosen_signal(both, inside[...])


def part_signal(spans, where, signal, bases, inside, values, *refs):
    out, room, sems = refs[-3:]
    step = room.shape[0] // sems.shape[0]
    for device, (first, count) in enumerate(spans):

        @pl.when(where[0] == device)
        def _(first=first, count=count):
            copies = []
            for i in range(count // step):
                some = values[i * step : (i + 1) * step, :]
                both = dot(jnp.concatenate([some, some], axis=1), bases[0])
                rows, slot = pl.ds(first + i * step, step), pl.ds(i * step, step)
                room[slot, :] = signal[rows, :] + chosen_signal(both, inside[rows, :])
                copies.append(pltpu.make_async_copy(room.at[slot], out.at[rows], sems.at[i]))
                copies[-1].start()
            for copy in copies:
                copy.wait()


def call(kernel, outs, ins, name, scratch=(), final=False, aliases=None):
    kind = jax.ShapeDtypeStruct if final else pltpu.VMEM
    return pl.pallas_call(
        kernel,
        out_shape=[kind(shape, dtype) for shape, dtype in outs],
        in_specs=ins,
        out_specs=[pinned if final else whole] * len(outs),
        scratch_shapes=scratch,
        compiler_params=pltpu.CompilerParams(vmem_limit_bytes=28 * 1024 * 1024),
        cost_estimate=pl.CostEstimate(flops=0, bytes_accessed=0, transcendentals=0),
        input_output_aliases=aliases or {},
        name=name,
    )


def body(frames, link_to_wire, neighbours, kernel, wide_filter, tight_filter, roi_mask):
    frames, roi_mask = frames[0], roi_mask[0]
    share, ticks = frames.shape
    blocks = lax.axis_size("chan")
    detectors = lax.axis_size("apa")
    padded = max(kernel.shape[1], lane // 2)
    width = 2 * padded
    here = lax.axis_index("chan")
    detector = lax.axis_index("apa")
    where = jnp.stack([here, detector]).astype(jnp.int32)
    wires = link_to_wire if share % lane == 0 else link_to_wire.reshape(blocks, share)
    table = jnp.asarray(forward_tables(ticks, blocks, padded))

    def around(parts):
        return [
            near(lax.ppermute(part, "chan", [(i, (i + s) % blocks) for i in range(blocks)]))
            for s, part in enumerate(parts, 1)
        ]

    *far, frames, table = call(
        functools.partial(far_spectra, blocks),
        [((share, width), bf16)] * (blocks - 1) + [((share, ticks), bf16), ((blocks, ticks, width), bf16)],
        [scalars, pinned, pinned], "far_spectra", [pltpu.SemaphoreType.DMA((5,))],
    )(where, distant(frames), distant(table))
    frames, table = near(frames), near(table)
    received = around(far)
    bands = call(
        functools.partial(edge_bands, blocks), [((blocks * HALO_CH, width), bf16)] * 2,
        [scalars] * 2 + [whole] * 3, "edge_bands",
    )(where, neighbours, frames, table, wires)
    halo = []
    for step, band in zip((1, -1), bands):
        pairs = [(a, a + step) for a in range(detectors) if 0 <= a + step < detectors]
        halo.append(lax.ppermute(band, "apa", pairs))
    shares = [
        jnp.concatenate([band[s * HALO_CH : (s + 1) * HALO_CH] for band in halo]) for s in range(1, blocks)
    ]
    halo = [near(band) for band in halo] + around(shares)
    tables = [channel_tables(planes[i].length, planes[i].rows) for i in (0, 2)]
    ready = call(
        functools.partial(prepare, blocks),
        [((all_rows, width), f32)] * 2 + [((all_rows, 2 * width), f32)] + [(part.shape, bf16) for part in tables],
        [scalars, pinned] + [whole] * 3 + [pinned] * 2, "prepare",
        [pltpu.VMEM(kernel.shape, f32), pltpu.SemaphoreType.DMA((3,))],
    )(where, distant(kernel), wires, frames, table, *(distant(jnp.asarray(part)) for part in tables))
    sums, diffs, folded, narrow, wide = map(near, ready)
    basis = jnp.asarray(inverse_tables(ticks, blocks, padded))
    basis_room = pltpu.VMEM(basis.shape, f32)
    filters = (wide_filter[None], tight_filter[None])
    mask = jnp.transpose(roi_mask)
    signal_shapes = [
        ((share, ticks), f32), ((max(blocks - 1, 1), 2 * width, 2 * ticks), bf16), ((share, ticks), f32)
    ]
    if blocks != 2:
        own, *sends = call(
            functools.partial(all_planes, blocks, share),
            [((share, width), f32)] + [((share, width), bf16)] * (blocks - 1),
            [scalars] * 2 + [whole] * (2 * blocks + 6), "all_planes",
            [pltpu.VMEM((CHANNELS, width), f32)],
        )(where, neighbours, *received, *halo, wires, folded, sums, diffs, narrow, wide)
        returned = around(sends)
        signal, bases, inside = call(
            functools.partial(own_signal, blocks), signal_shapes,
            [scalars] + [whole] * 5, "own_signal",
        )(where, near(own), basis, *filters, mask)
        out = pl.pallas_call(
            functools.partial(whole_signal, blocks),
            out_shape=jax.ShapeDtypeStruct((share, ticks), f32),
            in_specs=[whole] * (blocks + 2),
            out_specs=whole,
            name="whole_signal",
        )(near(signal), near(bases), near(inside), *returned)
        return out[None]

    below, above = share - PU, PU + PV - share
    sent, part = call(
        functools.partial(middle_plane, share), [((below, width), bf16), ((below, width), f32)],
        [scalars] + [whole] * 6, "middle_plane", [pltpu.VMEM((PV, width), f32)],
    )(where, *received, wires, folded, sums, diffs, narrow)
    (early,) = around([sent])
    (sent,) = call(
        functools.partial(outer_plane, share), [((PW, width), bf16)],
        [scalars] * 2 + [whole] * 10, "outer_plane", [pltpu.VMEM((PW, width), f32)],
    )(where, neighbours, *received, *halo, wires, folded, sums, diffs, narrow, wide)
    (late,) = around([sent])
    ready = call(
        functools.partial(own_planes, share), signal_shapes,
        [scalars] * 2 + [whole] * 11 + [pinned] + [whole] * 3, "own_planes",
        [pltpu.VMEM((share, width), f32), basis_room, pltpu.SemaphoreType.DMA],
    )(where, neighbours, *received, *halo, wires, folded, sums, diffs, narrow, wide, near(part), distant(basis), *filters, mask)
    signal, bases, inside = map(near, ready)

    def finish(values, spans, *before):
        step = math.gcd(*(count for _, count in spans))
        rows = max(count for _, count in spans)
        (out,) = call(
            functools.partial(part_signal, spans), [((share, ticks), f32)],
            [scalars] + [whole] * 4 + [pinned] * len(before), "part_signal",
            [pltpu.VMEM((rows, ticks), f32), pltpu.SemaphoreType.DMA((rows // step,))],
            final=True, aliases={5: 0} if before else None,
        )(where, signal, bases, inside, values, *before)
        return out

    out = finish(early, ((PU, below), (0, above)))
    return finish(late, ((0, PU), (above, PW)), out)[None]


def solution(mesh):
    placed = (
        P("apa", "chan", None),
        P("apa", None),
        P("apa", None),
        P(None, "chan", None),
        P(),
        P(),
        P("apa", "chan", None),
    )
    return jax.shard_map(
        body, mesh=mesh, in_specs=placed, out_specs=P("apa", "chan", None), check_vma=False
    )
```

time: 55.5 us -> 41.4 us (0.75)
  the two profiles are of different devices: /device:TPU:0 before, /device:TPU:24 now
where the time goes in v2:
time: 41.4 us; the launch traced here: 40.8 us
  Pallas kernels  25.8 us (62%)
  starting transfers between devices  8.68 us (21%)
  waiting for transfers between devices  4.55 us (11%)
  local copies, waits for them, and re-layouts  1.39 us (3%)
    pallas_call x1, Pallas kernels, body(): call(functools.partial(own_planes, share), signal_shapes, [scalars] * 2 +...  5.33 us
    pallas_call x1, Pallas kernels, body(): call(functools.partial(outer_plane, share), [((PW, width), bf16)], [scala...  5.3 us
    pallas_call x1, Pallas kernels, body(): call(functools.partial(prepare, blocks), [((all_rows, width), f32)] * 2 +...  4.76 us
    ppermute x2, waiting for transfers between devices, body(): halo.append(lax.ppermute(band, 'apa', pairs))  4.54 us
    ppermute x2, starting transfers between devices, body(): halo.append(lax.ppermute(band, 'apa', pairs))  4.37 us
    ppermute x4, starting transfers between devices, around(): lax.ppermute(part, 'chan', [(i, (i + s) % blocks) for i in range(blocks)])  4.31 us
    pallas_call x1, Pallas kernels, body(): call(functools.partial(middle_plane, share), [((below, width), bf16), ((b...  3.3 us
    pallas_call x2, Pallas kernels, finish(): call(functools.partial(part_signal, spans), [((share, ticks), f32)], [sca...  3.27 us
  transfers between devices with their start and end apart: 6, of which 1 were waited for; matrix products, arithmetic and copies ran while one was open for 0% of the time, Pallas kernels for 40%

profile of v2, /device:TPU:24, one launch (start us, length us, event | category | flops | bytes accessed | tf_op | source)
XLA Modules:
  0.0 40.8 jit_solution(13627112619490635760)
XLA Ops:
  0.0 0.1 pad_add_fusion.where
  0.1 2.5 %far_spectra.1 = (bf16[1280,128]{1,0:T(8,128)(2,1)S(1)}, bf16[1280,256]{1,0:T(8,128)(2,1)S(1)}, bf16[2,256,128]{2,1,0:T(8,128)(2,1)S(1)}) custom-call(s32[2]{0:T(128)S(1)} %pad_add_fusion.where, bf16[1280,256]{1,0:T(8,128)(2,1)} %bitcast.12, bf16[2,256,128]{2,1,0:T(8,128)(2,1)} %constant.16.clone.table), custom_call_target="tpu_custom_call" | custom-call | tf_op jit(solution)/shard_map/far_spectra/pallas_call | solution.py:497
  2.6 1.6 %collective-permute-start = (bf16[1280,128]{1,0:T(8,128)(2,1)S(1)}, bf16[1280,128]{1,0:T(8,128)(2,1)S(1)}, u32[]{:S(2)}, u32[]{:S(2)}) collective-permute-start(bf16[1280,128]{1,0:T(8,128)(2,1)S(1)} %get-tuple-element.20), channel_id=1, source_target_pairs={{0,1},{1,0},{2,3},{3,2},{4,5},{5,4},{6,7},{7,6},{8,9},{9,8},{10,11... | collective-permute-start | bytes 983048 | tf_op jit(solution)/shard_map/ppermute | solution.py:493
  4.2 0.7 %copy-done = s32[1,2560]{1,0:T(1,128)S(1)} copy-done((s32[1,2560]{1,0:T(1,128)S(1)}, s32[1,2560]{1,0:T(1,128)}, u32[]{:S(2)}) %copy-start) | copy-done | bytes 10264
  4.9 0.7 %copy-done.2 = s32[1,2]{1,0:T(1,128)S(1)} copy-done((s32[1,2]{1,0:T(1,128)S(1)}, s32[1,2]{1,0:T(1,128)}, u32[]{:S(2)}) %copy-start.2) | copy-done | bytes 32
  5.5 1.3 %edge_bands.1 = (bf16[256,128]{1,0:T(8,128)(2,1)S(1)}, bf16[256,128]{1,0:T(8,128)(2,1)S(1)}) custom-call(s32[2]{0:T(128)S(1)} %pad_add_fusion.where, s32[1,2]{1,0:T(1,128)S(1)} %copy-done.2, bf16[1280,256]{1,0:T(8,128)(2,1)S(1)} %get-tuple-element.21.frames, bf16[2,256,128]{2,1,0:T(8,128)(2,1)S(1)} %get-tuple-element.22.table, s32[1,2560]{1,0:T(1,128)S(1)} %copy-done), custom_call_target="tpu_custom_call" | custom-call | tf_op jit(solution)/shard_map/edge_bands/pallas_call | solution.py:504
  6.9 2.4 %collective-permute-start.2 = (bf16[256,128]{1,0:T(8,128)(2,1)S(1)}, bf16[256,128]{1,0:T(8,128)(2,1)S(1)}, u32[]{:S(2)}, u32[]{:S(2)}) collective-permute-start(bf16[256,128]{1,0:T(8,128)(2,1)S(1)} %get-tuple-element.24), channel_id=1, source_target_pairs={{2,0},{4,2},{6,4},{8,6},{10,8},{12,10},{14,12},{16,14},{18,16},{20... | collective-permute-start | bytes 196616 | tf_op jit(solution)/shard_map/ppermute | solution.py:511
  9.3 1.9 %collective-permute-start.1 = (bf16[256,128]{1,0:T(8,128)(2,1)S(1)}, bf16[256,128]{1,0:T(8,128)(2,1)S(1)}, u32[]{:S(2)}, u32[]{:S(2)}) collective-permute-start(bf16[256,128]{1,0:T(8,128)(2,1)S(1)} %get-tuple-element.23), channel_id=1, source_target_pairs={{0,2},{2,4},{4,6},{6,8},{8,10},{10,12},{12,14},{14,16},{16,18},{18... | collective-permute-start | bytes 196616 | tf_op jit(solution)/shard_map/ppermute | solution.py:511
  11.3 0.0 collective-permute-done.2.halo1
  11.3 4.5 %collective-permute-done.1.halo0 = bf16[256,128]{1,0:T(8,128)(2,1)S(1)} collective-permute-done((bf16[256,128]{1,0:T(8,128)(2,1)S(1)}, bf16[256,128]{1,0:T(8,128)(2,1)S(1)}, u32[]{:S(2)}, u32[]{:S(2)}) %collective-permute-start.1) | collective-permute-done | bytes 65568 | tf_op jit(solution)/shard_map/ppermute | solution.py:511
  15.8 0.0 copy-start.3
  15.8 0.6 %collective-permute-start.3 = (bf16[256,128]{1,0:T(8,128)(2,1)S(1)}, bf16[256,128]{1,0:T(8,128)(2,1)S(1)}, u32[]{:S(2)}, u32[]{:S(2)}) collective-permute-start(bf16[256,128]{1,0:T(8,128)(2,1)S(1)} %pad_maximum_fusion), channel_id=1, source_target_pairs={{0,1},{1,0},{2,3},{3,2},{4,5},{5,4},{6,7},{7,6},{8,9},{9,8},{10,11... | collective-permute-start | bytes 196616 | tf_op jit(solution)/shard_map/ppermute | solution.py:493
  16.4 4.8 %prepare.1 = (f32[1456,128]{1,0:T(8,128)S(1)}, f32[1456,128]{1,0:T(8,128)S(1)}, f32[1456,256]{1,0:T(8,128)S(1)}, bf16[4,416,416]{2,1,0:T(8,128)(2,1)S(1)}, bf16[4,624,624]{2,1,0:T(8,128)(2,1)S(1)}) custom-call(s32[2]{0:T(128)S(1)} %pad_add_fusion.where, f32[2,64,2816]{2,1,0:T(8,128)} %kernel_source.1, s32[1,2560]{1,0:T(1,128)S(1)} %copy-done.1, ...), custom_call_target="tpu_custom_call" | custom-call | tf_op jit(solution)/shard_map/prepare/pallas_call | solution.py:517
  21.2 0.0 collective-permute-done.3.halo2
  21.2 5.3 %outer_plane.1 = bf16[960,128]{1,0:T(8,128)(2,1)S(1)} custom-call(s32[2]{0:T(128)S(1)} %pad_add_fusion.where, s32[1,2]{1,0:T(1,128)S(1)} %copy-done.3, bf16[1280,128]{1,0:T(8,128)(2,1)S(1)} %collective-permute-done.far, bf16[256,128]{1,0:T(8,128)(2,1)S(1)} %collective-permute-done.1.halo0, bf16[256,128]{1,0:T(8,128)(2,1)S(1)} %collective-permute-done.2.halo1, ...), custom_call_target="tpu_custom_call" | custom-call | tf_op jit(solution)/shard_map/outer_plane/pallas_call | solution.py:558
  26.5 0.0 copy-start.4
  26.5 0.0 copy-start.5
  26.6 0.0 copy-start.6
  26.6 0.1 collective-permute-start.4
  26.6 3.3 %middle_plane.1 = (bf16[480,128]{1,0:T(8,128)(2,1)S(1)}, f32[480,128]{1,0:T(8,128)S(1)}) custom-call(s32[2]{0:T(128)S(1)} %pad_add_fusion.where, bf16[1280,128]{1,0:T(8,128)(2,1)S(1)} %collective-permute-done.far, s32[1,2560]{1,0:T(1,128)S(1)} %copy-done.1, f32[1456,256]{1,0:T(8,128)S(1)} %get-tuple-element.25.folded, ...), custom_call_target="tpu_custom_call" | custom-call | tf_op jit(solution)/shard_map/middle_plane/pallas_call | solution.py:553
  30.0 2.1 %collective-permute-start.5 = (bf16[480,128]{1,0:T(8,128)(2,1)S(1)}, bf16[480,128]{1,0:T(8,128)(2,1)S(1)}, u32[]{:S(2)}, u32[]{:S(2)}) collective-permute-start(bf16[480,128]{1,0:T(8,128)(2,1)S(1)} %get-tuple-element.34), channel_id=1, source_target_pairs={{0,1},{1,0},{2,3},{3,2},{4,5},{5,4},{6,7},{7,6},{8,9},{9,8},{10,11... | collective-permute-start | bytes 368648 | tf_op jit(solution)/shard_map/ppermute | solution.py:493
  32.1 5.3 %own_planes.1 = (f32[1280,256]{1,0:T(8,128)S(1)}, bf16[1,256,512]{2,1,0:T(8,128)(2,1)S(1)}, f32[1280,256]{1,0:T(8,128)S(1)}) custom-call(s32[2]{0:T(128)S(1)} %pad_add_fusion.where, s32[1,2]{1,0:T(1,128)S(1)} %copy-done.3, bf16[1280,128]{1,0:T(8,128)(2,1)S(1)} %collective-permute-done.far, bf16[256,128]{1,0:T(8,128)(2,1)S(1)} %collective-permute-done.1.halo0, ...), custom_call_target="tpu_custom_call" | custom-call | tf_op jit(solution)/shard_map/own_planes/pallas_call | solution.py:563
  37.4 1.6 %part_signal.2.refs_0_ = f32[1280,256]{1,0:T(8,128)} custom-call(s32[2]{0:T(128)S(1)} %pad_add_fusion.where, f32[1280,256]{1,0:T(8,128)S(1)} %get-tuple-element.31.signal, bf16[1,256,512]{2,1,0:T(8,128)(2,1)S(1)} %get-tuple-element.32.bases, f32[1280,256]{1,0:T(8,128)S(1)} %get-tuple-element.33.inside, bf16[480,128]{1,0:T(8,128)(2,1)S(1)} %collective-permute-done.5.values), custom_call_target="tpu_custom_call" | custom-call | tf_op jit(solution)/shard_map/part_signal/pallas_call | solution.py:573
  39.0 1.7 %part_signal.3 = f32[1280,256]{1,0:T(8,128)} custom-call(s32[2]{0:T(128)S(1)} %pad_add_fusion.where, f32[1280,256]{1,0:T(8,128)S(1)} %get-tuple-element.31.signal, bf16[1,256,512]{2,1,0:T(8,128)(2,1)S(1)} %get-tuple-element.32.bases, f32[1280,256]{1,0:T(8,128)S(1)} %get-tuple-element.33.inside, ...), custom_call_target="tpu_custom_call", output_to_operand_aliasing={{}: (5, {})} | custom-call | tf_op jit(solution)/shard_map/part_signal/pallas_call | solution.py:573
  (14 shorter events, 0.0 us)
Async XLA Ops:
  0.0 16.4 %copy-start.1 = (s32[1,2560]{1,0:T(1,128)S(1)}, s32[1,2560]{1,0:T(1,128)}, u32[]{:S(2)}) copy-start(s32[1,2560]{1,0:T(1,128)} %wires.9) | copy-start | bytes 30724
  2.6 18.6 %collective-permute-start = (bf16[1280,128]{1,0:T(8,128)(2,1)S(1)}, bf16[1280,128]{1,0:T(8,128)(2,1)S(1)}, u32[]{:S(2)}, u32[]{:S(2)}) collective-permute-start(bf16[1280,128]{1,0:T(8,128)(2,1)S(1)} %get-tuple-element.20), channel_id=1, source_target_pairs={{0,1},{1,0},{2,3},{3,2},{4,5},{5,4},{6,7},{7,6},{8,9},{9,8},{10,11... | collective-permute-start | bytes 983048 | tf_op jit(solution)/shard_map/ppermute | solution.py:493
  4.2 0.7 %copy-start = (s32[1,2560]{1,0:T(1,128)S(1)}, s32[1,2560]{1,0:T(1,128)}, u32[]{:S(2)}) copy-start(s32[1,2560]{1,0:T(1,128)} %wires.9) | copy-start | bytes 30724
  4.9 0.7 %copy-start.2 = (s32[1,2]{1,0:T(1,128)S(1)}, s32[1,2]{1,0:T(1,128)}, u32[]{:S(2)}) copy-start(s32[1,2]{1,0:T(1,128)} %neighbours.5) | copy-start | bytes 28
  6.9 4.4 %collective-permute-start.2 = (bf16[256,128]{1,0:T(8,128)(2,1)S(1)}, bf16[256,128]{1,0:T(8,128)(2,1)S(1)}, u32[]{:S(2)}, u32[]{:S(2)}) collective-permute-start(bf16[256,128]{1,0:T(8,128)(2,1)S(1)} %get-tuple-element.24), channel_id=1, source_target_pairs={{2,0},{4,2},{6,4},{8,6},{10,8},{12,10},{14,12},{16,14},{18,16},{20... | collective-permute-start | bytes 196616 | tf_op jit(solution)/shard_map/ppermute | solution.py:511
  9.3 6.5 %collective-permute-start.1 = (bf16[256,128]{1,0:T(8,128)(2,1)S(1)}, bf16[256,128]{1,0:T(8,128)(2,1)S(1)}, u32[]{:S(2)}, u32[]{:S(2)}) collective-permute-start(bf16[256,128]{1,0:T(8,128)(2,1)S(1)} %get-tuple-element.23), channel_id=1, source_target_pairs={{0,2},{2,4},{4,6},{6,8},{8,10},{10,12},{12,14},{14,16},{16,18},{18... | collective-permute-start | bytes 196616 | tf_op jit(solution)/shard_map/ppermute | solution.py:511
  15.8 5.4 %copy-start.3 = (s32[1,2]{1,0:T(1,128)S(1)}, s32[1,2]{1,0:T(1,128)}, u32[]{:S(2)}) copy-start(s32[1,2]{1,0:T(1,128)} %neighbours.5) | copy-start | bytes 28
  15.8 5.3 %collective-permute-start.3 = (bf16[256,128]{1,0:T(8,128)(2,1)S(1)}, bf16[256,128]{1,0:T(8,128)(2,1)S(1)}, u32[]{:S(2)}, u32[]{:S(2)}) collective-permute-start(bf16[256,128]{1,0:T(8,128)(2,1)S(1)} %pad_maximum_fusion), channel_id=1, source_target_pairs={{0,1},{1,0},{2,3},{3,2},{4,5},{5,4},{6,7},{7,6},{8,9},{9,8},{10,11... | collective-permute-start | bytes 196616 | tf_op jit(solution)/shard_map/ppermute | solution.py:493
  26.5 5.5 %copy-start.4 = (s32[1,80,4]{1,2,0:T(4,128)S(1)}, s32[1,80,4]{1,2,0:T(4,128)}, u32[]{:S(2)}) copy-start(s32[1,80,4]{1,2,0:T(4,128)} %param.17) | copy-start | bytes 3844
  26.5 5.5 %copy-start.5 = (f32[128]{0:T(128)S(1)}, f32[128]{0:T(128)}, u32[]{:S(2)}) copy-start(f32[128]{0:T(128)} %param.15) | copy-start | bytes 1540
  26.6 5.5 %copy-start.6 = (f32[128]{0:T(128)S(1)}, f32[128]{0:T(128)}, u32[]{:S(2)}) copy-start(f32[128]{0:T(128)} %param.16) | copy-start | bytes 1540
  26.6 12.4 %collective-permute-start.4 = (bf16[960,128]{1,0:T(8,128)(2,1)S(1)}, bf16[960,128]{1,0:T(8,128)(2,1)S(1)}, u32[]{:S(2)}, u32[]{:S(2)}) collective-permute-start(bf16[960,128]{1,0:T(8,128)(2,1)S(1)} %outer_plane.1), channel_id=1, source_target_pairs={{0,1},{1,0},{2,3},{3,2},{4,5},{5,4},{6,7},{7,6},{8,9},{9,8},{10,11... | collective-permute-start | bytes 737288 | tf_op jit(solution)/shard_map/ppermute | solution.py:493
  30.0 7.4 %collective-permute-start.5 = (bf16[480,128]{1,0:T(8,128)(2,1)S(1)}, bf16[480,128]{1,0:T(8,128)(2,1)S(1)}, u32[]{:S(2)}, u32[]{:S(2)}) collective-permute-start(bf16[480,128]{1,0:T(8,128)(2,1)S(1)} %get-tuple-element.34), channel_id=1, source_target_pairs={{0,1},{1,0},{2,3},{3,2},{4,5},{5,4},{6,7},{7,6},{8,9},{9,8},{10,11... | collective-permute-start | bytes 368648 | tf_op jit(solution)/shard_map/ppermute | solution.py:493

commit v3 on v2

v3 whole, which is shorter than its diff:
```python
import functools
import math

import jax
import jax.numpy as jnp
import ml_dtypes
import numpy as np
from jax import lax
from jax.experimental import pallas as pl
from jax.experimental.pallas import tpu as pltpu
from jax.sharding import PartitionSpec as P

PU = 800
PV = 800
PW = 960
HALO_CH = 128
BC = 16
BT = 64
CHANNELS = 2560

two_pi = 2.0 * math.pi
lane = 128
f32 = jnp.float32
bf16 = jnp.bfloat16
whole = pl.BlockSpec(memory_space=pltpu.VMEM)
pinned = pl.BlockSpec(memory_space=pltpu.HBM)


def near(array):
    return pltpu.with_memory_space_constraint(array, pltpu.VMEM)


def distant(array):
    return pltpu.with_memory_space_constraint(array, pltpu.HBM)


def ceil_to(size, step):
    return -(-size // step) * step


class Plane:
    def __init__(self, length, wire, count, keep, kernel_start, row):
        self.length, self.wire, self.count, self.keep = length, wire, count, keep
        self.kernel_start, self.row = kernel_start, row
        self.half = length // 2
        self.rows = ceil_to(self.half + 1, 16)


def make_planes():
    found, row, start = [], 0, 0
    for length, wire, count, keep in (
        (PU, 0, PU, 0),
        (PV, PU, PV, 0),
        (PW + 2 * HALO_CH, PU + PV, PW, HALO_CH),
    ):
        found.append(Plane(length, wire, count, keep, start, row))
        row += found[-1].rows
        start += length
    return found


planes = make_planes()
all_rows = planes[-1].row + planes[-1].rows


def split(values):
    high = values.astype(bf16)
    return high, (values - high.astype(f32)).astype(bf16)


def channel_tables(length, rows, order):
    index = np.arange(rows)
    angles = (index[:, None] * index[None, :] % length) * (two_pi / length)
    inside = (index <= length // 2).astype(np.float64)
    mask = inside[:, None] * inside[None, :]
    found = []
    for values in (np.cos(angles) * mask, np.sin(angles) * mask):
        high = values.astype(np.float32).astype(ml_dtypes.bfloat16)
        low = (values - high.astype(np.float64)).astype(np.float32).astype(ml_dtypes.bfloat16)
        found.append(np.concatenate([(high, low)[i] for i in order], axis=1))
    return np.stack(found)


def tick_angles(ticks):
    return (np.arange(ticks)[:, None] * np.arange(ticks // 2)[None, :] % ticks) * (two_pi / ticks)


def in_blocks(values, blocks, padded):
    parts = np.stack(np.split(values, blocks, axis=-1))
    return np.pad(parts, [(0, 0)] * (parts.ndim - 1) + [(0, padded - parts.shape[-1])])


def forward_tables(ticks, blocks, padded):
    angles = tick_angles(ticks)
    halves = [in_blocks(part, blocks, padded) for part in (np.cos(angles), -np.sin(angles))]
    return np.concatenate(halves, axis=-1).astype(np.float32).astype(ml_dtypes.bfloat16)


def inverse_tables(ticks, blocks, padded):
    angles = tick_angles(ticks)
    weights = np.where(np.arange(ticks // 2) == 0, 1.0, 2.0) / ticks
    halves = [in_blocks(part * weights, blocks, padded) for part in (np.cos(angles), -np.sin(angles))]
    return np.ascontiguousarray(np.swapaxes(np.concatenate(halves, axis=-1), 1, 2)).astype(np.float32)


def dot(left, right):
    return jnp.dot(left, right, preferred_element_type=f32)


def one_hot(rows, first, targets):
    numbers = lax.broadcasted_iota(jnp.int32, (rows, targets.shape[1]), 0) + first
    return jnp.where(numbers == targets, 1.0, 0.0).astype(bf16)


def wires_of(wires, block, share):
    if wires.shape[0] > 1:
        return wires[pl.ds(block, 1), :]
    return wires[:, pl.ds(pl.multiple_of(block * share, lane), share)]


def tick_spectra(blocks, frames_source, table_source, wires_source, neighbours_source, *refs):
    outs, bands, (frames, table, wires, neighbours) = refs[: blocks - 1], refs[blocks - 1 : blocks + 1], refs[blocks + 1 : blocks + 5]
    (sems,) = refs[blocks + 5 :]
    here, detector = lax.axis_index("chan"), lax.axis_index("apa")
    parts = 4
    size = frames.shape[0] // parts
    spans = [pl.ds(i * size, size) for i in range(parts)]
    pairs = [(table_source, table), (wires_source, wires), (neighbours_source, neighbours)]
    pairs += [(frames_source.at[span], frames.at[span]) for span in spans]
    copies = [pltpu.make_async_copy(source, target, sems.at[i]) for i, (source, target) in enumerate(pairs)]
    for copy in copies:
        copy.start()
    copies[0].wait()
    for copy, span in zip(copies[3:], spans):
        copy.wait()
        for s, out in enumerate(outs, 1):
            out[span, :] = dot(frames[span, :], table[lax.rem(here + s, blocks)]).astype(bf16)
    for copy in copies[1:3]:
        copy.wait()
    mine = wires_of(wires, here, frames.shape[0])
    head, tail = PU + PV, CHANNELS - HALO_CH
    to_next = jnp.where(neighbours[:, 1:2] == detector + 1, tail, head)
    to_before = jnp.where(neighbours[:, 0:1] == detector - 1, head, tail)
    for first, out in zip((to_next, to_before), bands):
        rows = dot(one_hot(HALO_CH, first, mine), frames[...]).astype(bf16)
        for s in range(blocks):
            spectra = dot(rows, table[lax.rem(here + s, blocks)])
            out[s * HALO_CH : (s + 1) * HALO_CH, :] = spectra.astype(bf16)


def lane_signs(width):
    return jnp.where(lax.broadcasted_iota(jnp.int32, (1, width), 1) < width // 2, 1.0, -1.0)


def rotated(values):
    width = values.shape[1]
    return pltpu.roll(values, width // 2, 1) * lane_signs(width)


def spread(values):
    width = values.shape[1]
    first = lax.broadcasted_iota(jnp.int32, values.shape, 1) < width // 2
    other = pltpu.roll(values, width // 2, 1)
    return jnp.concatenate([jnp.where(first, values, other), jnp.where(first, other, values)], axis=1)


def fold_of(offset, length, row):
    behind = 2 * offset > length
    return row + jnp.where(behind, length - offset, offset), jnp.where(behind, -1.0, 1.0)


def fold_of_wires(wires):
    first, second = wires < PU, wires < PU + PV
    offset = jnp.where(first, wires, jnp.where(second, wires - PU, wires - (PU + PV) + HALO_CH))
    length = jnp.where(first, PU, jnp.where(second, PV, planes[2].length))
    row = jnp.where(first, planes[0].row, jnp.where(second, planes[1].row, planes[2].row))
    return fold_of(offset, length, row)


def fold_of_halo(begin):
    offset = lax.broadcasted_iota(jnp.int32, (1, HALO_CH), 1) + begin
    return fold_of(offset, planes[2].length, planes[2].row)


def sign_columns(signs, width):
    return jnp.transpose(jnp.broadcast_to(signs, (width, signs.shape[1])))


def fold_operand(spectra, signs):
    turned = rotated(spectra.astype(f32)) * sign_columns(signs, spectra.shape[1])
    return jnp.concatenate([spectra, turned.astype(bf16)], axis=1)


def near_part(sources, wires, frames, table, folded, *refs):
    kept, sems = refs[:-1], refs[-1]
    copies = [pltpu.make_async_copy(source, target, sems.at[i]) for i, (source, target) in enumerate(zip(sources, kept))]
    for copy in copies:
        copy.start()
    here = lax.axis_index("chan")
    width = folded.shape[1] // 2
    targets, signs = fold_of_wires(wires_of(wires, here, frames.shape[0]))
    spectra = dot(frames[...], table[here])
    turned = rotated(spectra) * sign_columns(signs, width)
    operand = jnp.concatenate(split(spectra) + split(turned), axis=1)
    for plane in planes:
        rows = pl.ds(plane.row, plane.rows)
        both = dot(one_hot(plane.rows, plane.row, targets), operand)
        folded[rows, :width] = both[:, :width] + both[:, width : 2 * width]
        folded[rows, width:] = both[:, 2 * width : 3 * width] + both[:, 3 * width :]
    for copy in copies:
        copy.wait()


def kernel_factors(kernel, sums, diffs):
    harmonics, width = kernel.shape[1], sums.shape[1] // 2
    spare = width // 2 - harmonics
    for plane in planes:
        rows = pl.ds(plane.row, plane.rows)
        start = plane.kernel_start // lane * lane
        stop = ceil_to(plane.kernel_start + plane.length, lane)
        offset = plane.kernel_start - start
        parts = []
        for z in range(2):
            parts.append(kernel[z, :, start:stop])
            if spare:
                parts.append(jnp.zeros((spare, stop - start), f32))
        values = jnp.concatenate(parts, axis=0)
        direct = jnp.transpose(values[:, : ceil_to(offset + plane.rows, lane)])[offset : offset + plane.rows]
        row = lax.broadcasted_iota(jnp.int32, (plane.rows, 1), 0)
        source = jnp.where((row > 0) & (row < plane.half), plane.length - row + offset, -1)
        column = lax.broadcasted_iota(jnp.int32, (plane.rows, stop - start), 1)
        matrix = jnp.where(column == source, 1.0, 0.0).astype(bf16)
        both = lax.dot_general(
            matrix, jnp.concatenate(split(values), axis=0), (((1,), (1,)), ((), ())), preferred_element_type=f32
        )
        mirror = (both[:, :width] + both[:, width:]) * (1.0 / plane.length)
        row = lax.broadcasted_iota(jnp.int32, (plane.rows, width), 0)
        direct = jnp.where(row <= plane.half, direct * (1.0 / plane.length), 0.0)
        sums[rows, :] = spread(direct + mirror)
        diffs[rows, :] = spread(direct - mirror)


def multiplied(even, odd, plus, minus):
    width = even.shape[1]
    even_turned, odd_turned = rotated(even), rotated(odd)
    plus_re, plus_im, minus_re, minus_im = plus[:, :width], plus[:, width:], minus[:, :width], minus[:, width:]
    total = (even * plus_re + odd * minus_re) - (even_turned * plus_im + odd_turned * minus_im)
    gap = (even * minus_im + odd * plus_im) + (even_turned * minus_re + odd_turned * plus_re)
    return total, -gap


def far_operand(blocks, share, wires, received):
    here = lax.axis_index("chan")
    targets, signs = [], []
    for s in range(1, blocks):
        target, sign = fold_of_wires(wires_of(wires, lax.rem(here + blocks - s, blocks), share))
        targets.append(target)
        signs.append(sign)
    operand = fold_operand(jnp.concatenate([ref[...] for ref in received], axis=0), jnp.concatenate(signs, axis=1))
    return jnp.concatenate(targets, axis=1), operand


def halo_operand(blocks, neighbours, halo):
    bands, targets, signs = [], [], []
    detector = lax.axis_index("apa")
    lower, upper = neighbours[:, 0:1], neighbours[:, 1:2]
    never = -4 * planes[2].length
    for way in range(2):
        total = halo[way][:HALO_CH, :].astype(f32)
        for ref in halo[2:]:
            total += ref[way * HALO_CH : (way + 1) * HALO_CH, :].astype(f32)
        bands.append(total.astype(bf16))
        other = detector + 2 * way - 1
        begin = jnp.where(upper == other, planes[2].length - HALO_CH, never)
        begin = jnp.where(lower == other, 0, begin)
        target, sign = fold_of_halo(jnp.where(other < 0, never, begin))
        targets.append(target)
        signs.append(sign)
    operand = fold_operand(jnp.concatenate(bands, axis=0), jnp.concatenate(signs, axis=1))
    return jnp.concatenate(targets, axis=1), operand


def halves(plane, cosine, sine, turned):
    straight = plane.count // 2
    width = cosine.shape[1]
    row = lax.broadcasted_iota(jnp.int32, (straight, cosine.shape[0]), 0)
    column = lax.broadcasted_iota(jnp.int32, (straight, cosine.shape[0]), 1)
    matrix = jnp.where(column == plane.half - plane.keep - row, 1.0, 0.0).astype(bf16)
    if turned:
        both = dot(matrix, jnp.concatenate(split(cosine - sine), axis=1))
        return (cosine + sine)[:straight], both[:, :width] + both[:, width:]
    high, low = split(cosine - sine)
    return (cosine + sine)[:straight], dot(matrix, high) + dot(matrix, low)


def last_plane(far, bands, folded, sums, diffs, wide):
    plane = planes[2]
    rows = pl.ds(plane.row, plane.rows)
    both = folded[rows, :] + dot(one_hot(plane.rows, plane.row, far[0]), far[1])
    both += dot(one_hot(plane.rows, plane.row, bands[0]), bands[1])
    width = both.shape[1] // 2

    def transform(table, values):
        joined = jnp.concatenate(split(values), axis=1)
        result = dot(table, jnp.concatenate([joined, joined], axis=0))
        return result[:, :width] + result[:, width:]

    even, odd = transform(wide[0], both[:, :width]), transform(wide[1], both[:, width:])
    total, gap = multiplied(even, odd, sums[rows, :], diffs[rows, :])
    cosine, sine = transform(wide[0, plane.keep :], total), transform(wide[1, plane.keep :], gap)
    return jnp.concatenate(halves(plane, cosine, sine, True), axis=0)


def first_planes(far, folded, sums, diffs, narrow):
    plane = planes[0]
    count = plane.rows
    both = folded[: 2 * count, :] + dot(one_hot(2 * count, 0, far[0]), far[1])
    width = both.shape[1] // 2

    def transform(table, values):
        high, low = split(jnp.concatenate(values, axis=1))
        return dot(table, jnp.concatenate([high, high, low], axis=0))

    even = transform(narrow[0], [both[:count, :width], both[count:, :width]])
    odd = transform(narrow[1], [both[:count, width:], both[count:, width:]])
    totals, gaps = [], []
    for i in range(2):
        rows, lanes = slice(i * count, (i + 1) * count), slice(i * width, (i + 1) * width)
        total, gap = multiplied(even[:, lanes], odd[:, lanes], sums[rows, :], diffs[rows, :])
        totals.append(total)
        gaps.append(gap)
    return halves(plane, transform(narrow[0], totals), transform(narrow[1], gaps), False)


def put_first(result, *operands):
    lower, upper = first_planes(*operands)
    width, straight = result.shape[1], lower.shape[0]
    for i in range(2):
        lanes, start = slice(i * width, (i + 1) * width), planes[i].wire
        result[start : start + straight, :] = lower[:, lanes]
        result[start + straight : start + 2 * straight, :] = upper[:, lanes]


def all_planes(blocks, share, neighbours, *refs):
    received, halo = refs[: blocks - 1], refs[blocks - 1 : 2 * blocks]
    wires, folded, sums, diffs, narrow, wide, own = refs[2 * blocks : 2 * blocks + 7]
    sends, result = refs[2 * blocks + 7 : 3 * blocks + 6], refs[3 * blocks + 6]
    far = far_operand(blocks, share, wires, received)
    bands = halo_operand(blocks, neighbours, halo)
    put_first(result, far, folded, sums, diffs, narrow)
    result[planes[2].wire :, :] = last_plane(far, bands, folded, sums, diffs, wide)
    here = lax.axis_index("chan")
    own[...] = result[pl.ds(pl.multiple_of(here * share, share), share), :]
    for shift, out in enumerate(sends, 1):
        first = pl.multiple_of(lax.rem(here + shift, blocks) * share, share)
        out[...] = result[pl.ds(first, share), :].astype(bf16)


def leading_planes(share, neighbours, far, halo0, halo1, halo2, wires, folded, sums, diffs, narrow, wide, send, rest,
                   targets, operand, result):
    targets[...], operand[...] = far_operand(2, share, wires, [far])
    count = send.shape[0]

    @pl.when(lax.axis_index("chan") == 0)
    def _():
        bands = halo_operand(2, neighbours, (halo0, halo1, halo2))
        values = last_plane((targets[...], operand[...]), bands, folded, sums, diffs, wide)
        send[...] = values.astype(bf16)
        rest[...] = jnp.zeros(rest.shape, f32)

    @pl.when(lax.axis_index("chan") != 0)
    def _():
        put_first(result, (targets[...], operand[...]), folded, sums, diffs, narrow)
        send[...] = result[:count, :].astype(bf16)
        rest[...] = result[count:, :]


def trailing_planes(share, neighbours, halo0, halo1, halo2, targets, operand, rest, folded, sums, diffs, narrow, wide,
                    send, own, result):
    more = send.shape[0]
    operands = (targets[...], operand[...])

    @pl.when(lax.axis_index("chan") == 0)
    def _():
        put_first(result, operands, folded, sums, diffs, narrow)
        own[...] = result[:share, :]
        send[...] = result[share:, :].astype(bf16)

    @pl.when(lax.axis_index("chan") != 0)
    def _():
        bands = halo_operand(2, neighbours, (halo0, halo1, halo2))
        own[more:, :] = last_plane(operands, bands, folded, sums, diffs, wide)
        own[:more, :] = rest[more:, :]
        send[...] = rest[:more, :].astype(bf16)


def spread_mask(mask, share, ticks):
    marked = jnp.where(mask == 1, 1.0, 0.0).astype(bf16)
    row = lax.broadcasted_iota(jnp.int32, (share, mask.shape[1]), 0)
    column = lax.broadcasted_iota(jnp.int32, (share, mask.shape[1]), 1)
    taken = jnp.where(row // BC == column, 1.0, 0.0).astype(bf16)
    rows = lax.dot_general(taken, marked, (((1,), (1,)), ((), ())), preferred_element_type=f32).astype(bf16)
    row = lax.broadcasted_iota(jnp.int32, (mask.shape[0], ticks), 0)
    column = lax.broadcasted_iota(jnp.int32, (mask.shape[0], ticks), 1)
    return dot(rows, jnp.where(column // BT == row, 1.0, 0.0).astype(bf16))


def chosen_signal(both, inside):
    ticks = inside.shape[1]
    return jnp.where(inside > 0.5, both[:, :ticks], both[:, ticks:])


def scaled_basis(block, blocks, basis, filters, harmonics):
    padded = basis.shape[1] // 2
    ticks = basis.shape[2]
    gains = []
    for gain in filters:
        columns = gain[...] if blocks == 1 else None
        for b in range(blocks):
            piece = gain[:, b * harmonics : (b + 1) * harmonics]
            columns = piece if columns is None else jnp.where(block == b, piece, columns)
        if padded > harmonics:
            columns = jnp.concatenate([columns, jnp.zeros((1, padded - harmonics), f32)], axis=1)
        columns = jnp.concatenate([columns, columns], axis=1)
        tall = jnp.transpose(jnp.broadcast_to(columns, (lane, 2 * padded)))
        gains.append(jnp.concatenate([tall] * (ticks // lane), axis=1))
    values = basis[block]
    return split(jnp.concatenate([values * part for part in gains], axis=1))


def own_signal(blocks, own, basis_source, wide_filter, tight_filter, mask, signal, bases, inside, basis, sem):
    basis_copy = pltpu.make_async_copy(basis_source, basis, sem)
    basis_copy.start()
    inside[...] = spread_mask(mask[...], own.shape[0], signal.shape[1])
    basis_copy.wait()
    here = lax.axis_index("chan")
    ticks = signal.shape[1]
    harmonics = wide_filter.shape[1] // blocks
    filters = (wide_filter, tight_filter)
    high, low = scaled_basis(here, blocks, basis, filters, harmonics)
    joined = jnp.concatenate(split(own[...]), axis=1)
    both = dot(joined, jnp.concatenate([high, high], axis=0))
    both += dot(joined, jnp.concatenate([low, low], axis=0))
    signal[...] = chosen_signal(both, inside[...])
    for shift in range(1, blocks):
        parts = scaled_basis(lax.rem(here + blocks - shift, blocks), blocks, basis, filters, harmonics)
        bases[shift - 1] = jnp.concatenate(parts, axis=0)


def whole_signal(blocks, signal, bases, inside, *refs):
    out = refs[-1]
    both = None
    for shift in range(1, blocks):
        values = refs[shift - 1][...]
        term = dot(jnp.concatenate([values, values], axis=1), bases[shift - 1])
        both = term if both is None else both + term
    if both is None:
        out[...] = signal[...]
    else:
        out[...] = signal[...] + chosen_signal(both, inside[...])


def part_signal(spans, signal, bases, inside, values, *refs):
    out, room, sems = refs[-3:]
    step = room.shape[0] // sems.shape[0]
    for device, (first, count) in enumerate(spans):

        @pl.when(lax.axis_index("chan") == device)
        def _(first=first, count=count):
            copies = []
            for i in range(count // step):
                some = values[i * step : (i + 1) * step, :]
                both = dot(jnp.concatenate([some, some], axis=1), bases[0])
                rows, slot = pl.ds(first + i * step, step), pl.ds(i * step, step)
                room[slot, :] = signal[rows, :] + chosen_signal(both, inside[rows, :])
                copies.append(pltpu.make_async_copy(room.at[slot], out.at[rows], sems.at[i]))
                copies[-1].start()
            for copy in copies:
                copy.wait()


def call(kernel, outs, ins, name, scratch=(), final=False, aliases=None):
    kind = jax.ShapeDtypeStruct if final else pltpu.VMEM
    return pl.pallas_call(
        kernel,
        out_shape=[kind(shape, dtype) for shape, dtype in outs],
        in_specs=ins,
        out_specs=[pinned if final else whole] * len(outs),
        scratch_shapes=scratch,
        compiler_params=pltpu.CompilerParams(vmem_limit_bytes=28 * 1024 * 1024),
        cost_estimate=pl.CostEstimate(flops=0, bytes_accessed=0, transcendentals=0),
        input_output_aliases=aliases or {},
        name=name,
    )


def body(frames, link_to_wire, neighbours, kernel, wide_filter, tight_filter, roi_mask):
    frames, roi_mask = frames[0], roi_mask[0]
    share, ticks = frames.shape
    blocks = lax.axis_size("chan")
    detectors = lax.axis_size("apa")
    padded = max(kernel.shape[1], lane // 2)
    width = 2 * padded
    wires = link_to_wire if share % lane == 0 else link_to_wire.reshape(blocks, share)
    table = jnp.asarray(forward_tables(ticks, blocks, padded))

    def around(parts):
        return [
            near(lax.ppermute(part, "chan", [(i, (i + s) % blocks) for i in range(blocks)]))
            for s, part in enumerate(parts, 1)
        ]

    first = call(
        functools.partial(tick_spectra, blocks),
        [((share, width), bf16)] * (blocks - 1) + [((blocks * HALO_CH, width), bf16)] * 2
        + [((share, ticks), bf16), ((blocks, ticks, width), bf16), (wires.shape, jnp.int32), (neighbours.shape, jnp.int32)],
        [pinned] * 4, "tick_spectra", [pltpu.SemaphoreType.DMA((7,))],
    )(*map(distant, (frames, table, wires, neighbours)))
    far, bands = first[: blocks - 1], first[blocks - 1 : blocks + 1]
    frames, table, wires, neighbours = map(near, first[blocks + 1 :])
    received = around(far)
    tables = [channel_tables(planes[i].length, planes[i].rows, order) for i, order in ((0, (0, 1, 0)), (2, (0, 1)))]
    sources = [kernel, *map(jnp.asarray, tables)]
    folded, *ready = call(
        lambda *refs: near_part(refs[:3], *refs[3:]),
        [((all_rows, 2 * width), f32)] + [(part.shape, part.dtype) for part in sources],
        [pinned] * 3 + [whole] * 3, "near_part", [pltpu.SemaphoreType.DMA((3,))],
    )(*map(distant, sources), wires, frames, table)
    halo = []
    for step, band in zip((1, -1), bands):
        pairs = [(a, a + step) for a in range(detectors) if 0 <= a + step < detectors]
        halo.append(lax.ppermute(band, "apa", pairs))
    *halo, folded = lax.optimization_barrier((*halo, folded))
    shares = [
        jnp.concatenate([band[s * HALO_CH : (s + 1) * HALO_CH] for band in halo]) for s in range(1, blocks)
    ]
    halo = [near(band) for band in halo] + around(shares)
    kernel, narrow, wide = map(near, ready)
    folded = near(folded)
    sums, diffs = map(near, call(
        kernel_factors, [((all_rows, 2 * width), f32)] * 2, [whole], "kernel_factors",
    )(kernel))
    basis = jnp.asarray(inverse_tables(ticks, blocks, padded))
    filters = (wide_filter[None], tight_filter[None])
    mask = jnp.transpose(roi_mask)
    signal_shapes = [
        ((share, ticks), f32), ((max(blocks - 1, 1), 2 * width, 2 * ticks), bf16), ((share, ticks), f32)
    ]

    def own_part(own):
        return map(near, call(
            functools.partial(own_signal, blocks), signal_shapes,
            [whole, pinned] + [whole] * 3, "own_signal",
            [pltpu.VMEM(basis.shape, f32), pltpu.SemaphoreType.DMA],
        )(near(own), distant(basis), *filters, mask))

    if blocks != 2:
        own, *sends = call(
            functools.partial(all_planes, blocks, share),
            [((share, width), f32)] + [((share, width), bf16)] * (blocks - 1),
            [whole] * (2 * blocks + 7), "all_planes",
            [pltpu.VMEM((CHANNELS, width), f32)],
        )(neighbours, *received, *halo, wires, folded, sums, diffs, narrow, wide)
        returned = around(sends)
        signal, bases, inside = own_part(own)
        out = pl.pallas_call(
            functools.partial(whole_signal, blocks),
            out_shape=jax.ShapeDtypeStruct((share, ticks), f32),
            in_specs=[whole] * (blocks + 2),
            out_specs=whole,
            name="whole_signal",
        )(signal, bases, inside, *returned)
        return out[None]

    more = share - PW
    sent, rest, *operands = call(
        functools.partial(leading_planes, share),
        [((PW, width), bf16), ((PU + PV - PW, width), f32), ((1, share), jnp.int32), ((share, 2 * width), bf16)],
        [whole] * 11, "leading_planes", [pltpu.VMEM((PU + PV, width), f32)],
    )(neighbours, *received, *halo, wires, folded, sums, diffs, narrow, wide)
    (early,) = around([sent])
    sent, own = call(
        functools.partial(trailing_planes, share), [((more, width), bf16), ((share, width), f32)],
        [whole] * 12, "trailing_planes", [pltpu.VMEM((PU + PV, width), f32)],
    )(neighbours, *halo, *map(near, operands), near(rest), folded, sums, diffs, narrow, wide)
    (late,) = around([sent])
    signal, bases, inside = own_part(own)

    def finish(values, spans, *before):
        step = math.gcd(PW, more) // 2
        rows = max(count for _, count in spans)
        (out,) = call(
            functools.partial(part_signal, spans), [((share, ticks), f32)],
            [whole] * 4 + [pinned] * len(before), "part_signal",
            [pltpu.VMEM((rows, ticks), f32), pltpu.SemaphoreType.DMA((rows // step,))],
            final=True, aliases={4: 0} if before else None,
        )(signal, bases, inside, values, *before)
        return out

    out = finish(early, ((0, PW), (more, PW)))
    return finish(late, ((PW, more), (0, more)), out)[None]


def solution(mesh):
    placed = (
        P("apa", "chan", None),
        P("apa", None),
        P("apa", None),
        P(None, "chan", None),
        P(),
        P(),
        P("apa", "chan", None),
    )
    return jax.shard_map(
        body, mesh=mesh, in_specs=placed, out_specs=P("apa", "chan", None), check_vma=False
    )
```

time: 41.4 us -> 34.7 us (0.84)
  Pallas kernels: 25.8 us -> 19.9 us
  starting transfers between devices: 8.68 us -> 11.6 us
  waiting for transfers between devices: 4.55 us -> 2.65 us
  local copies, waits for them, and re-layouts: 1.39 us -> 0.03 us
    pallas_call x8, Pallas kernels: 25.8 us -> 19.9 us  [the longest x1 4.74 us: body(): call(functools.partial(leading_planes, share), [((PW, width), bf16), ((PU...]
    ppermute x2, waiting for transfers between devices: 4.54 us -> 0.01 us  [body(): halo.append(lax.ppermute(band, 'apa', pairs))]
    ppermute x4, waiting for transfers between devices: 0.01 us -> 2.64 us  [around(): lax.ppermute(part, 'chan', [(i, (i + s) % blocks) for i in range(blocks)])]
    ppermute x2, starting transfers between devices: 4.37 us -> 6.45 us  [body(): halo.append(lax.ppermute(band, 'apa', pairs))]
    unnamed x14 -> x6, local copies, waits for them, and re-layouts: 1.39 us -> 0.02 us
    ppermute x4, starting transfers between devices: 4.31 us -> 5.11 us  [around(): lax.ppermute(part, 'chan', [(i, (i + s) % blocks) for i in range(blocks)])]
  transfers between devices with their start and end apart: 6 -> 6, of which waited for: 1 -> 1; matrix products, arithmetic and copies ran while one was open for 0% -> 0% of each run, Pallas kernels for 40% -> 33%
where the time goes in v3:
time: 34.7 us; the launch traced here: 34.5 us
  Pallas kernels  19.9 us (57%)
  starting transfers between devices  11.6 us (33%)
  waiting for transfers between devices  2.65 us (8%)
    ppermute x2, starting transfers between devices, body(): halo.append(lax.ppermute(band, 'apa', pairs))  6.45 us
    ppermute x4, starting transfers between devices, around(): lax.ppermute(part, 'chan', [(i, (i + s) % blocks) for i in range(blocks)])  5.11 us
    pallas_call x1, Pallas kernels, body(): call(functools.partial(leading_planes, share), [((PW, width), bf16), ((PU...  4.74 us
    pallas_call x1, Pallas kernels, body(): call(functools.partial(trailing_planes, share), [((more, width), bf16), (...  3.78 us
    pallas_call x1, Pallas kernels, body(): call(lambda *refs: near_part(refs[:3], *refs[3:]), [((all_rows, 2 * width...  3.16 us
    pallas_call x1, Pallas kernels, body(): call(functools.partial(tick_spectra, blocks), [((share, width), bf16)] *...  2.85 us
    ppermute x4, waiting for transfers between devices, around(): lax.ppermute(part, 'chan', [(i, (i + s) % blocks) for i in range(blocks)])  2.64 us
    pallas_call x2, Pallas kernels, finish(): call(functools.partial(part_signal, spans), [((share, ticks), f32)], [who...  2.18 us
  transfers between devices with their start and end apart: 6, of which 1 were waited for; matrix products, arithmetic and copies ran while one was open for 0% of the time, Pallas kernels for 33%

profile of v3, /device:TPU:24, one launch (start us, length us, event | category | flops | bytes accessed | tf_op | source)
XLA Modules:
  0.0 34.5 jit_solution(10156344287445611092)
XLA Ops:
  0.0 2.8 %tick_spectra.1 = (bf16[1280,128]{1,0:T(8,128)(2,1)S(1)}, bf16[256,128]{1,0:T(8,128)(2,1)S(1)}, bf16[256,128]{1,0:T(8,128)(2,1)S(1)}, bf16[1280,256]{1,0:T(8,128...) custom-call(bf16[1280,256]{1,0:T(8,128)(2,1)} %bitcast.10, ...), custom_call_target="tpu_custom_call" | custom-call | tf_op jit(solution)/shard_map/tick_spectra/pallas_call | solution.py:513
  2.9 1.6 %collective-permute-start.3 = (bf16[1280,128]{1,0:T(8,128)(2,1)S(1)}, bf16[1280,128]{1,0:T(8,128)(2,1)S(1)}, u32[]{:S(2)}, u32[]{:S(2)}) collective-permute-start(bf16[1280,128]{1,0:T(8,128)(2,1)S(1)} %get-tuple-element.39), channel_id=1, source_target_pairs={{0,1},{1,0},{2,3},{3,2},{4,5},{5,4},{6,7},{7,6},{8,9},{9,8},{10,11... | collective-permute-start | bytes 983048 | tf_op jit(solution)/shard_map/ppermute | solution.py:509
  4.4 1.9 %collective-permute-start = (bf16[256,128]{1,0:T(8,128)(2,1)S(1)}, bf16[256,128]{1,0:T(8,128)(2,1)S(1)}, u32[]{:S(2)}, u32[]{:S(2)}) collective-permute-start(bf16[256,128]{1,0:T(8,128)(2,1)S(1)} %get-tuple-element.31), channel_id=1, source_target_pairs={{0,2},{2,4},{4,6},{6,8},{8,10},{10,12},{12,14},{14,16},{16,18},{18... | collective-permute-start | bytes 196616 | tf_op jit(solution)/shard_map/ppermute | solution.py:532
  6.4 4.5 %collective-permute-start.1 = (bf16[256,128]{1,0:T(8,128)(2,1)S(1)}, bf16[256,128]{1,0:T(8,128)(2,1)S(1)}, u32[]{:S(2)}, u32[]{:S(2)}) collective-permute-start(bf16[256,128]{1,0:T(8,128)(2,1)S(1)} %get-tuple-element.32), channel_id=1, source_target_pairs={{2,0},{4,2},{6,4},{8,6},{10,8},{12,10},{14,12},{16,14},{18,16},{20... | collective-permute-start | bytes 196616 | tf_op jit(solution)/shard_map/ppermute | solution.py:532
  10.9 3.2 %near_part.1 = (f32[1456,256]{1,0:T(8,128)S(1)}, f32[2,64,2816]{2,1,0:T(8,128)S(1)}, bf16[2,416,1248]{2,1,0:T(8,128)(2,1)S(1)}, bf16[2,624,1248]{2,1,0:T(8,128)(2,1)S(1)}) custom-call(f32[2,64,2816]{2,1,0:T(8,128)} %refs_0_.1, bf16[2,416,1248]{2,1,0:T(8,128)(2,1)} %constant.9.clone.refs_1_, bf16[2,624,1248]{2,1,0:T(8,128)(2,1)} %constant.10.clone.refs_2_, ...), custom_call_target="tpu_custom_call" | custom-call | tf_op jit(solution)/shard_map/near_part/pallas_call | solution.py:524
  14.1 0.0 collective-permute-done.halo0
  14.1 0.0 collective-permute-done.1.halo1
  14.1 0.6 %collective-permute-start.2 = (bf16[256,128]{1,0:T(8,128)(2,1)S(1)}, bf16[256,128]{1,0:T(8,128)(2,1)S(1)}, u32[]{:S(2)}, u32[]{:S(2)}) collective-permute-start(bf16[256,128]{1,0:T(8,128)(2,1)S(1)} %pad_maximum_fusion), channel_id=1, source_target_pairs={{0,1},{1,0},{2,3},{3,2},{4,5},{5,4},{6,7},{7,6},{8,9},{9,8},{10,11... | collective-permute-start | bytes 196616 | tf_op jit(solution)/shard_map/ppermute | solution.py:509
  14.7 1.1 %kernel_factors.1 = (f32[1456,256]{1,0:T(8,128)S(1)}, f32[1456,256]{1,0:T(8,128)S(1)}) custom-call(f32[2,64,2816]{2,1,0:T(8,128)S(1)} %get-tuple-element.41.kernel), custom_call_target="tpu_custom_call" | custom-call | tf_op jit(solution)/shard_map/kernel_factors/pallas_call | solution.py:540
  15.8 2.6 %collective-permute-done.2.halo2 = bf16[256,128]{1,0:T(8,128)(2,1)S(1)} collective-permute-done((bf16[256,128]{1,0:T(8,128)(2,1)S(1)}, bf16[256,128]{1,0:T(8,128)(2,1)S(1)}, u32[]{:S(2)}, u32[]{:S(2)}) %collective-permute-start.2) | collective-permute-done | bytes 65568 | tf_op jit(solution)/shard_map/ppermute | solution.py:509
  18.5 0.0 collective-permute-done.3.far
  18.5 4.7 %leading_planes.1 = (bf16[960,128]{1,0:T(8,128)(2,1)S(1)}, f32[640,128]{1,0:T(8,128)S(1)}, s32[1,1280]{1,0:T(1,128)S(1)}, bf16[1280,256]{1,0:T(8,128)(2,1)S(1)}) custom-call(s32[1,2]{1,0:T(1,128)S(1)} %get-tuple-element.30.neighbours, bf16[1280,128]{1,0:T(8,128)(2,1)S(1)} %collective-permute-done.3.far, bf16[256,128]{1,0:T(8,128)(2,1)S(1)} %collective-permute-done.halo0, ...), custom_call_target="tpu_custom_call" | custom-call | tf_op jit(solution)/shard_map/leading_planes/pallas_call | solution.py:576
  23.2 0.1 collective-permute-start.5
  23.3 0.0 copy-start
  23.3 0.0 copy-start.1
  23.3 0.0 copy-start.2
  23.3 3.8 %trailing_planes.1 = (bf16[320,128]{1,0:T(8,128)(2,1)S(1)}, f32[1280,128]{1,0:T(8,128)S(1)}) custom-call(s32[1,2]{1,0:T(1,128)S(1)} %get-tuple-element.30.neighbours, bf16[256,128]{1,0:T(8,128)(2,1)S(1)} %collective-permute-done.halo0, bf16[256,128]{1,0:T(8,128)(2,1)S(1)} %collective-permute-done.1.halo1, bf16[256,128]{1,0:T(8,128)(2,1)S(1)} %collective-permute-done.2.halo2, ...), custom_call_target="tpu_custom_call" | custom-call | tf_op jit(solution)/shard_map/trailing_planes/pallas_call | solution.py:582
  27.1 2.9 %collective-permute-start.4 = (bf16[320,128]{1,0:T(8,128)(2,1)S(1)}, bf16[320,128]{1,0:T(8,128)(2,1)S(1)}, u32[]{:S(2)}, u32[]{:S(2)}) collective-permute-start(bf16[320,128]{1,0:T(8,128)(2,1)S(1)} %get-tuple-element.53), channel_id=1, source_target_pairs={{0,1},{1,0},{2,3},{3,2},{4,5},{5,4},{6,7},{7,6},{8,9},{9,8},{10,11... | collective-permute-start | bytes 245768 | tf_op jit(solution)/shard_map/ppermute | solution.py:509
  30.0 0.0 copy-done
  30.0 2.1 %own_signal.1 = (f32[1280,256]{1,0:T(8,128)S(1)}, bf16[1,256,512]{2,1,0:T(8,128)(2,1)S(1)}, f32[1280,256]{1,0:T(8,128)S(1)}) custom-call(f32[1280,128]{1,0:T(8,128)S(1)} %get-tuple-element.49.own, f32[2,128,256]{2,1,0:T(8,128)} %constant.11.clone.basis_source, f32[1,128]{1,0:T(1,128)S(1)} %bitcast.8, f32[1,128]{1,0:T(1,128)S(1)} %bitcast.9, s32[4,80]{1,0:T(4,128)S(1)} %bitcast.7), custom_call_target="tpu_custom_call" | custom-call | tf_op jit(solution)/shard_map/own_signal/pallas_call | solution.py:551
  32.1 0.0 collective-permute-done.5.values
  32.1 1.2 %part_signal.2.refs_0_ = f32[1280,256]{1,0:T(8,128)} custom-call(f32[1280,256]{1,0:T(8,128)S(1)} %get-tuple-element.50.signal, bf16[1,256,512]{2,1,0:T(8,128)(2,1)S(1)} %get-tuple-element.51.bases, f32[1280,256]{1,0:T(8,128)S(1)} %get-tuple-element.52.inside, bf16[960,128]{1,0:T(8,128)(2,1)S(1)} %collective-permute-done.5.values), custom_call_target="tpu_custom_call" | custom-call | tf_op jit(solution)/shard_map/part_signal/pallas_call | solution.py:592
  33.3 0.0 collective-permute-done.4.values
  33.3 1.0 %part_signal.3 = f32[1280,256]{1,0:T(8,128)} custom-call(f32[1280,256]{1,0:T(8,128)S(1)} %get-tuple-element.50.signal, bf16[1,256,512]{2,1,0:T(8,128)(2,1)S(1)} %get-tuple-element.51.bases, f32[1280,256]{1,0:T(8,128)S(1)} %get-tuple-element.52.inside, bf16[320,128]{1,0:T(8,128)(2,1)S(1)} %collective-permute-done.4.values, ...), custom_call_target="tpu_custom_call", output_to_operand_aliasing={{}: (4, {})} | custom-call | tf_op jit(solution)/shard_map/part_signal/pallas_call | solution.py:592
  (5 shorter events, 0.0 us)
Async XLA Ops:
  2.9 15.6 %collective-permute-start.3 = (bf16[1280,128]{1,0:T(8,128)(2,1)S(1)}, bf16[1280,128]{1,0:T(8,128)(2,1)S(1)}, u32[]{:S(2)}, u32[]{:S(2)}) collective-permute-start(bf16[1280,128]{1,0:T(8,128)(2,1)S(1)} %get-tuple-element.39), channel_id=1, source_target_pairs={{0,1},{1,0},{2,3},{3,2},{4,5},{5,4},{6,7},{7,6},{8,9},{9,8},{10,11... | collective-permute-start | bytes 983048 | tf_op jit(solution)/shard_map/ppermute | solution.py:509
  4.4 9.6 %collective-permute-start = (bf16[256,128]{1,0:T(8,128)(2,1)S(1)}, bf16[256,128]{1,0:T(8,128)(2,1)S(1)}, u32[]{:S(2)}, u32[]{:S(2)}) collective-permute-start(bf16[256,128]{1,0:T(8,128)(2,1)S(1)} %get-tuple-element.31), channel_id=1, source_target_pairs={{0,2},{2,4},{4,6},{6,8},{8,10},{10,12},{12,14},{14,16},{16,18},{18... | collective-permute-start | bytes 196616 | tf_op jit(solution)/shard_map/ppermute | solution.py:532
  6.4 7.7 %collective-permute-start.1 = (bf16[256,128]{1,0:T(8,128)(2,1)S(1)}, bf16[256,128]{1,0:T(8,128)(2,1)S(1)}, u32[]{:S(2)}, u32[]{:S(2)}) collective-permute-start(bf16[256,128]{1,0:T(8,128)(2,1)S(1)} %get-tuple-element.32), channel_id=1, source_target_pairs={{2,0},{4,2},{6,4},{8,6},{10,8},{12,10},{14,12},{16,14},{18,16},{20... | collective-permute-start | bytes 196616 | tf_op jit(solution)/shard_map/ppermute | solution.py:532
  14.1 4.3 %collective-permute-start.2 = (bf16[256,128]{1,0:T(8,128)(2,1)S(1)}, bf16[256,128]{1,0:T(8,128)(2,1)S(1)}, u32[]{:S(2)}, u32[]{:S(2)}) collective-permute-start(bf16[256,128]{1,0:T(8,128)(2,1)S(1)} %pad_maximum_fusion), channel_id=1, source_target_pairs={{0,1},{1,0},{2,3},{3,2},{4,5},{5,4},{6,7},{7,6},{8,9},{9,8},{10,11... | collective-permute-start | bytes 196616 | tf_op jit(solution)/shard_map/ppermute | solution.py:509
  23.2 8.9 %collective-permute-start.5 = (bf16[960,128]{1,0:T(8,128)(2,1)S(1)}, bf16[960,128]{1,0:T(8,128)(2,1)S(1)}, u32[]{:S(2)}, u32[]{:S(2)}) collective-permute-start(bf16[960,128]{1,0:T(8,128)(2,1)S(1)} %get-tuple-element.54), channel_id=1, source_target_pairs={{0,1},{1,0},{2,3},{3,2},{4,5},{5,4},{6,7},{7,6},{8,9},{9,8},{10,11... | collective-permute-start | bytes 737288 | tf_op jit(solution)/shard_map/ppermute | solution.py:509
  23.3 6.7 %copy-start = (s32[1,80,4]{1,2,0:T(4,128)S(1)}, s32[1,80,4]{1,2,0:T(4,128)}, u32[]{:S(2)}) copy-start(s32[1,80,4]{1,2,0:T(4,128)} %param.17) | copy-start | bytes 3844
  23.3 6.7 %copy-start.1 = (f32[128]{0:T(128)S(1)}, f32[128]{0:T(128)}, u32[]{:S(2)}) copy-start(f32[128]{0:T(128)} %param.15) | copy-start | bytes 1540
  23.3 6.7 %copy-start.2 = (f32[128]{0:T(128)S(1)}, f32[128]{0:T(128)}, u32[]{:S(2)}) copy-start(f32[128]{0:T(128)} %param.16) | copy-start | bytes 1540
  27.1 6.2 %collective-permute-start.4 = (bf16[320,128]{1,0:T(8,128)(2,1)S(1)}, bf16[320,128]{1,0:T(8,128)(2,1)S(1)}, u32[]{:S(2)}, u32[]{:S(2)}) collective-permute-start(bf16[320,128]{1,0:T(8,128)(2,1)S(1)} %get-tuple-element.53), channel_id=1, source_target_pairs={{0,1},{1,0},{2,3},{3,2},{4,5},{5,4},{6,7},{7,6},{8,9},{9,8},{10,11... | collective-permute-start | bytes 245768 | tf_op jit(solution)/shard_map/ppermute | solution.py:509

commit v4 on v3

--- a/solution.py
+++ b/solution.py
@@ -68,7 +68,7 @@
     return high, (values - high.astype(f32)).astype(bf16)
 
 
-def channel_tables(length, rows, order):
+def channel_tables(length, rows):
     index = np.arange(rows)
     angles = (index[:, None] * index[None, :] % length) * (two_pi / length)
     inside = (index <= length // 2).astype(np.float64)
@@ -77,7 +77,7 @@
     for values in (np.cos(angles) * mask, np.sin(angles) * mask):
         high = values.astype(np.float32).astype(ml_dtypes.bfloat16)
         low = (values - high.astype(np.float64)).astype(np.float32).astype(ml_dtypes.bfloat16)
-        found.append(np.concatenate([(high, low)[i] for i in order], axis=1))
+        found.append(np.concatenate([high, low], axis=1))
     return np.stack(found)
 
 
@@ -108,8 +108,8 @@
 
 
 def one_hot(rows, first, targets):
-    numbers = lax.broadcasted_iota(jnp.int32, (rows, targets.shape[1]), 0) + first
-    return jnp.where(numbers == targets, 1.0, 0.0).astype(bf16)
+    numbers = lax.broadcasted_iota(jnp.int16, (rows, targets.shape[1]), 0)
+    return jnp.where(numbers == (targets - first).astype(jnp.int16), bf16(1), bf16(0))
 
 
 def wires_of(wires, block, share):
@@ -119,29 +119,35 @@
 
 
 def tick_spectra(blocks, frames_source, table_source, wires_source, neighbours_source, *refs):
-    outs, bands, (frames, table, wires, neighbours) = refs[: blocks - 1], refs[blocks - 1 : blocks + 1], refs[blocks + 1 : blocks + 5]
-    (sems,) = refs[blocks + 5 :]
-    here, detector = lax.axis_index("chan"), lax.axis_index("apa")
+    outs, (frames, table, wires, neighbours, sems) = refs[: blocks - 1], refs[blocks - 1 :]
     parts = 4
     size = frames.shape[0] // parts
     spans = [pl.ds(i * size, size) for i in range(parts)]
-    pairs = [(table_source, table), (wires_source, wires), (neighbours_source, neighbours)]
-    pairs += [(frames_source.at[span], frames.at[span]) for span in spans]
+    pairs = [(table_source, table)] + [(frames_source.at[span], frames.at[span]) for span in spans]
+    pairs += [(wires_source, wires), (neighbours_source, neighbours)]
     copies = [pltpu.make_async_copy(source, target, sems.at[i]) for i, (source, target) in enumerate(pairs)]
     for copy in copies:
         copy.start()
     copies[0].wait()
-    for copy, span in zip(copies[3:], spans):
+    here = lax.axis_index("chan")
+    for copy, span in zip(copies[1:], spans):
         copy.wait()
         for s, out in enumerate(outs, 1):
             out[span, :] = dot(frames[span, :], table[lax.rem(here + s, blocks)]).astype(bf16)
-    for copy in copies[1:3]:
+    for copy in copies[1 + parts :]:
         copy.wait()
+
+
+def partners(detector):
+    odd = detector % 2
+    return detector + 1 - 2 * odd, detector - 1 + 2 * odd
+
+
+def edge_bands(blocks, neighbours, frames, table, wires, *bands):
+    here = lax.axis_index("chan")
     mine = wires_of(wires, here, frames.shape[0])
-    head, tail = PU + PV, CHANNELS - HALO_CH
-    to_next = jnp.where(neighbours[:, 1:2] == detector + 1, tail, head)
-    to_before = jnp.where(neighbours[:, 0:1] == detector - 1, head, tail)
-    for first, out in zip((to_next, to_before), bands):
+    for other, out in zip(partners(lax.axis_index("apa")), bands):
+        first = jnp.where(neighbours[:, 1:2] == other, CHANNELS - HALO_CH, PU + PV)
         rows = dot(one_hot(HALO_CH, first, mine), frames[...]).astype(bf16)
         for s in range(blocks):
             spectra = dot(rows, table[lax.rem(here + s, blocks)])
@@ -183,11 +189,26 @@
 
 
 def sign_columns(signs, width):
-    return jnp.transpose(jnp.broadcast_to(signs, (width, signs.shape[1])))
+    return jnp.transpose(jnp.broadcast_to(signs, (width, signs.shape[1]))) * lane_signs(width)
+
+
+def backwards(count, last, limit, product):
+    parts = []
+    for start in range(0, count, lane):
+        size = min(lane, count - start)
+        high, low = min(last - start, limit - 1), max(last - start - size + 1, 0)
+        first = low // lane * lane
+        stop = min(ceil_to(high + 1, lane), limit)
+        row = lax.broadcasted_iota(jnp.int32, (size, stop - first), 0)
+        column = lax.broadcasted_iota(jnp.int32, (size, stop - first), 1)
+        matrix = jnp.where(column == last - start - first - row, 1.0, 0.0).astype(bf16)
+        parts.append(product(matrix, first, stop))
+    return jnp.concatenate(parts, axis=0)
 
 
 def fold_operand(spectra, signs):
-    turned = rotated(spectra.astype(f32)) * sign_columns(signs, spectra.shape[1])
+    width = spectra.shape[1]
+    turned = pltpu.roll(spectra.astype(f32), width // 2, 1) * signs
     return jnp.concatenate([spectra, turned.astype(bf16)], axis=1)
 
 
@@ -200,7 +221,7 @@
     width = folded.shape[1] // 2
     targets, signs = fold_of_wires(wires_of(wires, here, frames.shape[0]))
     spectra = dot(frames[...], table[here])
-    turned = rotated(spectra) * sign_columns(signs, width)
+    turned = pltpu.roll(spectra, width // 2, 1) * sign_columns(signs, width)
     operand = jnp.concatenate(split(spectra) + split(turned), axis=1)
     for plane in planes:
         rows = pl.ds(plane.row, plane.rows)
@@ -211,7 +232,7 @@
         copy.wait()
 
 
-def kernel_factors(kernel, sums, diffs):
+def factors(blocks, share, kernel, wires, sums, diffs, chosen, far_signs):
     harmonics, width = kernel.shape[1], sums.shape[1] // 2
     spare = width // 2 - harmonics
     for plane in planes:
@@ -226,18 +247,26 @@
                 parts.append(jnp.zeros((spare, stop - start), f32))
         values = jnp.concatenate(parts, axis=0)
         direct = jnp.transpose(values[:, : ceil_to(offset + plane.rows, lane)])[offset : offset + plane.rows]
-        row = lax.broadcasted_iota(jnp.int32, (plane.rows, 1), 0)
-        source = jnp.where((row > 0) & (row < plane.half), plane.length - row + offset, -1)
-        column = lax.broadcasted_iota(jnp.int32, (plane.rows, stop - start), 1)
-        matrix = jnp.where(column == source, 1.0, 0.0).astype(bf16)
-        both = lax.dot_general(
-            matrix, jnp.concatenate(split(values), axis=0), (((1,), (1,)), ((), ())), preferred_element_type=f32
-        )
+        pair = jnp.concatenate(split(values), axis=0)
+
+        def product(matrix, first, stop):
+            return lax.dot_general(
+                matrix, pair[:, first:stop], (((1,), (1,)), ((), ())), preferred_element_type=f32
+            )
+
+        both = backwards(plane.rows, plane.length + offset, stop - start, product)
         mirror = (both[:, :width] + both[:, width:]) * (1.0 / plane.length)
         row = lax.broadcasted_iota(jnp.int32, (plane.rows, width), 0)
         direct = jnp.where(row <= plane.half, direct * (1.0 / plane.length), 0.0)
+        mirror = jnp.where((row > 0) & (row < plane.half), mirror, 0.0)
         sums[rows, :] = spread(direct + mirror)
         diffs[rows, :] = spread(direct - mirror)
+    here = lax.axis_index("chan")
+    for s in range(1, blocks):
+        targets, signs = fold_of_wires(wires_of(wires, lax.rem(here + blocks - s, blocks), share))
+        span = pl.ds((s - 1) * share, share)
+        chosen[:, span] = one_hot(all_rows, 0, targets)
+        far_signs[span, :] = sign_columns(signs, width)
 
 
 def multiplied(even, odd, plus, minus):
@@ -249,106 +278,67 @@
     return total, -gap
 
 
-def far_operand(blocks, share, wires, received):
-    here = lax.axis_index("chan")
-    targets, signs = [], []
-    for s in range(1, blocks):
-        target, sign = fold_of_wires(wires_of(wires, lax.rem(here + blocks - s, blocks), share))
-        targets.append(target)
-        signs.append(sign)
-    operand = fold_operand(jnp.concatenate([ref[...] for ref in received], axis=0), jnp.concatenate(signs, axis=1))
-    return jnp.concatenate(targets, axis=1), operand
-
-
 def halo_operand(blocks, neighbours, halo):
     bands, targets, signs = [], [], []
-    detector = lax.axis_index("apa")
     lower, upper = neighbours[:, 0:1], neighbours[:, 1:2]
     never = -4 * planes[2].length
-    for way in range(2):
+    for way, other in enumerate(partners(lax.axis_index("apa"))):
         total = halo[way][:HALO_CH, :].astype(f32)
         for ref in halo[2:]:
             total += ref[way * HALO_CH : (way + 1) * HALO_CH, :].astype(f32)
         bands.append(total.astype(bf16))
-        other = detector + 2 * way - 1
         begin = jnp.where(upper == other, planes[2].length - HALO_CH, never)
         begin = jnp.where(lower == other, 0, begin)
         target, sign = fold_of_halo(jnp.where(other < 0, never, begin))
         targets.append(target)
         signs.append(sign)
-    operand = fold_operand(jnp.concatenate(bands, axis=0), jnp.concatenate(signs, axis=1))
+    signs = sign_columns(jnp.concatenate(signs, axis=1), bands[0].shape[1])
+    operand = fold_operand(jnp.concatenate(bands, axis=0), signs)
     return jnp.concatenate(targets, axis=1), operand
 
 
-def halves(plane, cosine, sine, turned):
-    straight = plane.count // 2
-    width = cosine.shape[1]
-    row = lax.broadcasted_iota(jnp.int32, (straight, cosine.shape[0]), 0)
-    column = lax.broadcasted_iota(jnp.int32, (straight, cosine.shape[0]), 1)
-    matrix = jnp.where(column == plane.half - plane.keep - row, 1.0, 0.0).astype(bf16)
-    if turned:
-        both = dot(matrix, jnp.concatenate(split(cosine - sine), axis=1))
-        return (cosine + sine)[:straight], both[:, :width] + both[:, width:]
-    high, low = split(cosine - sine)
-    return (cosine + sine)[:straight], dot(matrix, high) + dot(matrix, low)
-
-
-def last_plane(far, bands, folded, sums, diffs, wide):
-    plane = planes[2]
+def transform(table, values):
+    width = values.shape[1]
+    joined = jnp.concatenate(split(values), axis=1)
+    result = dot(table, jnp.concatenate([joined, joined], axis=0))
+    return result[:, :width] + result[:, width:]
+
+
+def to_frequencies(plane, chosen, operand, bands, folded, sums, diffs, table):
     rows = pl.ds(plane.row, plane.rows)
-    both = folded[rows, :] + dot(one_hot(plane.rows, plane.row, far[0]), far[1])
-    both += dot(one_hot(plane.rows, plane.row, bands[0]), bands[1])
+    both = folded[rows, :] + dot(chosen[rows, :], operand)
+    if bands is not None:
+        both += dot(one_hot(plane.rows, plane.row, bands[0]), bands[1])
     width = both.shape[1] // 2
-
-    def transform(table, values):
-        joined = jnp.concatenate(split(values), axis=1)
-        result = dot(table, jnp.concatenate([joined, joined], axis=0))
-        return result[:, :width] + result[:, width:]
-
-    even, odd = transform(wide[0], both[:, :width]), transform(wide[1], both[:, width:])
-    total, gap = multiplied(even, odd, sums[rows, :], diffs[rows, :])
-    cosine, sine = transform(wide[0, plane.keep :], total), transform(wide[1, plane.keep :], gap)
-    return jnp.concatenate(halves(plane, cosine, sine, True), axis=0)
-
-
-def first_planes(far, folded, sums, diffs, narrow):
-    plane = planes[0]
-    count = plane.rows
-    both = folded[: 2 * count, :] + dot(one_hot(2 * count, 0, far[0]), far[1])
-    width = both.shape[1] // 2
-
-    def transform(table, values):
-        high, low = split(jnp.concatenate(values, axis=1))
-        return dot(table, jnp.concatenate([high, high, low], axis=0))
-
-    even = transform(narrow[0], [both[:count, :width], both[count:, :width]])
-    odd = transform(narrow[1], [both[:count, width:], both[count:, width:]])
-    totals, gaps = [], []
-    for i in range(2):
-        rows, lanes = slice(i * count, (i + 1) * count), slice(i * width, (i + 1) * width)
-        total, gap = multiplied(even[:, lanes], odd[:, lanes], sums[rows, :], diffs[rows, :])
-        totals.append(total)
-        gaps.append(gap)
-    return halves(plane, transform(narrow[0], totals), transform(narrow[1], gaps), False)
-
-
-def put_first(result, *operands):
-    lower, upper = first_planes(*operands)
-    width, straight = result.shape[1], lower.shape[0]
-    for i in range(2):
-        lanes, start = slice(i * width, (i + 1) * width), planes[i].wire
-        result[start : start + straight, :] = lower[:, lanes]
-        result[start + straight : start + 2 * straight, :] = upper[:, lanes]
+    even, odd = transform(table[0], both[:, :width]), transform(table[1], both[:, width:])
+    return multiplied(even, odd, sums[rows, :], diffs[rows, :])
+
+
+def to_channels(result, plane, total, gap, table):
+    cosine, sine = transform(table[0, plane.keep :], total), transform(table[1, plane.keep :], gap)
+    straight, width = plane.count // 2, total.shape[1]
+    result[:straight, :] = (cosine + sine)[:straight]
+    back = jnp.concatenate(split(cosine - sine), axis=1)
+    turned = backwards(
+        straight, plane.half - plane.keep, back.shape[0], lambda matrix, first, stop: dot(matrix, back[first:stop])
+    )
+    result[straight : plane.count, :] = turned[:, :width] + turned[:, width:]
+
+
+def put(result, plane, chosen, operand, bands, folded, sums, diffs, table):
+    total, gap = to_frequencies(plane, chosen, operand, bands, folded, sums, diffs, table)
+    to_channels(result, plane, total, gap, table)
 
 
 def all_planes(blocks, share, neighbours, *refs):
     received, halo = refs[: blocks - 1], refs[blocks - 1 : 2 * blocks]
-    wires, folded, sums, diffs, narrow, wide, own = refs[2 * blocks : 2 * blocks + 7]
-    sends, result = refs[2 * blocks + 7 : 3 * blocks + 6], refs[3 * blocks + 6]
-    far = far_operand(blocks, share, wires, received)
-    bands = halo_operand(blocks, neighbours, halo)
-    put_first(result, far, folded, sums, diffs, narrow)
-    result[planes[2].wire :, :] = last_plane(far, bands, folded, sums, diffs, wide)
+    chosen, far_signs, folded, sums, diffs, narrow, wide, own = refs[2 * blocks : 2 * blocks + 8]
+    sends, result = refs[2 * blocks + 8 : 3 * blocks + 7], refs[3 * blocks + 7]
+    operand = fold_operand(jnp.concatenate([ref[...] for ref in received], axis=0), far_signs[...])
+    for plane in planes:
+        bands = halo_operand(blocks, neighbours, halo) if plane.keep else None
+        operands = (chosen, operand, bands, folded, sums, diffs, wide if plane.keep else narrow)
+        put(result.at[pl.ds(plane.wire, plane.count)], plane, *operands)
     here = lax.axis_index("chan")
     own[...] = result[pl.ds(pl.multiple_of(here * share, share), share), :]
     for shift, out in enumerate(sends, 1):
@@ -356,42 +346,60 @@
         out[...] = result[pl.ds(first, share), :].astype(bf16)
 
 
-def leading_planes(share, neighbours, far, halo0, halo1, halo2, wires, folded, sums, diffs, narrow, wide, send, rest,
-                   targets, operand, result):
-    targets[...], operand[...] = far_operand(2, share, wires, [far])
-    count = send.shape[0]
+def middle_plane(share, far, chosen, far_signs, folded, sums, diffs, narrow, wide_source, send, own, operand, wide, result, sem):
+    copy = pltpu.make_async_copy(wide_source, wide, sem)
+    copy.start()
+    middle = planes[1]
+    operand[...] = fold_operand(far[...], far_signs[...])
+    put(result, middle, chosen, operand[...], None, folded, sums, diffs, narrow)
+    below = share - middle.wire
+    above = middle.count - below
 
     @pl.when(lax.axis_index("chan") == 0)
     def _():
-        bands = halo_operand(2, neighbours, (halo0, halo1, halo2))
-        values = last_plane((targets[...], operand[...]), bands, folded, sums, diffs, wide)
-        send[...] = values.astype(bf16)
-        rest[...] = jnp.zeros(rest.shape, f32)
+        send[:above, :] = result[below:, :].astype(bf16)
+        send[above:, :] = jnp.zeros((below - above, send.shape[1]), bf16)
+        own[...] = result[:below, :]
 
     @pl.when(lax.axis_index("chan") != 0)
     def _():
-        put_first(result, (targets[...], operand[...]), folded, sums, diffs, narrow)
-        send[...] = result[:count, :].astype(bf16)
-        rest[...] = result[count:, :]
-
-
-def trailing_planes(share, neighbours, halo0, halo1, halo2, targets, operand, rest, folded, sums, diffs, narrow, wide,
-                    send, own, result):
-    more = send.shape[0]
-    operands = (targets[...], operand[...])
+        send[...] = result[:below, :].astype(bf16)
+        own[:above, :] = result[below:, :]
+        own[above:, :] = jnp.zeros((below - above, own.shape[1]), f32)
+
+    copy.wait()
+
+
+def outer_plane(neighbours, halo0, halo1, halo2, operand, chosen, folded, sums, diffs, narrow, wide, send, total, gap, result):
+    first, _, last = planes
+    bands = halo_operand(2, neighbours, (halo0, halo1, halo2))
 
     @pl.when(lax.axis_index("chan") == 0)
     def _():
-        put_first(result, operands, folded, sums, diffs, narrow)
-        own[...] = result[:share, :]
-        send[...] = result[share:, :].astype(bf16)
+        put(result, last, chosen, operand[...], bands, folded, sums, diffs, wide)
+        send[...] = result[...].astype(bf16)
 
     @pl.when(lax.axis_index("chan") != 0)
     def _():
-        bands = halo_operand(2, neighbours, (halo0, halo1, halo2))
-        own[more:, :] = last_plane(operands, bands, folded, sums, diffs, wide)
-        own[:more, :] = rest[more:, :]
-        send[...] = rest[:more, :].astype(bf16)
+        put(result, first, chosen, operand[...], None, folded, sums, diffs, narrow)
+        send[: first.count, :] = result[: first.count, :].astype(bf16)
+        send[first.count :, :] = jnp.zeros((last.count - first.count, send.shape[1]), bf16)
+        total[...], gap[...] = to_frequencies(last, chosen, operand[...], bands, folded, sums, diffs, wide)
+
+
+def inner_plane(operand, chosen, folded, sums, diffs, narrow, wide, total, gap, part, own):
+    first, middle, last = planes
+    above = own.shape[0] - last.count
+
+    @pl.when(lax.axis_index("chan") == 0)
+    def _():
+        put(own, first, chosen, operand[...], None, folded, sums, diffs, narrow)
+        own[first.count :, :] = part[...]
+
+    @pl.when(lax.axis_index("chan") != 0)
+    def _():
+        to_channels(own.at[pl.ds(above, last.count)], last, total[...], gap[...], wide)
+        own[:above, :] = part[:above, :]
 
 
 def spread_mask(mask, share, ticks):
@@ -479,6 +487,13 @@
                 copy.wait()
 
 
+costs = {
+    "tick_spectra": 500, "edge_bands": 200, "near_part": 600, "factors": 575, "middle_plane": 650, "outer_plane": 1100,
+    "inner_plane": 875, "own_signal": 500, "part_signal": 250, "all_planes": 2000,
+}
+costs = {name: cost * 1250000 for name, cost in costs.items()}
+
+
 def call(kernel, outs, ins, name, scratch=(), final=False, aliases=None):
     kind = jax.ShapeDtypeStruct if final else pltpu.VMEM
     return pl.pallas_call(
@@ -488,7 +503,7 @@
         out_specs=[pinned if final else whole] * len(outs),
         scratch_shapes=scratch,
         compiler_params=pltpu.CompilerParams(vmem_limit_bytes=28 * 1024 * 1024),
-        cost_estimate=pl.CostEstimate(flops=0, bytes_accessed=0, transcendentals=0),
+        cost_estimate=pl.CostEstimate(flops=costs[name], bytes_accessed=0, transcendentals=0),
         input_output_aliases=aliases or {},
         name=name,
     )
@@ -506,40 +521,44 @@
 
     def around(parts):
         return [
-            near(lax.ppermute(part, "chan", [(i, (i + s) % blocks) for i in range(blocks)]))
+            lax.ppermute(part, "chan", [(i, (i + s) % blocks) for i in range(blocks)])
             for s, part in enumerate(parts, 1)
         ]
 
     first = call(
         functools.partial(tick_spectra, blocks),
-        [((share, width), bf16)] * (blocks - 1) + [((blocks * HALO_CH, width), bf16)] * 2
+        [((share, width), bf16)] * (blocks - 1)
         + [((share, ticks), bf16), ((blocks, ticks, width), bf16), (wires.shape, jnp.int32), (neighbours.shape, jnp.int32)],
         [pinned] * 4, "tick_spectra", [pltpu.SemaphoreType.DMA((7,))],
     )(*map(distant, (frames, table, wires, neighbours)))
-    far, bands = first[: blocks - 1], first[blocks - 1 : blocks + 1]
-    frames, table, wires, neighbours = map(near, first[blocks + 1 :])
-    received = around(far)
-    tables = [channel_tables(planes[i].length, planes[i].rows, order) for i, order in ((0, (0, 1, 0)), (2, (0, 1)))]
-    sources = [kernel, *map(jnp.asarray, tables)]
+    frames, table, wires, neighbours = map(near, first[blocks - 1 :])
+    received = list(map(near, around(first[: blocks - 1])))
+    bands = call(
+        functools.partial(edge_bands, blocks), [((blocks * HALO_CH, width), bf16)] * 2, [whole] * 4, "edge_bands",
+    )(neighbours, frames, table, wires)
+    narrow, wide = (jnp.asarray(channel_tables(planes[i].length, planes[i].rows)) for i in (0, 2))
+    sources = [kernel, narrow] + ([wide] if blocks != 2 else [])
     folded, *ready = call(
-        lambda *refs: near_part(refs[:3], *refs[3:]),
+        lambda *refs: near_part(refs[: len(sources)], *refs[len(sources) :]),
         [((all_rows, 2 * width), f32)] + [(part.shape, part.dtype) for part in sources],
-        [pinned] * 3 + [whole] * 3, "near_part", [pltpu.SemaphoreType.DMA((3,))],
+        [pinned] * len(sources) + [whole] * 3, "near_part", [pltpu.SemaphoreType.DMA((len(sources),))],
     )(*map(distant, sources), wires, frames, table)
     halo = []
-    for step, band in zip((1, -1), bands):
-        pairs = [(a, a + step) for a in range(detectors) if 0 <= a + step < detectors]
+    for way, band in enumerate(bands):
+        pairs = [(a, partners(a)[way]) for a in range(detectors) if 0 <= partners(a)[way] < detectors]
         halo.append(lax.ppermute(band, "apa", pairs))
     *halo, folded = lax.optimization_barrier((*halo, folded))
     shares = [
         jnp.concatenate([band[s * HALO_CH : (s + 1) * HALO_CH] for band in halo]) for s in range(1, blocks)
     ]
-    halo = [near(band) for band in halo] + around(shares)
-    kernel, narrow, wide = map(near, ready)
+    halo = [near(band) for band in halo + around(shares)]
+    kernel, narrow, *rest = map(near, ready)
     folded = near(folded)
-    sums, diffs = map(near, call(
-        kernel_factors, [((all_rows, 2 * width), f32)] * 2, [whole], "kernel_factors",
-    )(kernel))
+    sums, diffs, chosen, far_signs = map(near, call(
+        functools.partial(factors, blocks, share),
+        [((all_rows, 2 * width), f32)] * 2 + [((all_rows, (blocks - 1) * share), bf16), (((blocks - 1) * share, width), f32)],
+        [whole] * 2, "factors",
+    )(kernel, wires))
     basis = jnp.asarray(inverse_tables(ticks, blocks, padded))
     filters = (wide_filter[None], tight_filter[None])
     mask = jnp.transpose(roi_mask)
@@ -558,10 +577,10 @@
         own, *sends = call(
             functools.partial(all_planes, blocks, share),
             [((share, width), f32)] + [((share, width), bf16)] * (blocks - 1),
-            [whole] * (2 * blocks + 7), "all_planes",
+            [whole] * (2 * blocks + 8), "all_planes",
             [pltpu.VMEM((CHANNELS, width), f32)],
-        )(neighbours, *received, *halo, wires, folded, sums, diffs, narrow, wide)
-        returned = around(sends)
+        )(neighbours, *received, *halo, chosen, far_signs, folded, sums, diffs, narrow, *rest)
+        returned = map(near, around(sends))
         signal, bases, inside = own_part(own)
         out = pl.pallas_call(
             functools.partial(whole_signal, blocks),
@@ -572,22 +591,25 @@
         )(signal, bases, inside, *returned)
         return out[None]
 
-    more = share - PW
-    sent, rest, *operands = call(
-        functools.partial(leading_planes, share),
-        [((PW, width), bf16), ((PU + PV - PW, width), f32), ((1, share), jnp.int32), ((share, 2 * width), bf16)],
-        [whole] * 11, "leading_planes", [pltpu.VMEM((PU + PV, width), f32)],
-    )(neighbours, *received, *halo, wires, folded, sums, diffs, narrow, wide)
+    below, above = share - PU, share - PW
+    sent, part, operand, wide = call(
+        functools.partial(middle_plane, share),
+        [((below, width), bf16), ((below, width), f32), ((share, 2 * width), bf16), (wide.shape, bf16)],
+        [whole] * 7 + [pinned], "middle_plane", [pltpu.VMEM((PV, width), f32), pltpu.SemaphoreType.DMA],
+    )(*received, chosen, far_signs, folded, sums, diffs, narrow, distant(wide))
     (early,) = around([sent])
-    sent, own = call(
-        functools.partial(trailing_planes, share), [((more, width), bf16), ((share, width), f32)],
-        [whole] * 12, "trailing_planes", [pltpu.VMEM((PU + PV, width), f32)],
-    )(neighbours, *halo, *map(near, operands), near(rest), folded, sums, diffs, narrow, wide)
-    (late,) = around([sent])
+    operands = (near(operand), chosen, folded, sums, diffs, narrow, near(wide))
+    last = ((planes[2].rows, width), f32)
+    sent, total, gap = call(
+        outer_plane, [((PW, width), bf16), last, last], [whole] * 11, "outer_plane", [pltpu.VMEM((PW, width), f32)],
+    )(neighbours, *halo, *operands)
+    sent, early = lax.optimization_barrier((sent, early))
+    (late,) = map(near, around([sent]))
+    (own,) = call(inner_plane, [((share, width), f32)], [whole] * 10, "inner_plane")(*operands, *map(near, (total, gap, part)))
     signal, bases, inside = own_part(own)
 
     def finish(values, spans, *before):
-        step = math.gcd(PW, more) // 2
+        step = math.gcd(PU, PW)
         rows = max(count for _, count in spans)
         (out,) = call(
             functools.partial(part_signal, spans), [((share, ticks), f32)],
@@ -597,8 +619,8 @@
         )(signal, bases, inside, values, *before)
         return out
 
-    out = finish(early, ((0, PW), (more, PW)))
-    return finish(late, ((PW, more), (0, more)), out)[None]
+    out = finish(near(early), ((PU, below), (0, above)))
+    return finish(late, ((0, PU), (above, PW)), out)[None]
 
 
 def solution(mesh):

time: 34.7 us -> 31.7 us (0.914)
  the two profiles are of different devices: /device:TPU:24 before, /device:TPU:0 now
where the time goes in v4:
time: 31.7 us; the launch traced here: 31.6 us
  Pallas kernels  20.7 us (65%)
  starting transfers between devices  7.15 us (23%)
  waiting for transfers between devices  3.4 us (11%)
  between operations  0.33 us (1%)
    ppermute x4, starting transfers between devices, around(): lax.ppermute(part, 'chan', [(i, (i + s) % blocks) for i in range(blocks)])  6.41 us
    pallas_call x1, Pallas kernels, body(): call(outer_plane, [((PW, width), bf16), last, last], [whole] * 11, 'outer...  4.59 us
    ppermute x4, waiting for transfers between devices, around(): lax.ppermute(part, 'chan', [(i, (i + s) % blocks) for i in range(blocks)])  3.4 us
    pallas_call x1, Pallas kernels, body(): call(functools.partial(middle_plane, share), [((below, width), bf16), ((b...  2.57 us
    pallas_call x1, Pallas kernels, body(): call(inner_plane, [((share, width), f32)], [whole] * 10, 'inner_plane')  2.48 us
    pallas_call x1, Pallas kernels, body(): call(lambda *refs: near_part(refs[:len(sources)], *refs[len(sources):]),...  2.43 us
    pallas_call x2, Pallas kernels, finish(): call(functools.partial(part_signal, spans), [((share, ticks), f32)], [who...  2.19 us
    pallas_call x1, Pallas kernels, own_part(): call(functools.partial(own_signal, blocks), signal_shapes, [whole, pinned...  2.05 us
  transfers between devices with their start and end apart: 6, of which 2 were waited for; matrix products, arithmetic and copies ran while one was open for 0% of the time, Pallas kernels for 56%

profile of v4, /device:TPU:0, one launch (start us, length us, event | category | flops | bytes accessed | tf_op | source)
XLA Modules:
  0.0 31.6 jit_solution(11858181993386224624)
XLA Ops:
  0.0 2.0 %tick_spectra.1 = (bf16[1280,128]{1,0:T(8,128)(2,1)S(1)}, bf16[1280,256]{1,0:T(8,128)(2,1)S(1)}, bf16[2,256,128]{2,1,0:T(8,128)(2,1)S(1)}, s32[1,2560]{1,0:T(1,128)S(1)}, s32[1,2]{1,0:T(1,128)S(1)}) custom-call(bf16[1280,256]{1,0:T(8,128)(2,1)} %bitcast.10, bf16[2,256,128]{2,1,0:T(8,128)(2,1)} %constant.8.clone.table_source, s32[1,2560]{1,0:T(1,128)} %wires_source.1, ...), custom_call_target="tpu_custom_call" | custom-call | flops 625000000 | tf_op jit(solution)/shard_map/tick_spectra/pallas_call | solution.py:528
  2.0 3.0 %collective-permute-start = (bf16[1280,128]{1,0:T(8,128)(2,1)S(1)}, bf16[1280,128]{1,0:T(8,128)(2,1)S(1)}, u32[]{:S(2)}, u32[]{:S(2)}) collective-permute-start(bf16[1280,128]{1,0:T(8,128)(2,1)S(1)} %get-tuple-element.34), channel_id=1, source_target_pairs={{0,1},{1,0},{2,3},{3,2},{4,5},{5,4},{6,7},{7,6},{8,9},{9,8},{10,11... | collective-permute-start | bytes 983048 | tf_op jit(solution)/shard_map/ppermute | solution.py:524
  5.0 0.8 %edge_bands.1 = (bf16[256,128]{1,0:T(8,128)(2,1)S(1)}, bf16[256,128]{1,0:T(8,128)(2,1)S(1)}) custom-call(s32[1,2]{1,0:T(1,128)S(1)} %get-tuple-element.41.neighbours, bf16[1280,256]{1,0:T(8,128)(2,1)S(1)} %get-tuple-element.36.refs_3_.frames, bf16[2,256,128]{2,1,0:T(8,128)(2,1)S(1)} %get-tuple-element.37.refs_4_.table, ...), custom_call_target="tpu_custom_call" | custom-call | flops 250000000 | tf_op jit(solution)/shard_map/edge_bands/pallas_call | solution.py:536
  5.9 0.1 collective-permute-start.1
  5.9 0.7 %collective-permute-start.2 = (bf16[256,128]{1,0:T(8,128)(2,1)S(1)}, bf16[256,128]{1,0:T(8,128)(2,1)S(1)}, u32[]{:S(2)}, u32[]{:S(2)}) collective-permute-start(bf16[256,128]{1,0:T(8,128)(2,1)S(1)} %get-tuple-element.43), channel_id=1, source_target_pairs={{2,4},{4,2},{6,8},{8,6},{10,12},{12,10},{14,16},{16,14},{18,20},{2... | collective-permute-start | bytes 196616 | tf_op jit(solution)/shard_map/ppermute | solution.py:549
  6.6 2.4 %near_part.1 = (f32[1456,256]{1,0:T(8,128)S(1)}, f32[2,64,2816]{2,1,0:T(8,128)S(1)}, bf16[2,416,832]{2,1,0:T(8,128)(2,1)S(1)}) custom-call(f32[2,64,2816]{2,1,0:T(8,128)} %refs_0_.1, bf16[2,416,832]{2,1,0:T(8,128)(2,1)} %constant.9.clone.refs_1_, s32[1,2560]{1,0:T(1,128)S(1)} %get-tuple-element.35.refs_2_.wires, ...), custom_call_target="tpu_custom_call" | custom-call | flops 750000000 | tf_op jit(solution)/shard_map/near_part/pallas_call | solution.py:541
  9.1 1.5 %factors.1 = (f32[1456,256]{1,0:T(8,128)S(1)}, f32[1456,256]{1,0:T(8,128)S(1)}, bf16[1456,1280]{1,0:T(8,128)(2,1)S(1)}, f32[1280,128]{1,0:T(8,128)S(1)}) custom-call(f32[2,64,2816]{2,1,0:T(8,128)S(1)} %get-tuple-element.38.kernel, s32[1,2560]{1,0:T(1,128)S(1)} %get-tuple-element.35.refs_2_.wires), custom_call_target="tpu_custom_call" | custom-call | flops 718750016 | tf_op jit(solution)/shard_map/factors/pallas_call | solution.py:557
  10.6 0.0 collective-permute-done.1.halo0
  10.6 0.0 collective-permute-done.2.halo1
  10.7 0.1 collective-permute-start.3
  10.7 2.0 %collective-permute-done.far = bf16[1280,128]{1,0:T(8,128)(2,1)S(1)} collective-permute-done((bf16[1280,128]{1,0:T(8,128)(2,1)S(1)}, bf16[1280,128]{1,0:T(8,128)(2,1)S(1)}, u32[]{:S(2)}, u32[]{:S(2)}) %collective-permute-start) | collective-permute-done | bytes 327712 | tf_op jit(solution)/shard_map/ppermute | solution.py:524
  12.7 2.6 %middle_plane.1 = (bf16[480,128]{1,0:T(8,128)(2,1)S(1)}, f32[480,128]{1,0:T(8,128)S(1)}, bf16[1280,256]{1,0:T(8,128)(2,1)S(1)}, bf16[2,624,1248]{2,1,0:T(8,128)(2,1)S(1)}) custom-call(bf16[1280,128]{1,0:T(8,128)(2,1)S(1)} %collective-permute-done.far, bf16[1456,1280]{1,0:T(8,128)(2,1)S(1)} %get-tuple-element.39.chosen, ...), custom_call_target="tpu_custom_call" | custom-call | flops 812499968 | tf_op jit(solution)/shard_map/middle_plane/pallas_call | solution.py:595
  15.3 1.8 %collective-permute-start.4 = (bf16[480,128]{1,0:T(8,128)(2,1)S(1)}, bf16[480,128]{1,0:T(8,128)(2,1)S(1)}, u32[]{:S(2)}, u32[]{:S(2)}) collective-permute-start(bf16[480,128]{1,0:T(8,128)(2,1)S(1)} %get-tuple-element.60), channel_id=1, source_target_pairs={{0,1},{1,0},{2,3},{3,2},{4,5},{5,4},{6,7},{7,6},{8,9},{9,8},{10,11... | collective-permute-start | bytes 368648 | tf_op jit(solution)/shard_map/ppermute | solution.py:524
  17.1 0.0 collective-permute-done.3.halo2
  17.1 4.6 %outer_plane.1 = (bf16[960,128]{1,0:T(8,128)(2,1)S(1)}, f32[624,128]{1,0:T(8,128)S(1)}, f32[624,128]{1,0:T(8,128)S(1)}) custom-call(s32[1,2]{1,0:T(1,128)S(1)} %get-tuple-element.41.neighbours, bf16[256,128]{1,0:T(8,128)(2,1)S(1)} %collective-permute-done.1.halo0, bf16[256,128]{1,0:T(8,128)(2,1)S(1)} %collective-permute-done.2.halo1, ...), custom_call_target="tpu_custom_call" | custom-call | flops 1375000064 | tf_op jit(solution)/shard_map/outer_plane/pallas_call | solution.py:603
  21.7 0.0 collective-permute-done.4.values
  21.7 1.5 %collective-permute-start.5 = (bf16[960,128]{1,0:T(8,128)(2,1)S(1)}, bf16[960,128]{1,0:T(8,128)(2,1)S(1)}, u32[]{:S(2)}, u32[]{:S(2)}) collective-permute-start(bf16[960,128]{1,0:T(8,128)(2,1)S(1)} %get-tuple-element.61), channel_id=1, source_target_pairs={{0,1},{1,0},{2,3},{3,2},{4,5},{5,4},{6,7},{7,6},{8,9},{9,8},{10,11... | collective-permute-start | bytes 737288 | tf_op jit(solution)/shard_map/ppermute | solution.py:524
  23.2 2.5 %inner_plane.1.own = f32[1280,128]{1,0:T(8,128)S(1)} custom-call(bf16[1280,256]{1,0:T(8,128)(2,1)S(1)} %get-tuple-element.49.operand, bf16[1456,1280]{1,0:T(8,128)(2,1)S(1)} %get-tuple-element.39.chosen, f32[1456,256]{1,0:T(8,128)S(1)} %get-tuple-element.45.folded, f32[1456,256]{1,0:T(8,128)S(1)} %get-tuple-element.46.sums, ...), custom_call_target="tpu_custom_call" | custom-call | flops 1093750016 | tf_op jit(solution)/shard_map/inner_plane/pallas_call | solution.py:608
  25.7 0.0 copy-done
  25.7 0.0 copy-done.1
  25.7 2.1 %own_signal.1 = (f32[1280,256]{1,0:T(8,128)S(1)}, bf16[1,256,512]{2,1,0:T(8,128)(2,1)S(1)}, f32[1280,256]{1,0:T(8,128)S(1)}) custom-call(f32[1280,128]{1,0:T(8,128)S(1)} %inner_plane.1.own, f32[2,128,256]{2,1,0:T(8,128)} %constant.11.clone.basis_source, f32[1,128]{1,0:T(1,128)S(1)} %bitcast.8, f32[1,128]{1,0:T(1,128)S(1)} %bitcast.9, s32[4,80]{1,0:T(4,128)S(1)} %bitcast.7), custom_call_target="tpu_custom_call" | custom-call | flops 625000000 | tf_op jit(solution)/shard_map/own_signal/pallas_call | solution.py:570
  27.8 1.0 %part_signal.2.refs_0_ = f32[1280,256]{1,0:T(8,128)} custom-call(f32[1280,256]{1,0:T(8,128)S(1)} %get-tuple-element.56.signal, bf16[1,256,512]{2,1,0:T(8,128)(2,1)S(1)} %get-tuple-element.57.bases, f32[1280,256]{1,0:T(8,128)S(1)} %get-tuple-element.58.inside, bf16[480,128]{1,0:T(8,128)(2,1)S(1)} %collective-permute-done.4.values), custom_call_target="tpu_custom_call" | custom-call | flops 312500000 | tf_op jit(solution)/shard_map/part_signal/pallas_call | solution.py:614
  28.8 1.4 %collective-permute-done.5.values = bf16[960,128]{1,0:T(8,128)(2,1)S(1)} collective-permute-done((bf16[960,128]{1,0:T(8,128)(2,1)S(1)}, bf16[960,128]{1,0:T(8,128)(2,1)S(1)}, u32[]{:S(2)}, u32[]{:S(2)}) %collective-permute-start.5) | collective-permute-done | bytes 245792 | tf_op jit(solution)/shard_map/ppermute | solution.py:524
  30.3 1.2 %part_signal.3 = f32[1280,256]{1,0:T(8,128)} custom-call(f32[1280,256]{1,0:T(8,128)S(1)} %get-tuple-element.56.signal, bf16[1,256,512]{2,1,0:T(8,128)(2,1)S(1)} %get-tuple-element.57.bases, f32[1280,256]{1,0:T(8,128)S(1)} %get-tuple-element.58.inside, bf16[960,128]{1,0:T(8,128)(2,1)S(1)} %collective-permute-done.5.values, ...), custom_call_target="tpu_custom_call", output_to_operand_aliasing={{}: (4, {})} | custom-call | flops 312500000 | tf_op jit(solution)/shard_map/part_signal/pallas_call | solution.py:614
  (7 shorter events, 0.0 us)
Async XLA Ops:
  2.0 10.7 %collective-permute-start = (bf16[1280,128]{1,0:T(8,128)(2,1)S(1)}, bf16[1280,128]{1,0:T(8,128)(2,1)S(1)}, u32[]{:S(2)}, u32[]{:S(2)}) collective-permute-start(bf16[1280,128]{1,0:T(8,128)(2,1)S(1)} %get-tuple-element.34), channel_id=1, source_target_pairs={{0,1},{1,0},{2,3},{3,2},{4,5},{5,4},{6,7},{7,6},{8,9},{9,8},{10,11... | collective-permute-start | bytes 983048 | tf_op jit(solution)/shard_map/ppermute | solution.py:524
  5.9 4.7 %collective-permute-start.1 = (bf16[256,128]{1,0:T(8,128)(2,1)S(1)}, bf16[256,128]{1,0:T(8,128)(2,1)S(1)}, u32[]{:S(2)}, u32[]{:S(2)}) collective-permute-start(bf16[256,128]{1,0:T(8,128)(2,1)S(1)} %get-tuple-element.42), channel_id=1, source_target_pairs={{0,2},{2,0},{4,6},{6,4},{8,10},{10,8},{12,14},{14,12},{16,18},{18,... | collective-permute-start | bytes 196616 | tf_op jit(solution)/shard_map/ppermute | solution.py:549
  5.9 4.7 %collective-permute-start.2 = (bf16[256,128]{1,0:T(8,128)(2,1)S(1)}, bf16[256,128]{1,0:T(8,128)(2,1)S(1)}, u32[]{:S(2)}, u32[]{:S(2)}) collective-permute-start(bf16[256,128]{1,0:T(8,128)(2,1)S(1)} %get-tuple-element.43), channel_id=1, source_target_pairs={{2,4},{4,2},{6,8},{8,6},{10,12},{12,10},{14,16},{16,14},{18,20},{2... | collective-permute-start | bytes 196616 | tf_op jit(solution)/shard_map/ppermute | solution.py:549
  10.7 6.5 %collective-permute-start.3 = (bf16[256,128]{1,0:T(8,128)(2,1)S(1)}, bf16[256,128]{1,0:T(8,128)(2,1)S(1)}, u32[]{:S(2)}, u32[]{:S(2)}) collective-permute-start(bf16[256,128]{1,0:T(8,128)(2,1)S(1)} %pad_maximum_fusion), channel_id=1, source_target_pairs={{0,1},{1,0},{2,3},{3,2},{4,5},{5,4},{6,7},{7,6},{8,9},{9,8},{10,11... | collective-permute-start | bytes 196616 | tf_op jit(solution)/shard_map/ppermute | solution.py:524
  15.3 6.4 %collective-permute-start.4 = (bf16[480,128]{1,0:T(8,128)(2,1)S(1)}, bf16[480,128]{1,0:T(8,128)(2,1)S(1)}, u32[]{:S(2)}, u32[]{:S(2)}) collective-permute-start(bf16[480,128]{1,0:T(8,128)(2,1)S(1)} %get-tuple-element.60), channel_id=1, source_target_pairs={{0,1},{1,0},{2,3},{3,2},{4,5},{5,4},{6,7},{7,6},{8,9},{9,8},{10,11... | collective-permute-start | bytes 368648 | tf_op jit(solution)/shard_map/ppermute | solution.py:524
  21.7 8.5 %collective-permute-start.5 = (bf16[960,128]{1,0:T(8,128)(2,1)S(1)}, bf16[960,128]{1,0:T(8,128)(2,1)S(1)}, u32[]{:S(2)}, u32[]{:S(2)}) collective-permute-start(bf16[960,128]{1,0:T(8,128)(2,1)S(1)} %get-tuple-element.61), channel_id=1, source_target_pairs={{0,1},{1,0},{2,3},{3,2},{4,5},{5,4},{6,7},{7,6},{8,9},{9,8},{10,11... | collective-permute-start | bytes 737288 | tf_op jit(solution)/shard_map/ppermute | solution.py:524
  23.2 2.5 %copy-start = (s32[1,80,4]{1,2,0:T(4,128)S(1)}, s32[1,80,4]{1,2,0:T(4,128)}, u32[]{:S(2)}) copy-start(s32[1,80,4]{1,2,0:T(4,128)} %param.17) | copy-start | bytes 3844
  23.2 2.5 %copy-start.1 = (f32[128]{0:T(128)S(1)}, f32[128]{0:T(128)}, u32[]{:S(2)}) copy-start(f32[128]{0:T(128)} %param.15) | copy-start | bytes 1540
  23.2 2.5 %copy-start.2 = (f32[128]{0:T(128)S(1)}, f32[128]{0:T(128)}, u32[]{:S(2)}) copy-start(f32[128]{0:T(128)} %param.16) | copy-start | bytes 1540

commit v5 on v4

--- a/solution.py
+++ b/solution.py
@@ -68,7 +68,7 @@
     return high, (values - high.astype(f32)).astype(bf16)
 
 
-def channel_tables(length, rows):
+def channel_tables(length, rows, order):
     index = np.arange(rows)
     angles = (index[:, None] * index[None, :] % length) * (two_pi / length)
     inside = (index <= length // 2).astype(np.float64)
@@ -77,7 +77,7 @@
     for values in (np.cos(angles) * mask, np.sin(angles) * mask):
         high = values.astype(np.float32).astype(ml_dtypes.bfloat16)
         low = (values - high.astype(np.float64)).astype(np.float32).astype(ml_dtypes.bfloat16)
-        found.append(np.concatenate([high, low], axis=1))
+        found.append(np.concatenate([(high, low)[i] for i in order], axis=1))
     return np.stack(found)
 
 
@@ -232,7 +232,9 @@
         copy.wait()
 
 
-def factors(blocks, share, kernel, wires, sums, diffs, chosen, far_signs):
+def factors(blocks, share, kernel, wires, wide_source, sums, diffs, chosen, far_signs, wide, sem):
+    copy = pltpu.make_async_copy(wide_source, wide, sem)
+    copy.start()
     harmonics, width = kernel.shape[1], sums.shape[1] // 2
     spare = width // 2 - harmonics
     for plane in planes:
@@ -267,6 +269,7 @@
         span = pl.ds((s - 1) * share, share)
         chosen[:, span] = one_hot(all_rows, 0, targets)
         far_signs[span, :] = sign_columns(signs, width)
+    copy.wait()
 
 
 def multiplied(even, odd, plus, minus):
@@ -297,48 +300,81 @@
     return jnp.concatenate(targets, axis=1), operand
 
 
-def transform(table, values):
+def one_plane(table, values):
     width = values.shape[1]
     joined = jnp.concatenate(split(values), axis=1)
     result = dot(table, jnp.concatenate([joined, joined], axis=0))
     return result[:, :width] + result[:, width:]
 
 
-def to_frequencies(plane, chosen, operand, bands, folded, sums, diffs, table):
-    rows = pl.ds(plane.row, plane.rows)
-    both = folded[rows, :] + dot(chosen[rows, :], operand)
-    if bands is not None:
-        both += dot(one_hot(plane.rows, plane.row, bands[0]), bands[1])
+def two_planes(table, values):
+    high, low = split(jnp.concatenate(values, axis=1))
+    return dot(table, jnp.concatenate([high, high, low], axis=0))
+
+
+def first_frequencies(folded, sums, diffs, table):
+    count, width = planes[0].rows, folded.shape[1] // 2
+    spans = [slice(i * count, (i + 1) * count) for i in range(2)]
+    even = two_planes(table[0], [folded[rows, :width] for rows in spans])
+    odd = two_planes(table[1], [folded[rows, width:] for rows in spans])
+    found = []
+    for i, rows in enumerate(spans):
+        lanes = slice(i * width, (i + 1) * width)
+        found.append(multiplied(even[:, lanes], odd[:, lanes], sums[rows, :], diffs[rows, :]))
+    return [jnp.concatenate(pair, axis=1) for pair in zip(*found)]
+
+
+def last_frequencies(bands, folded, sums, diffs, table):
+    plane = planes[2]
+    rows, edge = pl.ds(plane.row, plane.rows), ceil_to(HALO_CH + 1, 16)
+    both = folded[rows, :]
     width = both.shape[1] // 2
-    even, odd = transform(table[0], both[:, :width]), transform(table[1], both[:, width:])
+    both = jnp.concatenate([both[:edge] + dot(one_hot(edge, plane.row, bands[0]), bands[1]), both[edge:]], axis=0)
+    even, odd = one_plane(table[0], both[:, :width]), one_plane(table[1], both[:, width:])
     return multiplied(even, odd, sums[rows, :], diffs[rows, :])
 
 
-def to_channels(result, plane, total, gap, table):
-    cosine, sine = transform(table[0, plane.keep :], total), transform(table[1, plane.keep :], gap)
-    straight, width = plane.count // 2, total.shape[1]
+def put_first(result, total, gap, table):
+    width, straight = result.shape[1], planes[0].count // 2
+    cosine, sine = two_planes(table[0], [total]), two_planes(table[1], [gap])
+    lower = cosine + sine
+    high, low = split(cosine - sine)
+    upper = backwards(
+        straight, planes[0].half, high.shape[0],
+        lambda matrix, first, stop: dot(matrix, high[first:stop]) + dot(matrix, low[first:stop]),
+    )
+    for i in range(2):
+        lanes, start = slice(i * width, (i + 1) * width), planes[i].wire
+        result[start : start + straight, :] = lower[:straight, lanes]
+        result[start + straight : start + 2 * straight, :] = upper[:, lanes]
+
+
+def put_last(result, total, gap, table):
+    plane = planes[2]
+    width, straight = result.shape[1], plane.count // 2
+    cosine, sine = one_plane(table[0, plane.keep :], total), one_plane(table[1, plane.keep :], gap)
     result[:straight, :] = (cosine + sine)[:straight]
     back = jnp.concatenate(split(cosine - sine), axis=1)
     turned = backwards(
         straight, plane.half - plane.keep, back.shape[0], lambda matrix, first, stop: dot(matrix, back[first:stop])
     )
-    result[straight : plane.count, :] = turned[:, :width] + turned[:, width:]
-
-
-def put(result, plane, chosen, operand, bands, folded, sums, diffs, table):
-    total, gap = to_frequencies(plane, chosen, operand, bands, folded, sums, diffs, table)
-    to_channels(result, plane, total, gap, table)
+    result[straight:, :] = turned[:, :width] + turned[:, width:]
+
+
+def far_part(parts, *refs):
+    received, (chosen, far_signs, near, folded) = refs[:parts], refs[parts:]
+    operand = fold_operand(jnp.concatenate([ref[...] for ref in received], axis=0), far_signs[...])
+    folded[...] = near[...] + dot(chosen[...], operand)
 
 
 def all_planes(blocks, share, neighbours, *refs):
-    received, halo = refs[: blocks - 1], refs[blocks - 1 : 2 * blocks]
-    chosen, far_signs, folded, sums, diffs, narrow, wide, own = refs[2 * blocks : 2 * blocks + 8]
-    sends, result = refs[2 * blocks + 8 : 3 * blocks + 7], refs[3 * blocks + 7]
-    operand = fold_operand(jnp.concatenate([ref[...] for ref in received], axis=0), far_signs[...])
-    for plane in planes:
-        bands = halo_operand(blocks, neighbours, halo) if plane.keep else None
-        operands = (chosen, operand, bands, folded, sums, diffs, wide if plane.keep else narrow)
-        put(result.at[pl.ds(plane.wire, plane.count)], plane, *operands)
+    halo = refs[: blocks + 1]
+    folded, sums, diffs, narrow, wide, own = refs[blocks + 1 : blocks + 7]
+    sends, result = refs[blocks + 7 : 2 * blocks + 6], refs[2 * blocks + 6]
+    last = planes[2]
+    put_first(result, *first_frequencies(folded, sums, diffs, narrow), narrow)
+    parts = last_frequencies(halo_operand(blocks, neighbours, halo), folded, sums, diffs, wide)
+    put_last(result.at[pl.ds(last.wire, last.count)], *parts, wide)
     here = lax.axis_index("chan")
     own[...] = result[pl.ds(pl.multiple_of(here * share, share), share), :]
     for shift, out in enumerate(sends, 1):
@@ -346,60 +382,43 @@
         out[...] = result[pl.ds(first, share), :].astype(bf16)
 
 
-def middle_plane(share, far, chosen, far_signs, folded, sums, diffs, narrow, wide_source, send, own, operand, wide, result, sem):
-    copy = pltpu.make_async_copy(wide_source, wide, sem)
-    copy.start()
-    middle = planes[1]
-    operand[...] = fold_operand(far[...], far_signs[...])
-    put(result, middle, chosen, operand[...], None, folded, sums, diffs, narrow)
-    below = share - middle.wire
-    above = middle.count - below
+def leading_planes(neighbours, halo0, halo1, halo2, folded, sums, diffs, narrow, wide, send, rest, result):
+    last = planes[2]
+    count = send.shape[0]
 
     @pl.when(lax.axis_index("chan") == 0)
     def _():
-        send[:above, :] = result[below:, :].astype(bf16)
-        send[above:, :] = jnp.zeros((below - above, send.shape[1]), bf16)
-        own[...] = result[:below, :]
+        bands = halo_operand(2, neighbours, (halo0, halo1, halo2))
+        put_last(result.at[: last.count], *last_frequencies(bands, folded, sums, diffs, wide), wide)
+        left = last.count - count
+        send[...] = result[left : last.count, :].astype(bf16)
+        rest[:left, :] = result[:left, :]
 
     @pl.when(lax.axis_index("chan") != 0)
     def _():
-        send[...] = result[:below, :].astype(bf16)
-        own[:above, :] = result[below:, :]
-        own[above:, :] = jnp.zeros((below - above, own.shape[1]), f32)
-
-    copy.wait()
-
-
-def outer_plane(neighbours, halo0, halo1, halo2, operand, chosen, folded, sums, diffs, narrow, wide, send, total, gap, result):
-    first, _, last = planes
-    bands = halo_operand(2, neighbours, (halo0, halo1, halo2))
+        put_first(result, *first_frequencies(folded, sums, diffs, narrow), narrow)
+        send[...] = result[:count, :].astype(bf16)
+        rest[...] = result[count:, :]
+
+
+def trailing_planes(neighbours, halo0, halo1, halo2, folded, sums, diffs, narrow, wide, rest, send, own, result):
+    count, share, last = send.shape[0], own.shape[0], planes[2]
 
     @pl.when(lax.axis_index("chan") == 0)
     def _():
-        put(result, last, chosen, operand[...], bands, folded, sums, diffs, wide)
-        send[...] = result[...].astype(bf16)
+        put_first(result, *first_frequencies(folded, sums, diffs, narrow), narrow)
+        own[...] = result[:share, :]
+        left = result.shape[0] - share
+        send[:left, :] = result[share:, :].astype(bf16)
+        send[left:, :] = rest[: count - left, :].astype(bf16)
 
     @pl.when(lax.axis_index("chan") != 0)
     def _():
-        put(result, first, chosen, operand[...], None, folded, sums, diffs, narrow)
-        send[: first.count, :] = result[: first.count, :].astype(bf16)
-        send[first.count :, :] = jnp.zeros((last.count - first.count, send.shape[1]), bf16)
-        total[...], gap[...] = to_frequencies(last, chosen, operand[...], bands, folded, sums, diffs, wide)
-
-
-def inner_plane(operand, chosen, folded, sums, diffs, narrow, wide, total, gap, part, own):
-    first, middle, last = planes
-    above = own.shape[0] - last.count
-
-    @pl.when(lax.axis_index("chan") == 0)
-    def _():
-        put(own, first, chosen, operand[...], None, folded, sums, diffs, narrow)
-        own[first.count :, :] = part[...]
-
-    @pl.when(lax.axis_index("chan") != 0)
-    def _():
-        to_channels(own.at[pl.ds(above, last.count)], last, total[...], gap[...], wide)
-        own[:above, :] = part[:above, :]
+        above = share - last.count
+        bands = halo_operand(2, neighbours, (halo0, halo1, halo2))
+        put_last(own.at[pl.ds(above, last.count)], *last_frequencies(bands, folded, sums, diffs, wide), wide)
+        own[:above, :] = rest[count:, :]
+        send[...] = rest[:count, :].astype(bf16)
 
 
 def spread_mask(mask, share, ticks):
@@ -488,8 +507,8 @@
 
 
 costs = {
-    "tick_spectra": 500, "edge_bands": 200, "near_part": 600, "factors": 575, "middle_plane": 650, "outer_plane": 1100,
-    "inner_plane": 875, "own_signal": 500, "part_signal": 250, "all_planes": 2000,
+    "tick_spectra": 500, "edge_bands": 200, "near_part": 600, "factors": 575, "far_part": 300, "leading_planes": 850, "trailing_planes": 850,
+    "own_signal": 500, "part_signal": 250, "all_planes": 2000,
 }
 costs = {name: cost * 1250000 for name, cost in costs.items()}
 
@@ -536,8 +555,9 @@
     bands = call(
         functools.partial(edge_bands, blocks), [((blocks * HALO_CH, width), bf16)] * 2, [whole] * 4, "edge_bands",
     )(neighbours, frames, table, wires)
-    narrow, wide = (jnp.asarray(channel_tables(planes[i].length, planes[i].rows)) for i in (0, 2))
-    sources = [kernel, narrow] + ([wide] if blocks != 2 else [])
+    narrow = jnp.asarray(channel_tables(planes[0].length, planes[0].rows, (0, 1, 0)))
+    wide = jnp.asarray(channel_tables(planes[2].length, planes[2].rows, (0, 1)))
+    sources = [kernel, narrow]
     folded, *ready = call(
         lambda *refs: near_part(refs[: len(sources)], *refs[len(sources) :]),
         [((all_rows, 2 * width), f32)] + [(part.shape, part.dtype) for part in sources],
@@ -552,13 +572,19 @@
         jnp.concatenate([band[s * HALO_CH : (s + 1) * HALO_CH] for band in halo]) for s in range(1, blocks)
     ]
     halo = [near(band) for band in halo + around(shares)]
-    kernel, narrow, *rest = map(near, ready)
+    kernel, narrow = map(near, ready)
     folded = near(folded)
-    sums, diffs, chosen, far_signs = map(near, call(
+    spare_rows = (blocks - 1) * share
+    both = ((all_rows, 2 * width), f32)
+    sums, diffs, chosen, far_signs, wide = map(near, call(
         functools.partial(factors, blocks, share),
-        [((all_rows, 2 * width), f32)] * 2 + [((all_rows, (blocks - 1) * share), bf16), (((blocks - 1) * share, width), f32)],
-        [whole] * 2, "factors",
-    )(kernel, wires))
+        [both, both, ((all_rows, spare_rows), bf16), ((spare_rows, width), f32), (wide.shape, bf16)],
+        [whole] * 2 + [pinned], "factors", [pltpu.SemaphoreType.DMA],
+    )(kernel, wires, distant(wide)))
+    (folded,) = call(
+        functools.partial(far_part, blocks - 1), [both], [whole] * (blocks + 2), "far_part",
+    )(*received, chosen, far_signs, folded)
+    operands = (neighbours, *halo, near(folded), sums, diffs, narrow, wide)
     basis = jnp.asarray(inverse_tables(ticks, blocks, padded))
     filters = (wide_filter[None], tight_filter[None])
     mask = jnp.transpose(roi_mask)
@@ -567,19 +593,19 @@
     ]
 
     def own_part(own):
-        return map(near, call(
+        return call(
             functools.partial(own_signal, blocks), signal_shapes,
             [whole, pinned] + [whole] * 3, "own_signal",
             [pltpu.VMEM(basis.shape, f32), pltpu.SemaphoreType.DMA],
-        )(near(own), distant(basis), *filters, mask))
+        )(near(own), distant(basis), *filters, mask)
 
     if blocks != 2:
         own, *sends = call(
             functools.partial(all_planes, blocks, share),
             [((share, width), f32)] + [((share, width), bf16)] * (blocks - 1),
-            [whole] * (2 * blocks + 8), "all_planes",
+            [whole] * (blocks + 7), "all_planes",
             [pltpu.VMEM((CHANNELS, width), f32)],
-        )(neighbours, *received, *halo, chosen, far_signs, folded, sums, diffs, narrow, *rest)
+        )(*operands)
         returned = map(near, around(sends))
         signal, bases, inside = own_part(own)
         out = pl.pallas_call(
@@ -588,39 +614,36 @@
             in_specs=[whole] * (blocks + 2),
             out_specs=whole,
             name="whole_signal",
-        )(signal, bases, inside, *returned)
+        )(*map(near, (signal, bases, inside)), *returned)
         return out[None]
 
-    below, above = share - PU, share - PW
-    sent, part, operand, wide = call(
-        functools.partial(middle_plane, share),
-        [((below, width), bf16), ((below, width), f32), ((share, 2 * width), bf16), (wide.shape, bf16)],
-        [whole] * 7 + [pinned], "middle_plane", [pltpu.VMEM((PV, width), f32), pltpu.SemaphoreType.DMA],
-    )(*received, chosen, far_signs, folded, sums, diffs, narrow, distant(wide))
-    (early,) = around([sent])
-    operands = (near(operand), chosen, folded, sums, diffs, narrow, near(wide))
-    last = ((planes[2].rows, width), f32)
-    sent, total, gap = call(
-        outer_plane, [((PW, width), bf16), last, last], [whole] * 11, "outer_plane", [pltpu.VMEM((PW, width), f32)],
-    )(neighbours, *halo, *operands)
-    sent, early = lax.optimization_barrier((sent, early))
+    below, above = share - PU, PU + PV - share
+    sent, rest = call(
+        leading_planes, [((PU, width), bf16), ((PV, width), f32)],
+        [whole] * 9, "leading_planes", [pltpu.VMEM((PU + PV, width), f32)],
+    )(*operands)
+    (early,) = map(near, around([sent]))
+    sent, own = call(
+        trailing_planes, [((below, width), bf16), ((share, width), f32)],
+        [whole] * 10, "trailing_planes", [pltpu.VMEM((PU + PV, width), f32)],
+    )(*operands, near(rest))
+    signal, bases, inside = own_part(own)
+    signal = near(signal)
     (late,) = map(near, around([sent]))
-    (own,) = call(inner_plane, [((share, width), f32)], [whole] * 10, "inner_plane")(*operands, *map(near, (total, gap, part)))
-    signal, bases, inside = own_part(own)
 
     def finish(values, spans, *before):
-        step = math.gcd(PU, PW)
+        step = math.gcd(PU, below)
         rows = max(count for _, count in spans)
         (out,) = call(
             functools.partial(part_signal, spans), [((share, ticks), f32)],
             [whole] * 4 + [pinned] * len(before), "part_signal",
             [pltpu.VMEM((rows, ticks), f32), pltpu.SemaphoreType.DMA((rows // step,))],
             final=True, aliases={4: 0} if before else None,
-        )(signal, bases, inside, values, *before)
+        )(signal, near(bases), near(inside), values, *before)
         return out
 
-    out = finish(near(early), ((PU, below), (0, above)))
-    return finish(late, ((0, PU), (above, PW)), out)[None]
+    out = finish(early, ((0, PU), (below, PU)))
+    return finish(late, ((PU, below), (0, below)), out)[None]
 
 
 def solution(mesh):

time: 31.7 us -> 28.9 us (0.912)
  the two profiles are of different devices: /device:TPU:0 before, /device:TPU:24 now
where the time goes in v5:
time: 28.9 us; the launch traced here: 28.7 us
  Pallas kernels  17.1 us (59%)
  starting transfers between devices  8.35 us (29%)
  waiting for transfers between devices  2.88 us (10%)
    ppermute x4, starting transfers between devices, around(): lax.ppermute(part, 'chan', [(i, (i + s) % blocks) for i in range(blocks)])  4.91 us
    ppermute x2, starting transfers between devices, body(): halo.append(lax.ppermute(band, 'apa', pairs))  3.44 us
    pallas_call x1, Pallas kernels, body(): call(leading_planes, [((PU, width), bf16), ((PV, width), f32)], [whole] *...  2.44 us
    pallas_call x1, Pallas kernels, body(): call(lambda *refs: near_part(refs[:len(sources)], *refs[len(sources):]),...  2.44 us
    pallas_call x2, Pallas kernels, finish(): call(functools.partial(part_signal, spans), [((share, ticks), f32)], [who...  2.17 us
    ppermute x4, waiting for transfers between devices, around(): lax.ppermute(part, 'chan', [(i, (i + s) % blocks) for i in range(blocks)])  2.13 us
    pallas_call x1, Pallas kernels, own_part(): call(functools.partial(own_signal, blocks), signal_shapes, [whole, pinned...  2.06 us
    pallas_call x1, Pallas kernels, body(): call(trailing_planes, [((below, width), bf16), ((share, width), f32)], [w...  2.03 us
  transfers between devices with their start and end apart: 6, of which 4 were waited for; matrix products, arithmetic and copies ran while one was open for 0% of the time, Pallas kernels for 41%

profile of v5, /device:TPU:24, one launch (start us, length us, event | category | flops | bytes accessed | tf_op | source)
XLA Modules:
  0.0 28.7 jit_solution(6424254696139284277)
XLA Ops:
  0.0 2.0 %tick_spectra.1 = (bf16[1280,128]{1,0:T(8,128)(2,1)S(1)}, bf16[1280,256]{1,0:T(8,128)(2,1)S(1)}, bf16[2,256,128]{2,1,0:T(8,128)(2,1)S(1)}, s32[1,2560]{1,0:T(1,128)S(1)}, s32[1,2]{1,0:T(1,128)S(1)}) custom-call(bf16[1280,256]{1,0:T(8,128)(2,1)} %bitcast.10, bf16[2,256,128]{2,1,0:T(8,128)(2,1)} %constant.8.clone.table_source, s32[1,2560]{1,0:T(1,128)} %wires_source.1, ...), custom_call_target="tpu_custom_call" | custom-call | flops 625000000 | tf_op jit(solution)/shard_map/tick_spectra/pallas_call | solution.py:547
  2.0 1.6 %collective-permute-start.3 = (bf16[1280,128]{1,0:T(8,128)(2,1)S(1)}, bf16[1280,128]{1,0:T(8,128)(2,1)S(1)}, u32[]{:S(2)}, u32[]{:S(2)}) collective-permute-start(bf16[1280,128]{1,0:T(8,128)(2,1)S(1)} %get-tuple-element.39), channel_id=1, source_target_pairs={{0,1},{1,0},{2,3},{3,2},{4,5},{5,4},{6,7},{7,6},{8,9},{9,8},{10,11... | collective-permute-start | bytes 983048 | tf_op jit(solution)/shard_map/ppermute | solution.py:543
  3.6 0.8 %edge_bands.1 = (bf16[256,128]{1,0:T(8,128)(2,1)S(1)}, bf16[256,128]{1,0:T(8,128)(2,1)S(1)}) custom-call(s32[1,2]{1,0:T(1,128)S(1)} %get-tuple-element.30.neighbours, bf16[1280,256]{1,0:T(8,128)(2,1)S(1)} %get-tuple-element.31.frames.refs_3_, bf16[2,256,128]{2,1,0:T(8,128)(2,1)S(1)} %get-tuple-element.32.table.refs_4_, ...), custom_call_target="tpu_custom_call" | custom-call | flops 250000000 | tf_op jit(solution)/shard_map/edge_bands/pallas_call | solution.py:555
  4.4 0.1 collective-permute-start
  4.5 3.4 %collective-permute-start.1 = (bf16[256,128]{1,0:T(8,128)(2,1)S(1)}, bf16[256,128]{1,0:T(8,128)(2,1)S(1)}, u32[]{:S(2)}, u32[]{:S(2)}) collective-permute-start(bf16[256,128]{1,0:T(8,128)(2,1)S(1)} %get-tuple-element.35), channel_id=1, source_target_pairs={{2,4},{4,2},{6,8},{8,6},{10,12},{12,10},{14,16},{16,14},{18,20},{2... | collective-permute-start | bytes 196616 | tf_op jit(solution)/shard_map/ppermute | solution.py:569
  7.9 2.4 %near_part.1 = (f32[1456,256]{1,0:T(8,128)S(1)}, f32[2,64,2816]{2,1,0:T(8,128)S(1)}, bf16[2,416,1248]{2,1,0:T(8,128)(2,1)S(1)}) custom-call(f32[2,64,2816]{2,1,0:T(8,128)} %refs_0_.1, bf16[2,416,1248]{2,1,0:T(8,128)(2,1)} %constant.9.clone.refs_1_, s32[1,2560]{1,0:T(1,128)S(1)} %get-tuple-element.33.wires.refs_2_, ...), custom_call_target="tpu_custom_call" | custom-call | flops 750000000 | tf_op jit(solution)/shard_map/near_part/pallas_call | solution.py:561
  10.3 0.0 collective-permute-done.halo0
  10.3 0.8 %collective-permute-done.1.halo1 = bf16[256,128]{1,0:T(8,128)(2,1)S(1)} collective-permute-done((bf16[256,128]{1,0:T(8,128)(2,1)S(1)}, bf16[256,128]{1,0:T(8,128)(2,1)S(1)}, u32[]{:S(2)}, u32[]{:S(2)}) %collective-permute-start.1) | collective-permute-done | bytes 65568 | tf_op jit(solution)/shard_map/ppermute | solution.py:569
  11.1 0.6 %collective-permute-start.2 = (bf16[256,128]{1,0:T(8,128)(2,1)S(1)}, bf16[256,128]{1,0:T(8,128)(2,1)S(1)}, u32[]{:S(2)}, u32[]{:S(2)}) collective-permute-start(bf16[256,128]{1,0:T(8,128)(2,1)S(1)} %pad_maximum_fusion), channel_id=1, source_target_pairs={{0,1},{1,0},{2,3},{3,2},{4,5},{5,4},{6,7},{7,6},{8,9},{9,8},{10,11... | collective-permute-start | bytes 196616 | tf_op jit(solution)/shard_map/ppermute | solution.py:543
  11.7 1.9 %factors.1 = (f32[1456,256]{1,0:T(8,128)S(1)}, f32[1456,256]{1,0:T(8,128)S(1)}, bf16[1456,1280]{1,0:T(8,128)(2,1)S(1)}, f32[1280,128]{1,0:T(8,128)S(1)}, bf16[2,624,1248]{2,1,0:T(8,128)(2,1)S(1)}) custom-call(f32[2,64,2816]{2,1,0:T(8,128)S(1)} %get-tuple-element.40.kernel, s32[1,2560]{1,0:T(1,128)S(1)} %get-tuple-element.33.wires.refs_2_, ...), custom_call_target="tpu_custom_call" | custom-call | flops 718750016 | tf_op jit(solution)/shard_map/factors/pallas_call | solution.py:579
  13.6 0.0 collective-permute-done.3.refs_0_
  13.6 1.3 %far_part.1.folded = f32[1456,256]{1,0:T(8,128)S(1)} custom-call(bf16[1280,128]{1,0:T(8,128)(2,1)S(1)} %collective-permute-done.3.refs_0_, bf16[1456,1280]{1,0:T(8,128)(2,1)S(1)} %get-tuple-element.41.refs_1_, f32[1280,128]{1,0:T(8,128)S(1)} %get-tuple-element.42.refs_2_, f32[1456,256]{1,0:T(8,128)S(1)} %get-tuple-element.43.refs_3_), custom_call_target="tpu_custom_call" | custom-call | flops 375000000 | tf_op jit(solution)/shard_map/far_part/pallas_call | solution.py:584
  14.9 0.8 %collective-permute-done.2.halo2 = bf16[256,128]{1,0:T(8,128)(2,1)S(1)} collective-permute-done((bf16[256,128]{1,0:T(8,128)(2,1)S(1)}, bf16[256,128]{1,0:T(8,128)(2,1)S(1)}, u32[]{:S(2)}, u32[]{:S(2)}) %collective-permute-start.2) | collective-permute-done | bytes 65568 | tf_op jit(solution)/shard_map/ppermute | solution.py:543
  15.7 2.4 %leading_planes.1 = (bf16[800,128]{1,0:T(8,128)(2,1)S(1)}, f32[800,128]{1,0:T(8,128)S(1)}) custom-call(s32[1,2]{1,0:T(1,128)S(1)} %get-tuple-element.30.neighbours, bf16[256,128]{1,0:T(8,128)(2,1)S(1)} %collective-permute-done.halo0, bf16[256,128]{1,0:T(8,128)(2,1)S(1)} %collective-permute-done.1.halo1, bf16[256,128]{1,0:T(8,128)(2,1)S(1)} %collective-permute-done.2.halo2, ...), custom_call_target="tpu_custom_call" | custom-call | flops 1062499968 | tf_op jit(solution)/shard_map/leading_planes/pallas_call | solution.py:621
  18.1 0.3 collective-permute-start.5
  18.4 2.0 %trailing_planes.1 = (bf16[480,128]{1,0:T(8,128)(2,1)S(1)}, f32[1280,128]{1,0:T(8,128)S(1)}) custom-call(s32[1,2]{1,0:T(1,128)S(1)} %get-tuple-element.30.neighbours, bf16[256,128]{1,0:T(8,128)(2,1)S(1)} %collective-permute-done.halo0, bf16[256,128]{1,0:T(8,128)(2,1)S(1)} %collective-permute-done.1.halo1, bf16[256,128]{1,0:T(8,128)(2,1)S(1)} %collective-permute-done.2.halo2, ...), custom_call_target="tpu_custom_call" | custom-call | flops 1062499968 | tf_op jit(solution)/shard_map/trailing_planes/pallas_call | solution.py:626
  20.4 2.5 %collective-permute-start.4 = (bf16[480,128]{1,0:T(8,128)(2,1)S(1)}, bf16[480,128]{1,0:T(8,128)(2,1)S(1)}, u32[]{:S(2)}, u32[]{:S(2)}) collective-permute-start(bf16[480,128]{1,0:T(8,128)(2,1)S(1)} %get-tuple-element.53), channel_id=1, source_target_pairs={{0,1},{1,0},{2,3},{3,2},{4,5},{5,4},{6,7},{7,6},{8,9},{9,8},{10,11... | collective-permute-start | bytes 368648 | tf_op jit(solution)/shard_map/ppermute | solution.py:543
  22.9 0.0 copy-done
  22.9 0.0 copy-done.2
  22.9 2.1 %own_signal.1 = (f32[1280,256]{1,0:T(8,128)S(1)}, bf16[1,256,512]{2,1,0:T(8,128)(2,1)S(1)}, f32[1280,256]{1,0:T(8,128)S(1)}) custom-call(f32[1280,128]{1,0:T(8,128)S(1)} %get-tuple-element.49.own, f32[2,128,256]{2,1,0:T(8,128)} %constant.11.clone.basis_source, f32[1,128]{1,0:T(1,128)S(1)} %bitcast.8, f32[1,128]{1,0:T(1,128)S(1)} %bitcast.9, s32[4,80]{1,0:T(4,128)S(1)} %bitcast.7), custom_call_target="tpu_custom_call" | custom-call | flops 625000000 | tf_op jit(solution)/shard_map/own_signal/pallas_call | solution.py:596
  25.0 1.2 %collective-permute-done.5.values = bf16[800,128]{1,0:T(8,128)(2,1)S(1)} collective-permute-done((bf16[800,128]{1,0:T(8,128)(2,1)S(1)}, bf16[800,128]{1,0:T(8,128)(2,1)S(1)}, u32[]{:S(2)}, u32[]{:S(2)}) %collective-permute-start.5) | collective-permute-done | bytes 204832 | tf_op jit(solution)/shard_map/ppermute | solution.py:543
  26.2 1.2 %part_signal.2.refs_0_ = f32[1280,256]{1,0:T(8,128)} custom-call(f32[1280,256]{1,0:T(8,128)S(1)} %get-tuple-element.50.signal, bf16[1,256,512]{2,1,0:T(8,128)(2,1)S(1)} %get-tuple-element.51.bases, f32[1280,256]{1,0:T(8,128)S(1)} %get-tuple-element.52.inside, bf16[800,128]{1,0:T(8,128)(2,1)S(1)} %collective-permute-done.5.values), custom_call_target="tpu_custom_call" | custom-call | flops 312500000 | tf_op jit(solution)/shard_map/part_signal/pallas_call | solution.py:637
  27.3 0.2 collective-permute-done.4.values
  27.5 1.0 %part_signal.3 = f32[1280,256]{1,0:T(8,128)} custom-call(f32[1280,256]{1,0:T(8,128)S(1)} %get-tuple-element.50.signal, bf16[1,256,512]{2,1,0:T(8,128)(2,1)S(1)} %get-tuple-element.51.bases, f32[1280,256]{1,0:T(8,128)S(1)} %get-tuple-element.52.inside, bf16[480,128]{1,0:T(8,128)(2,1)S(1)} %collective-permute-done.4.values, ...), custom_call_target="tpu_custom_call", output_to_operand_aliasing={{}: (4, {})} | custom-call | flops 312500000 | tf_op jit(solution)/shard_map/part_signal/pallas_call | solution.py:637
  (7 shorter events, 0.0 us)
Async XLA Ops:
  2.0 11.6 %collective-permute-start.3 = (bf16[1280,128]{1,0:T(8,128)(2,1)S(1)}, bf16[1280,128]{1,0:T(8,128)(2,1)S(1)}, u32[]{:S(2)}, u32[]{:S(2)}) collective-permute-start(bf16[1280,128]{1,0:T(8,128)(2,1)S(1)} %get-tuple-element.39), channel_id=1, source_target_pairs={{0,1},{1,0},{2,3},{3,2},{4,5},{5,4},{6,7},{7,6},{8,9},{9,8},{10,11... | collective-permute-start | bytes 983048 | tf_op jit(solution)/shard_map/ppermute | solution.py:543
  4.4 5.9 %collective-permute-start = (bf16[256,128]{1,0:T(8,128)(2,1)S(1)}, bf16[256,128]{1,0:T(8,128)(2,1)S(1)}, u32[]{:S(2)}, u32[]{:S(2)}) collective-permute-start(bf16[256,128]{1,0:T(8,128)(2,1)S(1)} %get-tuple-element.34), channel_id=1, source_target_pairs={{0,2},{2,0},{4,6},{6,4},{8,10},{10,8},{12,14},{14,12},{16,18},{18,... | collective-permute-start | bytes 196616 | tf_op jit(solution)/shard_map/ppermute | solution.py:569
  4.5 6.6 %collective-permute-start.1 = (bf16[256,128]{1,0:T(8,128)(2,1)S(1)}, bf16[256,128]{1,0:T(8,128)(2,1)S(1)}, u32[]{:S(2)}, u32[]{:S(2)}) collective-permute-start(bf16[256,128]{1,0:T(8,128)(2,1)S(1)} %get-tuple-element.35), channel_id=1, source_target_pairs={{2,4},{4,2},{6,8},{8,6},{10,12},{12,10},{14,16},{16,14},{18,20},{2... | collective-permute-start | bytes 196616 | tf_op jit(solution)/shard_map/ppermute | solution.py:569
  11.1 4.5 %collective-permute-start.2 = (bf16[256,128]{1,0:T(8,128)(2,1)S(1)}, bf16[256,128]{1,0:T(8,128)(2,1)S(1)}, u32[]{:S(2)}, u32[]{:S(2)}) collective-permute-start(bf16[256,128]{1,0:T(8,128)(2,1)S(1)} %pad_maximum_fusion), channel_id=1, source_target_pairs={{0,1},{1,0},{2,3},{3,2},{4,5},{5,4},{6,7},{7,6},{8,9},{9,8},{10,11... | collective-permute-start | bytes 196616 | tf_op jit(solution)/shard_map/ppermute | solution.py:543
  18.1 8.1 %collective-permute-start.5 = (bf16[800,128]{1,0:T(8,128)(2,1)S(1)}, bf16[800,128]{1,0:T(8,128)(2,1)S(1)}, u32[]{:S(2)}, u32[]{:S(2)}) collective-permute-start(bf16[800,128]{1,0:T(8,128)(2,1)S(1)} %get-tuple-element.54), channel_id=1, source_target_pairs={{0,1},{1,0},{2,3},{3,2},{4,5},{5,4},{6,7},{7,6},{8,9},{9,8},{10,11... | collective-permute-start | bytes 614408 | tf_op jit(solution)/shard_map/ppermute | solution.py:543
  18.4 4.5 %copy-start = (s32[1,80,4]{1,2,0:T(4,128)S(1)}, s32[1,80,4]{1,2,0:T(4,128)}, u32[]{:S(2)}) copy-start(s32[1,80,4]{1,2,0:T(4,128)} %param.17) | copy-start | bytes 3844
  18.4 4.5 %copy-start.1 = (f32[128]{0:T(128)S(1)}, f32[128]{0:T(128)}, u32[]{:S(2)}) copy-start(f32[128]{0:T(128)} %param.15) | copy-start | bytes 1540
  18.4 4.5 %copy-start.2 = (f32[128]{0:T(128)S(1)}, f32[128]{0:T(128)}, u32[]{:S(2)}) copy-start(f32[128]{0:T(128)} %param.16) | copy-start | bytes 1540
  20.4 7.1 %collective-permute-start.4 = (bf16[480,128]{1,0:T(8,128)(2,1)S(1)}, bf16[480,128]{1,0:T(8,128)(2,1)S(1)}, u32[]{:S(2)}, u32[]{:S(2)}) collective-permute-start(bf16[480,128]{1,0:T(8,128)(2,1)S(1)} %get-tuple-element.53), channel_id=1, source_target_pairs={{0,1},{1,0},{2,3},{3,2},{4,5},{5,4},{6,7},{7,6},{8,9},{9,8},{10,11... | collective-permute-start | bytes 368648 | tf_op jit(solution)/shard_map/ppermute | solution.py:543

commit v6 on v5

--- a/solution.py
+++ b/solution.py
@@ -120,7 +120,7 @@
 
 def tick_spectra(blocks, frames_source, table_source, wires_source, neighbours_source, *refs):
     outs, (frames, table, wires, neighbours, sems) = refs[: blocks - 1], refs[blocks - 1 :]
-    parts = 4
+    parts = 1
     size = frames.shape[0] // parts
     spans = [pl.ds(i * size, size) for i in range(parts)]
     pairs = [(table_source, table)] + [(frames_source.at[span], frames.at[span]) for span in spans]
@@ -632,7 +632,7 @@
     (late,) = map(near, around([sent]))
 
     def finish(values, spans, *before):
-        step = math.gcd(PU, below)
+        step = values.shape[0] // 2
         rows = max(count for _, count in spans)
         (out,) = call(
             functools.partial(part_signal, spans), [((share, ticks), f32)],

time: 28.9 us -> 28.5 us (0.986)
  Pallas kernels: 17.1 us -> 16.7 us
    pallas_call x1, Pallas kernels: 1.98 us -> 1.56 us  [body(): call(functools.partial(tick_spectra, blocks), [((share, width), bf16)] *...]
  transfers between devices with their start and end apart: 6 -> 6, of which waited for: 4 -> 4; matrix products, arithmetic and copies ran while one was open for 0% -> 0% of each run, Pallas kernels for 41% -> 42%
where the time goes in v6:
time: 28.5 us; the launch traced here: 28.2 us
  Pallas kernels  16.7 us (59%)
  starting transfers between devices  8.36 us (29%)
  waiting for transfers between devices  2.86 us (10%)
    ppermute x4, starting transfers between devices, around(): lax.ppermute(part, 'chan', [(i, (i + s) % blocks) for i in range(blocks)])  4.91 us
    ppermute x2, starting transfers between devices, body(): halo.append(lax.ppermute(band, 'apa', pairs))  3.45 us
    pallas_call x1, Pallas kernels, body(): call(leading_planes, [((PU, width), bf16), ((PV, width), f32)], [whole] *...  2.44 us
    pallas_call x1, Pallas kernels, body(): call(lambda *refs: near_part(refs[:len(sources)], *refs[len(sources):]),...  2.43 us
    pallas_call x2, Pallas kernels, finish(): call(functools.partial(part_signal, spans), [((share, ticks), f32)], [who...  2.2 us
    ppermute x4, waiting for transfers between devices, around(): lax.ppermute(part, 'chan', [(i, (i + s) % blocks) for i in range(blocks)])  2.1 us
    pallas_call x1, Pallas kernels, own_part(): call(functools.partial(own_signal, blocks), signal_shapes, [whole, pinned...  2.05 us
    pallas_call x1, Pallas kernels, body(): call(trailing_planes, [((below, width), bf16), ((share, width), f32)], [w...  2.03 us
  transfers between devices with their start and end apart: 6, of which 4 were waited for; matrix products, arithmetic and copies ran while one was open for 0% of the time, Pallas kernels for 42%

profile of v6, /device:TPU:24, one launch (start us, length us, event | category | flops | bytes accessed | tf_op | source)
XLA Modules:
  0.0 28.2 jit_solution(4943071554706151306)
XLA Ops:
  0.0 1.6 %tick_spectra.1 = (bf16[1280,128]{1,0:T(8,128)(2,1)S(1)}, bf16[1280,256]{1,0:T(8,128)(2,1)S(1)}, bf16[2,256,128]{2,1,0:T(8,128)(2,1)S(1)}, s32[1,2560]{1,0:T(1,128)S(1)}, s32[1,2]{1,0:T(1,128)S(1)}) custom-call(bf16[1280,256]{1,0:T(8,128)(2,1)} %bitcast.10, bf16[2,256,128]{2,1,0:T(8,128)(2,1)} %constant.8.clone.table_source, s32[1,2560]{1,0:T(1,128)} %wires_source.1, ...), custom_call_target="tpu_custom_call" | custom-call | flops 625000000 | tf_op jit(solution)/shard_map/tick_spectra/pallas_call | solution.py:547
  1.6 1.6 %collective-permute-start.3 = (bf16[1280,128]{1,0:T(8,128)(2,1)S(1)}, bf16[1280,128]{1,0:T(8,128)(2,1)S(1)}, u32[]{:S(2)}, u32[]{:S(2)}) collective-permute-start(bf16[1280,128]{1,0:T(8,128)(2,1)S(1)} %get-tuple-element.39), channel_id=1, source_target_pairs={{0,1},{1,0},{2,3},{3,2},{4,5},{5,4},{6,7},{7,6},{8,9},{9,8},{10,11... | collective-permute-start | bytes 983048 | tf_op jit(solution)/shard_map/ppermute | solution.py:543
  3.2 0.8 %edge_bands.1 = (bf16[256,128]{1,0:T(8,128)(2,1)S(1)}, bf16[256,128]{1,0:T(8,128)(2,1)S(1)}) custom-call(s32[1,2]{1,0:T(1,128)S(1)} %get-tuple-element.30.neighbours, bf16[1280,256]{1,0:T(8,128)(2,1)S(1)} %get-tuple-element.31.frames.refs_3_, bf16[2,256,128]{2,1,0:T(8,128)(2,1)S(1)} %get-tuple-element.32.table.refs_4_, ...), custom_call_target="tpu_custom_call" | custom-call | flops 250000000 | tf_op jit(solution)/shard_map/edge_bands/pallas_call | solution.py:555
  4.0 0.1 collective-permute-start
  4.1 3.4 %collective-permute-start.1 = (bf16[256,128]{1,0:T(8,128)(2,1)S(1)}, bf16[256,128]{1,0:T(8,128)(2,1)S(1)}, u32[]{:S(2)}, u32[]{:S(2)}) collective-permute-start(bf16[256,128]{1,0:T(8,128)(2,1)S(1)} %get-tuple-element.35), channel_id=1, source_target_pairs={{2,4},{4,2},{6,8},{8,6},{10,12},{12,10},{14,16},{16,14},{18,20},{2... | collective-permute-start | bytes 196616 | tf_op jit(solution)/shard_map/ppermute | solution.py:569
  7.5 2.4 %near_part.1 = (f32[1456,256]{1,0:T(8,128)S(1)}, f32[2,64,2816]{2,1,0:T(8,128)S(1)}, bf16[2,416,1248]{2,1,0:T(8,128)(2,1)S(1)}) custom-call(f32[2,64,2816]{2,1,0:T(8,128)} %refs_0_.1, bf16[2,416,1248]{2,1,0:T(8,128)(2,1)} %constant.9.clone.refs_1_, s32[1,2560]{1,0:T(1,128)S(1)} %get-tuple-element.33.wires.refs_2_, ...), custom_call_target="tpu_custom_call" | custom-call | flops 750000000 | tf_op jit(solution)/shard_map/near_part/pallas_call | solution.py:561
  9.9 0.0 collective-permute-done.halo0
  9.9 0.8 %collective-permute-done.1.halo1 = bf16[256,128]{1,0:T(8,128)(2,1)S(1)} collective-permute-done((bf16[256,128]{1,0:T(8,128)(2,1)S(1)}, bf16[256,128]{1,0:T(8,128)(2,1)S(1)}, u32[]{:S(2)}, u32[]{:S(2)}) %collective-permute-start.1) | collective-permute-done | bytes 65568 | tf_op jit(solution)/shard_map/ppermute | solution.py:569
  10.7 0.6 %collective-permute-start.2 = (bf16[256,128]{1,0:T(8,128)(2,1)S(1)}, bf16[256,128]{1,0:T(8,128)(2,1)S(1)}, u32[]{:S(2)}, u32[]{:S(2)}) collective-permute-start(bf16[256,128]{1,0:T(8,128)(2,1)S(1)} %pad_maximum_fusion), channel_id=1, source_target_pairs={{0,1},{1,0},{2,3},{3,2},{4,5},{5,4},{6,7},{7,6},{8,9},{9,8},{10,11... | collective-permute-start | bytes 196616 | tf_op jit(solution)/shard_map/ppermute | solution.py:543
  11.3 1.9 %factors.1 = (f32[1456,256]{1,0:T(8,128)S(1)}, f32[1456,256]{1,0:T(8,128)S(1)}, bf16[1456,1280]{1,0:T(8,128)(2,1)S(1)}, f32[1280,128]{1,0:T(8,128)S(1)}, bf16[2,624,1248]{2,1,0:T(8,128)(2,1)S(1)}) custom-call(f32[2,64,2816]{2,1,0:T(8,128)S(1)} %get-tuple-element.40.kernel, s32[1,2560]{1,0:T(1,128)S(1)} %get-tuple-element.33.wires.refs_2_, ...), custom_call_target="tpu_custom_call" | custom-call | flops 718750016 | tf_op jit(solution)/shard_map/factors/pallas_call | solution.py:579
  13.2 0.0 collective-permute-done.3.refs_0_
  13.2 1.3 %far_part.1.folded = f32[1456,256]{1,0:T(8,128)S(1)} custom-call(bf16[1280,128]{1,0:T(8,128)(2,1)S(1)} %collective-permute-done.3.refs_0_, bf16[1456,1280]{1,0:T(8,128)(2,1)S(1)} %get-tuple-element.41.refs_1_, f32[1280,128]{1,0:T(8,128)S(1)} %get-tuple-element.42.refs_2_, f32[1456,256]{1,0:T(8,128)S(1)} %get-tuple-element.43.refs_3_), custom_call_target="tpu_custom_call" | custom-call | flops 375000000 | tf_op jit(solution)/shard_map/far_part/pallas_call | solution.py:584
  14.5 0.8 %collective-permute-done.2.halo2 = bf16[256,128]{1,0:T(8,128)(2,1)S(1)} collective-permute-done((bf16[256,128]{1,0:T(8,128)(2,1)S(1)}, bf16[256,128]{1,0:T(8,128)(2,1)S(1)}, u32[]{:S(2)}, u32[]{:S(2)}) %collective-permute-start.2) | collective-permute-done | bytes 65568 | tf_op jit(solution)/shard_map/ppermute | solution.py:543
  15.2 2.4 %leading_planes.1 = (bf16[800,128]{1,0:T(8,128)(2,1)S(1)}, f32[800,128]{1,0:T(8,128)S(1)}) custom-call(s32[1,2]{1,0:T(1,128)S(1)} %get-tuple-element.30.neighbours, bf16[256,128]{1,0:T(8,128)(2,1)S(1)} %collective-permute-done.halo0, bf16[256,128]{1,0:T(8,128)(2,1)S(1)} %collective-permute-done.1.halo1, bf16[256,128]{1,0:T(8,128)(2,1)S(1)} %collective-permute-done.2.halo2, ...), custom_call_target="tpu_custom_call" | custom-call | flops 1062499968 | tf_op jit(solution)/shard_map/leading_planes/pallas_call | solution.py:621
  17.7 0.2 collective-permute-start.5
  17.9 2.0 %trailing_planes.1 = (bf16[480,128]{1,0:T(8,128)(2,1)S(1)}, f32[1280,128]{1,0:T(8,128)S(1)}) custom-call(s32[1,2]{1,0:T(1,128)S(1)} %get-tuple-element.30.neighbours, bf16[256,128]{1,0:T(8,128)(2,1)S(1)} %collective-permute-done.halo0, bf16[256,128]{1,0:T(8,128)(2,1)S(1)} %collective-permute-done.1.halo1, bf16[256,128]{1,0:T(8,128)(2,1)S(1)} %collective-permute-done.2.halo2, ...), custom_call_target="tpu_custom_call" | custom-call | flops 1062499968 | tf_op jit(solution)/shard_map/trailing_planes/pallas_call | solution.py:626
  20.0 2.5 %collective-permute-start.4 = (bf16[480,128]{1,0:T(8,128)(2,1)S(1)}, bf16[480,128]{1,0:T(8,128)(2,1)S(1)}, u32[]{:S(2)}, u32[]{:S(2)}) collective-permute-start(bf16[480,128]{1,0:T(8,128)(2,1)S(1)} %get-tuple-element.53), channel_id=1, source_target_pairs={{0,1},{1,0},{2,3},{3,2},{4,5},{5,4},{6,7},{7,6},{8,9},{9,8},{10,11... | collective-permute-start | bytes 368648 | tf_op jit(solution)/shard_map/ppermute | solution.py:543
  22.5 0.0 copy-done
  22.5 0.0 copy-done.1
  22.5 2.1 %own_signal.1 = (f32[1280,256]{1,0:T(8,128)S(1)}, bf16[1,256,512]{2,1,0:T(8,128)(2,1)S(1)}, f32[1280,256]{1,0:T(8,128)S(1)}) custom-call(f32[1280,128]{1,0:T(8,128)S(1)} %get-tuple-element.49.own, f32[2,128,256]{2,1,0:T(8,128)} %constant.11.clone.basis_source, f32[1,128]{1,0:T(1,128)S(1)} %bitcast.8, f32[1,128]{1,0:T(1,128)S(1)} %bitcast.9, s32[4,80]{1,0:T(4,128)S(1)} %bitcast.7), custom_call_target="tpu_custom_call" | custom-call | flops 625000000 | tf_op jit(solution)/shard_map/own_signal/pallas_call | solution.py:596
  24.5 1.2 %collective-permute-done.5.values = bf16[800,128]{1,0:T(8,128)(2,1)S(1)} collective-permute-done((bf16[800,128]{1,0:T(8,128)(2,1)S(1)}, bf16[800,128]{1,0:T(8,128)(2,1)S(1)}, u32[]{:S(2)}, u32[]{:S(2)}) %collective-permute-start.5) | collective-permute-done | bytes 204832 | tf_op jit(solution)/shard_map/ppermute | solution.py:543
  25.7 1.2 %part_signal.2.refs_0_ = f32[1280,256]{1,0:T(8,128)} custom-call(f32[1280,256]{1,0:T(8,128)S(1)} %get-tuple-element.50.signal, bf16[1,256,512]{2,1,0:T(8,128)(2,1)S(1)} %get-tuple-element.51.bases, f32[1280,256]{1,0:T(8,128)S(1)} %get-tuple-element.52.inside, bf16[800,128]{1,0:T(8,128)(2,1)S(1)} %collective-permute-done.5.values), custom_call_target="tpu_custom_call" | custom-call | flops 312500000 | tf_op jit(solution)/shard_map/part_signal/pallas_call | solution.py:637
  26.9 0.1 collective-permute-done.4.values
  27.1 1.0 %part_signal.3 = f32[1280,256]{1,0:T(8,128)} custom-call(f32[1280,256]{1,0:T(8,128)S(1)} %get-tuple-element.50.signal, bf16[1,256,512]{2,1,0:T(8,128)(2,1)S(1)} %get-tuple-element.51.bases, f32[1280,256]{1,0:T(8,128)S(1)} %get-tuple-element.52.inside, bf16[480,128]{1,0:T(8,128)(2,1)S(1)} %collective-permute-done.4.values, ...), custom_call_target="tpu_custom_call", output_to_operand_aliasing={{}: (4, {})} | custom-call | flops 312500000 | tf_op jit(solution)/shard_map/part_signal/pallas_call | solution.py:637
  (7 shorter events, 0.0 us)
Async XLA Ops:
  1.6 11.6 %collective-permute-start.3 = (bf16[1280,128]{1,0:T(8,128)(2,1)S(1)}, bf16[1280,128]{1,0:T(8,128)(2,1)S(1)}, u32[]{:S(2)}, u32[]{:S(2)}) collective-permute-start(bf16[1280,128]{1,0:T(8,128)(2,1)S(1)} %get-tuple-element.39), channel_id=1, source_target_pairs={{0,1},{1,0},{2,3},{3,2},{4,5},{5,4},{6,7},{7,6},{8,9},{9,8},{10,11... | collective-permute-start | bytes 983048 | tf_op jit(solution)/shard_map/ppermute | solution.py:543
  4.0 5.9 %collective-permute-start = (bf16[256,128]{1,0:T(8,128)(2,1)S(1)}, bf16[256,128]{1,0:T(8,128)(2,1)S(1)}, u32[]{:S(2)}, u32[]{:S(2)}) collective-permute-start(bf16[256,128]{1,0:T(8,128)(2,1)S(1)} %get-tuple-element.34), channel_id=1, source_target_pairs={{0,2},{2,0},{4,6},{6,4},{8,10},{10,8},{12,14},{14,12},{16,18},{18,... | collective-permute-start | bytes 196616 | tf_op jit(solution)/shard_map/ppermute | solution.py:569
  4.1 6.6 %collective-permute-start.1 = (bf16[256,128]{1,0:T(8,128)(2,1)S(1)}, bf16[256,128]{1,0:T(8,128)(2,1)S(1)}, u32[]{:S(2)}, u32[]{:S(2)}) collective-permute-start(bf16[256,128]{1,0:T(8,128)(2,1)S(1)} %get-tuple-element.35), channel_id=1, source_target_pairs={{2,4},{4,2},{6,8},{8,6},{10,12},{12,10},{14,16},{16,14},{18,20},{2... | collective-permute-start | bytes 196616 | tf_op jit(solution)/shard_map/ppermute | solution.py:569
  10.7 4.5 %collective-permute-start.2 = (bf16[256,128]{1,0:T(8,128)(2,1)S(1)}, bf16[256,128]{1,0:T(8,128)(2,1)S(1)}, u32[]{:S(2)}, u32[]{:S(2)}) collective-permute-start(bf16[256,128]{1,0:T(8,128)(2,1)S(1)} %pad_maximum_fusion), channel_id=1, source_target_pairs={{0,1},{1,0},{2,3},{3,2},{4,5},{5,4},{6,7},{7,6},{8,9},{9,8},{10,11... | collective-permute-start | bytes 196616 | tf_op jit(solution)/shard_map/ppermute | solution.py:543
  17.7 8.1 %collective-permute-start.5 = (bf16[800,128]{1,0:T(8,128)(2,1)S(1)}, bf16[800,128]{1,0:T(8,128)(2,1)S(1)}, u32[]{:S(2)}, u32[]{:S(2)}) collective-permute-start(bf16[800,128]{1,0:T(8,128)(2,1)S(1)} %get-tuple-element.54), channel_id=1, source_target_pairs={{0,1},{1,0},{2,3},{3,2},{4,5},{5,4},{6,7},{7,6},{8,9},{9,8},{10,11... | collective-permute-start | bytes 614408 | tf_op jit(solution)/shard_map/ppermute | solution.py:543
  17.9 4.6 %copy-start = (s32[1,80,4]{1,2,0:T(4,128)S(1)}, s32[1,80,4]{1,2,0:T(4,128)}, u32[]{:S(2)}) copy-start(s32[1,80,4]{1,2,0:T(4,128)} %param.17) | copy-start | bytes 3844
  17.9 4.6 %copy-start.1 = (f32[128]{0:T(128)S(1)}, f32[128]{0:T(128)}, u32[]{:S(2)}) copy-start(f32[128]{0:T(128)} %param.15) | copy-start | bytes 1540
  17.9 4.6 %copy-start.2 = (f32[128]{0:T(128)S(1)}, f32[128]{0:T(128)}, u32[]{:S(2)}) copy-start(f32[128]{0:T(128)} %param.16) | copy-start | bytes 1540
  20.0 7.1 %collective-permute-start.4 = (bf16[480,128]{1,0:T(8,128)(2,1)S(1)}, bf16[480,128]{1,0:T(8,128)(2,1)S(1)}, u32[]{:S(2)}, u32[]{:S(2)}) collective-permute-start(bf16[480,128]{1,0:T(8,128)(2,1)S(1)} %get-tuple-element.53), channel_id=1, source_target_pairs={{0,1},{1,0},{2,3},{3,2},{4,5},{5,4},{6,7},{7,6},{8,9},{9,8},{10,11... | collective-permute-start | bytes 368648 | tf_op jit(solution)/shard_map/ppermute | solution.py:543

commit v7 on v6

--- a/solution.py
+++ b/solution.py
@@ -60,6 +60,8 @@
 
 
 planes = make_planes()
+edge = slice(0, ceil_to(HALO_CH + 1, 16) + 32)
+inner = slice(edge.stop, planes[2].rows)
 all_rows = planes[-1].row + planes[-1].rows
 
 
@@ -77,7 +79,7 @@
     for values in (np.cos(angles) * mask, np.sin(angles) * mask):
         high = values.astype(np.float32).astype(ml_dtypes.bfloat16)
         low = (values - high.astype(np.float64)).astype(np.float32).astype(ml_dtypes.bfloat16)
-        found.append(np.concatenate([(high, low)[i] for i in order], axis=1))
+        found.append(np.concatenate([(high, low)[i][:, columns] for i, columns in order], axis=1))
     return np.stack(found)
 
 
@@ -232,8 +234,8 @@
         copy.wait()
 
 
-def factors(blocks, share, kernel, wires, wide_source, sums, diffs, chosen, far_signs, wide, sem):
-    copy = pltpu.make_async_copy(wide_source, wide, sem)
+def factors(blocks, share, kernel, wires, table_source, sums, diffs, chosen, far_signs, table, sem):
+    copy = pltpu.make_async_copy(table_source, table, sem)
     copy.start()
     harmonics, width = kernel.shape[1], sums.shape[1] // 2
     spare = width // 2 - harmonics
@@ -300,11 +302,25 @@
     return jnp.concatenate(targets, axis=1), operand
 
 
+def paired(values):
+    joined = jnp.concatenate(split(values), axis=1)
+    return jnp.concatenate([joined, joined], axis=0)
+
+
+def added(both):
+    width = both.shape[1] // 2
+    return both[:, :width] + both[:, width:]
+
+
 def one_plane(table, values):
-    width = values.shape[1]
-    joined = jnp.concatenate(split(values), axis=1)
-    result = dot(table, jnp.concatenate([joined, joined], axis=0))
-    return result[:, :width] + result[:, width:]
+    return added(dot(table, jnp.concatenate([paired(values[part]) for part in (inner, edge)], axis=0)))
+
+
+def inner_sums(folded, table):
+    plane, width = planes[2], folded.shape[1] // 2
+    both = folded[pl.ds(plane.row + inner.start, inner.stop - inner.start), :]
+    stop = 2 * (inner.stop - inner.start)
+    return [added(dot(table[i, :, :stop], paired(both[:, i * width : (i + 1) * width]))) for i in range(2)]
 
 
 def two_planes(table, values):
@@ -324,14 +340,14 @@
     return [jnp.concatenate(pair, axis=1) for pair in zip(*found)]
 
 
-def last_frequencies(bands, folded, sums, diffs, table):
-    plane = planes[2]
-    rows, edge = pl.ds(plane.row, plane.rows), ceil_to(HALO_CH + 1, 16)
-    both = folded[rows, :]
-    width = both.shape[1] // 2
-    both = jnp.concatenate([both[:edge] + dot(one_hot(edge, plane.row, bands[0]), bands[1]), both[edge:]], axis=0)
-    even, odd = one_plane(table[0], both[:, :width]), one_plane(table[1], both[:, width:])
-    return multiplied(even, odd, sums[rows, :], diffs[rows, :])
+def last_frequencies(bands, folded, sums, diffs, table, sums_of_inner=None):
+    plane, width = planes[2], folded.shape[1] // 2
+    rows, start = pl.ds(plane.row, plane.rows), 2 * (inner.stop - inner.start)
+    both = folded[pl.ds(plane.row, edge.stop), :] + dot(one_hot(edge.stop, plane.row, bands[0]), bands[1])
+    found = []
+    for i, base in enumerate(sums_of_inner or inner_sums(folded, table)):
+        found.append(base + added(dot(table[i, :, start:], paired(both[:, i * width : (i + 1) * width]))))
+    return multiplied(*found, sums[rows, :], diffs[rows, :])
 
 
 def put_first(result, total, gap, table):
@@ -362,9 +378,13 @@
 
 
 def far_part(parts, *refs):
-    received, (chosen, far_signs, near, folded) = refs[:parts], refs[parts:]
+    received, (chosen, far_signs, near, wide, folded, even, odd) = refs[:parts], refs[parts:]
     operand = fold_operand(jnp.concatenate([ref[...] for ref in received], axis=0), far_signs[...])
     folded[...] = near[...] + dot(chosen[...], operand)
+
+    @pl.when((parts == 1) & (lax.axis_index("chan") == 0))
+    def _():
+        even[...], odd[...] = inner_sums(folded, wide)
 
 
 def all_planes(blocks, share, neighbours, *refs):
@@ -382,14 +402,15 @@
         out[...] = result[pl.ds(first, share), :].astype(bf16)
 
 
-def leading_planes(neighbours, halo0, halo1, halo2, folded, sums, diffs, narrow, wide, send, rest, result):
+def leading_planes(neighbours, halo0, halo1, halo2, folded, sums, diffs, narrow, wide, even, odd, send, rest, result):
     last = planes[2]
     count = send.shape[0]
 
     @pl.when(lax.axis_index("chan") == 0)
     def _():
         bands = halo_operand(2, neighbours, (halo0, halo1, halo2))
-        put_last(result.at[: last.count], *last_frequencies(bands, folded, sums, diffs, wide), wide)
+        parts = last_frequencies(bands, folded, sums, diffs, wide, [even[...], odd[...]])
+        put_last(result.at[: last.count], *parts, wide)
         left = last.count - count
         send[...] = result[left : last.count, :].astype(bf16)
         rest[:left, :] = result[:left, :]
@@ -555,9 +576,9 @@
     bands = call(
         functools.partial(edge_bands, blocks), [((blocks * HALO_CH, width), bf16)] * 2, [whole] * 4, "edge_bands",
     )(neighbours, frames, table, wires)
-    narrow = jnp.asarray(channel_tables(planes[0].length, planes[0].rows, (0, 1, 0)))
-    wide = jnp.asarray(channel_tables(planes[2].length, planes[2].rows, (0, 1)))
-    sources = [kernel, narrow]
+    narrow = jnp.asarray(channel_tables(planes[0].length, planes[0].rows, [(i, slice(None)) for i in (0, 1, 0)]))
+    wide = jnp.asarray(channel_tables(planes[2].length, planes[2].rows, [(i, part) for part in (inner, edge) for i in (0, 1)]))
+    sources = [kernel, wide]
     folded, *ready = call(
         lambda *refs: near_part(refs[: len(sources)], *refs[len(sources) :]),
         [((all_rows, 2 * width), f32)] + [(part.shape, part.dtype) for part in sources],
@@ -572,18 +593,19 @@
         jnp.concatenate([band[s * HALO_CH : (s + 1) * HALO_CH] for band in halo]) for s in range(1, blocks)
     ]
     halo = [near(band) for band in halo + around(shares)]
-    kernel, narrow = map(near, ready)
+    kernel, wide = map(near, ready)
     folded = near(folded)
     spare_rows = (blocks - 1) * share
     both = ((all_rows, 2 * width), f32)
-    sums, diffs, chosen, far_signs, wide = map(near, call(
+    sums, diffs, chosen, far_signs, narrow = map(near, call(
         functools.partial(factors, blocks, share),
-        [both, both, ((all_rows, spare_rows), bf16), ((spare_rows, width), f32), (wide.shape, bf16)],
+        [both, both, ((all_rows, spare_rows), bf16), ((spare_rows, width), f32), (narrow.shape, bf16)],
         [whole] * 2 + [pinned], "factors", [pltpu.SemaphoreType.DMA],
-    )(kernel, wires, distant(wide)))
-    (folded,) = call(
-        functools.partial(far_part, blocks - 1), [both], [whole] * (blocks + 2), "far_part",
-    )(*received, chosen, far_signs, folded)
+    )(kernel, wires, distant(narrow)))
+    single = ((planes[2].rows, width), f32)
+    folded, *parts = call(
+        functools.partial(far_part, blocks - 1), [both, single, single], [whole] * (blocks + 3), "far_part",
+    )(*received, chosen, far_signs, folded, wide)
     operands = (neighbours, *halo, near(folded), sums, diffs, narrow, wide)
     basis = jnp.asarray(inverse_tables(ticks, blocks, padded))
     filters = (wide_filter[None], tight_filter[None])
@@ -620,8 +642,8 @@
     below, above = share - PU, PU + PV - share
     sent, rest = call(
         leading_planes, [((PU, width), bf16), ((PV, width), f32)],
-        [whole] * 9, "leading_planes", [pltpu.VMEM((PU + PV, width), f32)],
-    )(*operands)
+        [whole] * 11, "leading_planes", [pltpu.VMEM((PU + PV, width), f32)],
+    )(*operands, *map(near, parts))
     (early,) = map(near, around([sent]))
     sent, own = call(
         trailing_planes, [((below, width), bf16), ((share, width), f32)],

time: 28.5 us -> 28.3 us (level)
  waiting for transfers between devices: 2.86 us -> 2.48 us
    pallas_call x1, Pallas kernels: 1.26 us -> 2.09 us  [body(): call(functools.partial(far_part, blocks - 1), [both, single, single], [wh...]
    pallas_call x1, Pallas kernels: 2.44 us -> 2.05 us  [body(): call(leading_planes, [((PU, width), bf16), ((PV, width), f32)], [whole] *...]
    ppermute x4, waiting for transfers between devices: 2.1 us -> 1.73 us  [around(): lax.ppermute(part, 'chan', [(i, (i + s) % blocks) for i in range(blocks)])]
    pallas_call x1, Pallas kernels: 1.91 us -> 1.61 us  [body(): call(functools.partial(factors, blocks, share), [both, both, ((all_rows,...]
  transfers between devices with their start and end apart: 6 -> 6, of which waited for: 4 -> 4; matrix products, arithmetic and copies ran while one was open for 0% -> 0% of each run, Pallas kernels for 42% -> 44%
where the time goes in v7:
time: 28.3 us; the launch traced here: 28.1 us
  Pallas kernels  16.9 us (60%)
  starting transfers between devices  8.43 us (30%)
  waiting for transfers between devices  2.48 us (9%)
    ppermute x4, starting transfers between devices, around(): lax.ppermute(part, 'chan', [(i, (i + s) % blocks) for i in range(blocks)])  4.98 us
    ppermute x2, starting transfers between devices, body(): halo.append(lax.ppermute(band, 'apa', pairs))  3.45 us
    pallas_call x1, Pallas kernels, body(): call(lambda *refs: near_part(refs[:len(sources)], *refs[len(sources):]),...  2.44 us
    pallas_call x2, Pallas kernels, finish(): call(functools.partial(part_signal, spans), [((share, ticks), f32)], [who...  2.2 us
    pallas_call x1, Pallas kernels, body(): call(functools.partial(far_part, blocks - 1), [both, single, single], [wh...  2.09 us
    pallas_call x1, Pallas kernels, body(): call(trailing_planes, [((below, width), bf16), ((share, width), f32)], [w...  2.08 us
    pallas_call x1, Pallas kernels, own_part(): call(functools.partial(own_signal, blocks), signal_shapes, [whole, pinned...  2.06 us
    pallas_call x1, Pallas kernels, body(): call(leading_planes, [((PU, width), bf16), ((PV, width), f32)], [whole] *...  2.05 us
  transfers between devices with their start and end apart: 6, of which 4 were waited for; matrix products, arithmetic and copies ran while one was open for 0% of the time, Pallas kernels for 44%

profile of v7, /device:TPU:24, one launch (start us, length us, event | category | flops | bytes accessed | tf_op | source)
XLA Modules:
  0.0 28.1 jit_solution(11088071804620093668)
XLA Ops:
  0.0 1.6 %tick_spectra.1 = (bf16[1280,128]{1,0:T(8,128)(2,1)S(1)}, bf16[1280,256]{1,0:T(8,128)(2,1)S(1)}, bf16[2,256,128]{2,1,0:T(8,128)(2,1)S(1)}, s32[1,2560]{1,0:T(1,128)S(1)}, s32[1,2]{1,0:T(1,128)S(1)}) custom-call(bf16[1280,256]{1,0:T(8,128)(2,1)} %bitcast.10, bf16[2,256,128]{2,1,0:T(8,128)(2,1)} %constant.8.clone.table_source, s32[1,2560]{1,0:T(1,128)} %wires_source.1, ...), custom_call_target="tpu_custom_call" | custom-call | flops 625000000 | tf_op jit(solution)/shard_map/tick_spectra/pallas_call | solution.py:568
  1.6 1.6 %collective-permute-start.3 = (bf16[1280,128]{1,0:T(8,128)(2,1)S(1)}, bf16[1280,128]{1,0:T(8,128)(2,1)S(1)}, u32[]{:S(2)}, u32[]{:S(2)}) collective-permute-start(bf16[1280,128]{1,0:T(8,128)(2,1)S(1)} %get-tuple-element.42), channel_id=1, source_target_pairs={{0,1},{1,0},{2,3},{3,2},{4,5},{5,4},{6,7},{7,6},{8,9},{9,8},{10,11... | collective-permute-start | bytes 983048 | tf_op jit(solution)/shard_map/ppermute | solution.py:564
  3.2 0.8 %edge_bands.1 = (bf16[256,128]{1,0:T(8,128)(2,1)S(1)}, bf16[256,128]{1,0:T(8,128)(2,1)S(1)}) custom-call(s32[1,2]{1,0:T(1,128)S(1)} %get-tuple-element.33.neighbours, bf16[1280,256]{1,0:T(8,128)(2,1)S(1)} %get-tuple-element.34.frames.refs_3_, bf16[2,256,128]{2,1,0:T(8,128)(2,1)S(1)} %get-tuple-element.35.table.refs_4_, ...), custom_call_target="tpu_custom_call" | custom-call | flops 250000000 | tf_op jit(solution)/shard_map/edge_bands/pallas_call | solution.py:576
  4.0 0.1 collective-permute-start
  4.1 3.4 %collective-permute-start.1 = (bf16[256,128]{1,0:T(8,128)(2,1)S(1)}, bf16[256,128]{1,0:T(8,128)(2,1)S(1)}, u32[]{:S(2)}, u32[]{:S(2)}) collective-permute-start(bf16[256,128]{1,0:T(8,128)(2,1)S(1)} %get-tuple-element.38), channel_id=1, source_target_pairs={{2,4},{4,2},{6,8},{8,6},{10,12},{12,10},{14,16},{16,14},{18,20},{2... | collective-permute-start | bytes 196616 | tf_op jit(solution)/shard_map/ppermute | solution.py:590
  7.5 2.4 %near_part.1 = (f32[1456,256]{1,0:T(8,128)S(1)}, f32[2,64,2816]{2,1,0:T(8,128)S(1)}, bf16[2,624,1248]{2,1,0:T(8,128)(2,1)S(1)}) custom-call(f32[2,64,2816]{2,1,0:T(8,128)} %refs_0_.1, bf16[2,624,1248]{2,1,0:T(8,128)(2,1)} %constant.10.clone.refs_1_, s32[1,2560]{1,0:T(1,128)S(1)} %get-tuple-element.36.wires.refs_2_, ...), custom_call_target="tpu_custom_call" | custom-call | flops 750000000 | tf_op jit(solution)/shard_map/near_part/pallas_call | solution.py:582
  9.9 0.0 collective-permute-done.halo0
  9.9 0.7 %collective-permute-done.1.halo1 = bf16[256,128]{1,0:T(8,128)(2,1)S(1)} collective-permute-done((bf16[256,128]{1,0:T(8,128)(2,1)S(1)}, bf16[256,128]{1,0:T(8,128)(2,1)S(1)}, u32[]{:S(2)}, u32[]{:S(2)}) %collective-permute-start.1) | collective-permute-done | bytes 65568 | tf_op jit(solution)/shard_map/ppermute | solution.py:590
  10.7 0.6 %collective-permute-start.2 = (bf16[256,128]{1,0:T(8,128)(2,1)S(1)}, bf16[256,128]{1,0:T(8,128)(2,1)S(1)}, u32[]{:S(2)}, u32[]{:S(2)}) collective-permute-start(bf16[256,128]{1,0:T(8,128)(2,1)S(1)} %pad_maximum_fusion), channel_id=1, source_target_pairs={{0,1},{1,0},{2,3},{3,2},{4,5},{5,4},{6,7},{7,6},{8,9},{9,8},{10,11... | collective-permute-start | bytes 196616 | tf_op jit(solution)/shard_map/ppermute | solution.py:564
  11.3 1.6 %factors.1 = (f32[1456,256]{1,0:T(8,128)S(1)}, f32[1456,256]{1,0:T(8,128)S(1)}, bf16[1456,1280]{1,0:T(8,128)(2,1)S(1)}, f32[1280,128]{1,0:T(8,128)S(1)}, bf16[2,416,1248]{2,1,0:T(8,128)(2,1)S(1)}) custom-call(f32[2,64,2816]{2,1,0:T(8,128)S(1)} %get-tuple-element.43.kernel, s32[1,2560]{1,0:T(1,128)S(1)} %get-tuple-element.36.wires.refs_2_, ...), custom_call_target="tpu_custom_call" | custom-call | flops 718750016 | tf_op jit(solution)/shard_map/factors/pallas_call | solution.py:600
  12.9 0.0 collective-permute-done.3.refs_0_
  12.9 2.1 %far_part.1 = (f32[1456,256]{1,0:T(8,128)S(1)}, f32[624,128]{1,0:T(8,128)S(1)}, f32[624,128]{1,0:T(8,128)S(1)}) custom-call(bf16[1280,128]{1,0:T(8,128)(2,1)S(1)} %collective-permute-done.3.refs_0_, bf16[1456,1280]{1,0:T(8,128)(2,1)S(1)} %get-tuple-element.44.refs_1_, f32[1280,128]{1,0:T(8,128)S(1)} %get-tuple-element.45.refs_2_, ...), custom_call_target="tpu_custom_call" | custom-call | flops 375000000 | tf_op jit(solution)/shard_map/far_part/pallas_call | solution.py:606
  15.0 0.2 collective-permute-done.2.halo2
  15.2 2.1 %leading_planes.1 = (bf16[800,128]{1,0:T(8,128)(2,1)S(1)}, f32[800,128]{1,0:T(8,128)S(1)}) custom-call(s32[1,2]{1,0:T(1,128)S(1)} %get-tuple-element.33.neighbours, bf16[256,128]{1,0:T(8,128)(2,1)S(1)} %collective-permute-done.halo0, bf16[256,128]{1,0:T(8,128)(2,1)S(1)} %collective-permute-done.1.halo1, bf16[256,128]{1,0:T(8,128)(2,1)S(1)} %collective-permute-done.2.halo2, ...), custom_call_target="tpu_custom_call" | custom-call | flops 1062499968 | tf_op jit(solution)/shard_map/leading_planes/pallas_call | solution.py:643
  17.3 0.4 %collective-permute-start.5 = (bf16[800,128]{1,0:T(8,128)(2,1)S(1)}, bf16[800,128]{1,0:T(8,128)(2,1)S(1)}, u32[]{:S(2)}, u32[]{:S(2)}) collective-permute-start(bf16[800,128]{1,0:T(8,128)(2,1)S(1)} %get-tuple-element.60), channel_id=1, source_target_pairs={{0,1},{1,0},{2,3},{3,2},{4,5},{5,4},{6,7},{7,6},{8,9},{9,8},{10,11... | collective-permute-start | bytes 614408 | tf_op jit(solution)/shard_map/ppermute | solution.py:564
  17.7 2.1 %trailing_planes.1 = (bf16[480,128]{1,0:T(8,128)(2,1)S(1)}, f32[1280,128]{1,0:T(8,128)S(1)}) custom-call(s32[1,2]{1,0:T(1,128)S(1)} %get-tuple-element.33.neighbours, bf16[256,128]{1,0:T(8,128)(2,1)S(1)} %collective-permute-done.halo0, bf16[256,128]{1,0:T(8,128)(2,1)S(1)} %collective-permute-done.1.halo1, bf16[256,128]{1,0:T(8,128)(2,1)S(1)} %collective-permute-done.2.halo2, ...), custom_call_target="tpu_custom_call" | custom-call | flops 1062499968 | tf_op jit(solution)/shard_map/trailing_planes/pallas_call | solution.py:648
  19.8 2.4 %collective-permute-start.4 = (bf16[480,128]{1,0:T(8,128)(2,1)S(1)}, bf16[480,128]{1,0:T(8,128)(2,1)S(1)}, u32[]{:S(2)}, u32[]{:S(2)}) collective-permute-start(bf16[480,128]{1,0:T(8,128)(2,1)S(1)} %get-tuple-element.59), channel_id=1, source_target_pairs={{0,1},{1,0},{2,3},{3,2},{4,5},{5,4},{6,7},{7,6},{8,9},{9,8},{10,11... | collective-permute-start | bytes 368648 | tf_op jit(solution)/shard_map/ppermute | solution.py:564
  22.2 0.0 copy-done
  22.2 0.0 copy-done.1
  22.2 2.1 %own_signal.1 = (f32[1280,256]{1,0:T(8,128)S(1)}, bf16[1,256,512]{2,1,0:T(8,128)(2,1)S(1)}, f32[1280,256]{1,0:T(8,128)S(1)}) custom-call(f32[1280,128]{1,0:T(8,128)S(1)} %get-tuple-element.55.own, f32[2,128,256]{2,1,0:T(8,128)} %constant.11.clone.basis_source, f32[1,128]{1,0:T(1,128)S(1)} %bitcast.8, f32[1,128]{1,0:T(1,128)S(1)} %bitcast.9, s32[4,80]{1,0:T(4,128)S(1)} %bitcast.7), custom_call_target="tpu_custom_call" | custom-call | flops 625000000 | tf_op jit(solution)/shard_map/own_signal/pallas_call | solution.py:618
  24.3 1.0 %collective-permute-done.5.values = bf16[800,128]{1,0:T(8,128)(2,1)S(1)} collective-permute-done((bf16[800,128]{1,0:T(8,128)(2,1)S(1)}, bf16[800,128]{1,0:T(8,128)(2,1)S(1)}, u32[]{:S(2)}, u32[]{:S(2)}) %collective-permute-start.5) | collective-permute-done | bytes 204832 | tf_op jit(solution)/shard_map/ppermute | solution.py:564
  25.3 1.2 %part_signal.2.refs_0_ = f32[1280,256]{1,0:T(8,128)} custom-call(f32[1280,256]{1,0:T(8,128)S(1)} %get-tuple-element.56.signal, bf16[1,256,512]{2,1,0:T(8,128)(2,1)S(1)} %get-tuple-element.57.bases, f32[1280,256]{1,0:T(8,128)S(1)} %get-tuple-element.58.inside, bf16[800,128]{1,0:T(8,128)(2,1)S(1)} %collective-permute-done.5.values), custom_call_target="tpu_custom_call" | custom-call | flops 312500000 | tf_op jit(solution)/shard_map/part_signal/pallas_call | solution.py:659
  26.5 0.5 %collective-permute-done.4.values = bf16[480,128]{1,0:T(8,128)(2,1)S(1)} collective-permute-done((bf16[480,128]{1,0:T(8,128)(2,1)S(1)}, bf16[480,128]{1,0:T(8,128)(2,1)S(1)}, u32[]{:S(2)}, u32[]{:S(2)}) %collective-permute-start.4) | collective-permute-done | bytes 122912 | tf_op jit(solution)/shard_map/ppermute | solution.py:564
  26.9 1.0 %part_signal.3 = f32[1280,256]{1,0:T(8,128)} custom-call(f32[1280,256]{1,0:T(8,128)S(1)} %get-tuple-element.56.signal, bf16[1,256,512]{2,1,0:T(8,128)(2,1)S(1)} %get-tuple-element.57.bases, f32[1280,256]{1,0:T(8,128)S(1)} %get-tuple-element.58.inside, bf16[480,128]{1,0:T(8,128)(2,1)S(1)} %collective-permute-done.4.values, ...), custom_call_target="tpu_custom_call", output_to_operand_aliasing={{}: (4, {})} | custom-call | flops 312500000 | tf_op jit(solution)/shard_map/part_signal/pallas_call | solution.py:659
  (7 shorter events, 0.0 us)
Async XLA Ops:
  1.6 11.3 %collective-permute-start.3 = (bf16[1280,128]{1,0:T(8,128)(2,1)S(1)}, bf16[1280,128]{1,0:T(8,128)(2,1)S(1)}, u32[]{:S(2)}, u32[]{:S(2)}) collective-permute-start(bf16[1280,128]{1,0:T(8,128)(2,1)S(1)} %get-tuple-element.42), channel_id=1, source_target_pairs={{0,1},{1,0},{2,3},{3,2},{4,5},{5,4},{6,7},{7,6},{8,9},{9,8},{10,11... | collective-permute-start | bytes 983048 | tf_op jit(solution)/shard_map/ppermute | solution.py:564
  4.0 5.9 %collective-permute-start = (bf16[256,128]{1,0:T(8,128)(2,1)S(1)}, bf16[256,128]{1,0:T(8,128)(2,1)S(1)}, u32[]{:S(2)}, u32[]{:S(2)}) collective-permute-start(bf16[256,128]{1,0:T(8,128)(2,1)S(1)} %get-tuple-element.37), channel_id=1, source_target_pairs={{0,2},{2,0},{4,6},{6,4},{8,10},{10,8},{12,14},{14,12},{16,18},{18,... | collective-permute-start | bytes 196616 | tf_op jit(solution)/shard_map/ppermute | solution.py:590
  4.1 6.6 %collective-permute-start.1 = (bf16[256,128]{1,0:T(8,128)(2,1)S(1)}, bf16[256,128]{1,0:T(8,128)(2,1)S(1)}, u32[]{:S(2)}, u32[]{:S(2)}) collective-permute-start(bf16[256,128]{1,0:T(8,128)(2,1)S(1)} %get-tuple-element.38), channel_id=1, source_target_pairs={{2,4},{4,2},{6,8},{8,6},{10,12},{12,10},{14,16},{16,14},{18,20},{2... | collective-permute-start | bytes 196616 | tf_op jit(solution)/shard_map/ppermute | solution.py:590
  10.7 4.5 %collective-permute-start.2 = (bf16[256,128]{1,0:T(8,128)(2,1)S(1)}, bf16[256,128]{1,0:T(8,128)(2,1)S(1)}, u32[]{:S(2)}, u32[]{:S(2)}) collective-permute-start(bf16[256,128]{1,0:T(8,128)(2,1)S(1)} %pad_maximum_fusion), channel_id=1, source_target_pairs={{0,1},{1,0},{2,3},{3,2},{4,5},{5,4},{6,7},{7,6},{8,9},{9,8},{10,11... | collective-permute-start | bytes 196616 | tf_op jit(solution)/shard_map/ppermute | solution.py:564
  17.3 8.0 %collective-permute-start.5 = (bf16[800,128]{1,0:T(8,128)(2,1)S(1)}, bf16[800,128]{1,0:T(8,128)(2,1)S(1)}, u32[]{:S(2)}, u32[]{:S(2)}) collective-permute-start(bf16[800,128]{1,0:T(8,128)(2,1)S(1)} %get-tuple-element.60), channel_id=1, source_target_pairs={{0,1},{1,0},{2,3},{3,2},{4,5},{5,4},{6,7},{7,6},{8,9},{9,8},{10,11... | collective-permute-start | bytes 614408 | tf_op jit(solution)/shard_map/ppermute | solution.py:564
  17.7 4.5 %copy-start = (s32[1,80,4]{1,2,0:T(4,128)S(1)}, s32[1,80,4]{1,2,0:T(4,128)}, u32[]{:S(2)}) copy-start(s32[1,80,4]{1,2,0:T(4,128)} %param.17) | copy-start | bytes 3844
  17.7 4.5 %copy-start.1 = (f32[128]{0:T(128)S(1)}, f32[128]{0:T(128)}, u32[]{:S(2)}) copy-start(f32[128]{0:T(128)} %param.15) | copy-start | bytes 1540
  17.7 4.5 %copy-start.2 = (f32[128]{0:T(128)S(1)}, f32[128]{0:T(128)}, u32[]{:S(2)}) copy-start(f32[128]{0:T(128)} %param.16) | copy-start | bytes 1540
  19.8 7.1 %collective-permute-start.4 = (bf16[480,128]{1,0:T(8,128)(2,1)S(1)}, bf16[480,128]{1,0:T(8,128)(2,1)S(1)}, u32[]{:S(2)}, u32[]{:S(2)}) collective-permute-start(bf16[480,128]{1,0:T(8,128)(2,1)S(1)} %get-tuple-element.59), channel_id=1, source_target_pairs={{0,1},{1,0},{2,3},{3,2},{4,5},{5,4},{6,7},{7,6},{8,9},{9,8},{10,11... | collective-permute-start | bytes 368648 | tf_op jit(solution)/shard_map/ppermute | solution.py:564
